TPU v7x, 128 devices: a whole 4x4x4 slice. The times are simulated.
128 devices in a mesh: gx: 16 (over x, z_hi, core), gy: 8 (over y, z_lo).
Axes of the slice: x: 4, y: 4, z: 4 (z_hi: 2, z_lo: 2; z = z_hi * 2 + z_lo), core: 2. Of those that a mesh axis runs over, the one named last changes fastest.
Arguments:
- fields: float32 [4, 3, 64, 16, 16, 128], P(None, None, None, 'gx', 'gy'), may hold values from -6 to 6
- velocity: float32 [2, 3, 64, 128, 16, 16], P(None, None, None, ('gx', 'gy')), may hold values from -3 to 3
Outputs:
- advanced: float32 [4, 3, 64, 16, 16, 128], P(None, None, None, 'gx', 'gy')
All inputs are finite; a program needn't handle non-finite values.
Results may differ from a plain program's by a relative error of at most 0.0003.
Values sent between devices are 32-bit elements; how exact they have to be, the bound alone decides.
No kernel may reach another device: no remote copies, remote signals or barrier semaphores. Data moves between devices by JAX's collectives and lax.ppermute only.
A program may use at most 64 MiB of HBM per device.

v0:
```python
import jax
import jax.numpy as jnp
import numpy as np
from jax import lax
from jax.sharding import PartitionSpec as P

STEP_SIZE = 0.025
FLUX_COEF = 3.0
PENALTY = 3.0


def padded(shard, sides, width):
    for axis, dim in sides:
        count, length = (lax.axis_size(axis), shard.shape[dim])
        up = [(i, (i + 1) % count) for i in range(count - 1)]
        down = [(j, i) for i, j in up]
        last = lax.slice_in_dim(shard, length - width, length, axis=dim)
        first = lax.slice_in_dim(shard, 0, width, axis=dim)
        before = lax.ppermute(last, axis, up)
        after = lax.ppermute(first, axis, down)
        shard = jnp.concatenate([before, shard, after], axis=dim)
    return shard


def derivative_table():
    points = np.array([-1.0, -1.0 / np.sqrt(5.0), 1.0 / np.sqrt(5.0), 1.0])
    weights_bary = np.ones(4)
    for first in range(4):
        for second in range(4):
            if first != second:
                weights_bary[first] = weights_bary[first] / (points[first] - points[second])
    table = np.zeros((4, 4))
    for first in range(4):
        for second in range(4):
            if first != second:
                table[first, second] = (
                    weights_bary[second] / weights_bary[first] / (points[first] - points[second])
                )
        table[first, first] = -np.sum(table[first])
    return jnp.asarray(table.astype(np.float32))


def along(table, block, direction):
    forms = ["pa,kabcxyz->kpbcxyz", "pb,kabcxyz->kapcxyz", "pc,kabcxyz->kabpxyz"]
    return jnp.einsum(forms[direction], table, block, precision=lax.Precision.HIGHEST)


def cross_speed(speed, field):
    return jnp.stack(
        [
            speed[1] * field[:, 2] - speed[2] * field[:, 1],
            speed[2] * field[:, 0] - speed[0] * field[:, 2],
            speed[0] * field[:, 1] - speed[1] * field[:, 0],
        ],
        axis=1,
    )


def normal_cross(direction, jump):
    zeros = jnp.zeros_like(jump[:, 0])
    if direction == 0:
        parts = [zeros, -jump[:, 2], jump[:, 1]]
    elif direction == 1:
        parts = [jump[:, 2], zeros, -jump[:, 0]]
    else:
        parts = [-jump[:, 1], jump[:, 0], zeros]
    return jnp.stack(parts, axis=1)


def outer_rims(lower, upper, elem_dim):
    count = lower.shape[elem_dim]
    return jnp.concatenate(
        [
            lax.slice_in_dim(lower, 0, 1, axis=elem_dim),
            lax.slice_in_dim(upper, count - 1, count, axis=elem_dim),
        ],
        axis=elem_dim,
    )


def split_arrived(arrived, elem_dim):
    return (
        lax.slice_in_dim(arrived, 0, 1, axis=elem_dim),
        lax.slice_in_dim(arrived, 3, 4, axis=elem_dim),
    )


def device_borders(direction, lower, upper):
    elem_dim = 4 + direction
    if direction == 2:
        empty = jnp.zeros_like(lax.slice_in_dim(lower, 0, 1, axis=elem_dim))
        return (empty, empty)
    outgoing = outer_rims(lower, upper, elem_dim)
    if direction == 0:
        arrived = padded(outgoing, (("gx", 4),), 1)
    else:
        arrived = padded(outgoing, (("gy", 5),), 1)
    return split_arrived(arrived, elem_dim)


def tendency(field, speed):
    table = derivative_table()
    elec = cross_speed(speed, field)
    result = jnp.stack(
        [
            along(table, elec[:, 2], 1) - along(table, elec[:, 1], 2),
            along(table, elec[:, 0], 2) - along(table, elec[:, 2], 0),
            along(table, elec[:, 1], 0) - along(table, elec[:, 0], 1),
        ],
        axis=1,
    )
    packed = jnp.concatenate([elec, field], axis=1)
    for direction in range(3):
        node_dim = 2 + direction
        elem_dim = 4 + direction
        lower = lax.index_in_dim(packed, 0, node_dim, keepdims=False)
        upper = lax.index_in_dim(packed, 3, node_dim, keepdims=False)
        recv_low, recv_high = device_borders(direction, lower, upper)
        count = lower.shape[elem_dim]
        outer_high = jnp.concatenate(
            [lax.slice_in_dim(lower, 1, count, axis=elem_dim), recv_high], axis=elem_dim
        )
        outer_low = jnp.concatenate(
            [recv_low, lax.slice_in_dim(upper, 0, count - 1, axis=elem_dim)], axis=elem_dim
        )
        jump_high = outer_high - upper
        jump_low = outer_low - lower
        term_high = (
            FLUX_COEF * normal_cross(direction, jump_high[:, :3]) + PENALTY * jump_high[:, 3:]
        )
        term_low = -FLUX_COEF * normal_cross(direction, jump_low[:, :3]) + PENALTY * jump_low[:, 3:]
        high_index = (slice(None),) * node_dim + (3,)
        low_index = (slice(None),) * node_dim + (0,)
        result = result.at[high_index].add(term_high)
        result = result.at[low_index].add(term_low)
    return result


def advance(field, speed):
    first = tendency(field, speed)
    middle = field + STEP_SIZE * first
    second = tendency(middle, speed)
    return field + 0.5 * STEP_SIZE * (first + second)


def relayout(block):
    groups_x = lax.axis_size("gx")
    groups_y = lax.axis_size("gy")
    phases, comps, nodes, slab, wide_x, wide_y = block.shape
    elem_x = wide_x // groups_x
    elem_y = wide_y // groups_y
    pieces = block.reshape(phases, comps, nodes, slab, groups_x, elem_x, groups_y, elem_y)
    pieces = jnp.transpose(pieces, (0, 1, 2, 3, 4, 6, 5, 7))
    pieces = pieces.reshape(phases, comps, nodes, slab, groups_x * groups_y, elem_x * elem_y)
    moved = lax.all_to_all(pieces, ("gx", "gy"), split_axis=4, concat_axis=3, tiled=True)
    moved = jnp.transpose(moved, (0, 1, 2, 4, 5, 3))
    return moved.reshape(phases, comps, 4, 4, 4, elem_x, elem_y, groups_x * groups_y * slab)


def shards(fields, velocity):
    krylov, comps, nodes, elem_x, elem_y, depth = fields.shape
    state = fields.reshape(krylov, comps, 4, 4, 4, elem_x, elem_y, depth)
    phase_count = velocity.shape[0]
    for step in range(phase_count):
        speed = relayout(velocity[step : step + 1])[0]
        state = advance(state, speed)
    return state.reshape(krylov, comps, nodes, elem_x, elem_y, depth)


def solution(mesh):
    return jax.shard_map(
        shards,
        mesh=mesh,
        in_specs=(
            P(None, None, None, "gx", "gy", None),
            P(None, None, None, ("gx", "gy"), None, None),
        ),
        out_specs=P(None, None, None, "gx", "gy", None),
        check_vma=False,
    )
```

profile of v0, /device:TPU:13, one launch (start us, length us, event | category | flops | bytes accessed | tf_op | source)
XLA Modules:
  0.0 210.2 jit_solution(16279374425056423833)
XLA Ops:
  2.5 10.7 %all-to-all-start = ((f32[128,1,384]{2,1,0:T(1,128)}), f32[128,1,384]{2,1,0:T(1,128)S(1)}, u32[]{:S(2)}, u32[]{:S(2)}) async-start(f32[128,1,384]{2,1,0:T(1,128)} %reshape.2771), calls=%async_computation | async-start | bytes 393216 | tf_op jit(solution)/shard_map/all_to_all | solution.py:155
  15.2 5.1 %all-to-all-done = f32[128,1,384]{2,1,0:T(1,128)S(1)} async-done(((f32[128,1,384]{2,1,0:T(1,128)}), f32[128,1,384]{2,1,0:T(1,128)S(1)}, u32[]{:S(2)}, u32[]{:S(2)}) %all-to-all-start) | async-done | bytes 196640 | tf_op jit(solution)/shard_map/all_to_all | solution.py:155
  20.3 8.2 %all-to-all-start.1 = ((f32[128,1,384]{2,1,0:T(1,128)}), f32[128,1,384]{2,1,0:T(1,128)S(1)}, u32[]{:S(2)}, u32[]{:S(2)}) async-start(f32[128,1,384]{2,1,0:T(1,128)} %reshape.2773), calls=%async_computation.1 | async-start | bytes 393216 | tf_op jit(solution)/shard_map/all_to_all | solution.py:155
  38.8 1.8 reduce.49
  42.8 1.7 fusion.1
  47.5 3.3 %collective-permute-start.3 = (f32[4,6,4,4,1,1,128]{6,5,2,0,1,3,4:T(1,128)S(1)}, f32[4,6,4,4,1,1,128]{6,5,2,0,1,3,4:T(1,128)S(1)}, u32[]{:S(2)}, u32[]{:S(2)}) collective-permute-start(f32[4,6,4,4,1,1,128]{6,5,2,0,1,3,4:T(1,128)S(1)} %get-tuple-element.408), channel_id=1, source_target_pairs={{0,1},{1,2},{2,3},{3,4},{4,5},{5,6},{6,7},{8,9},{9,10},{10,11},{11... | collective-permute-start | bytes 589832 | tf_op jit(solution)/shard_map/ppermute | solution.py:19
  51.1 2.9 %collective-permute-start.2 = (f32[4,6,4,4,1,1,128]{6,5,2,0,1,3,4:T(1,128)S(1)}, f32[4,6,4,4,1,1,128]{6,5,2,0,1,3,4:T(1,128)S(1)}, u32[]{:S(2)}, u32[]{:S(2)}) collective-permute-start(f32[4,6,4,4,1,1,128]{6,5,2,0,1,3,4:T(1,128)S(1)} %get-tuple-element.413), channel_id=1, source_target_pairs={{1,0},{2,1},{3,2},{4,3},{5,4},{6,5},{7,6},{9,8},{10,9},{11,10},{12... | collective-permute-start | bytes 589832 | tf_op jit(solution)/shard_map/ppermute | solution.py:20
  54.0 5.9 %collective-permute-start.1 = (f32[4,6,4,4,1,2,128]{6,5,0,1,2,3,4:T(2,128)S(1)}, f32[4,6,4,4,1,2,128]{6,5,0,1,2,3,4:T(2,128)S(1)}, u32[]{:S(2)}, u32[]{:S(2)}) collective-permute-start(f32[4,6,4,4,1,2,128]{6,5,0,1,2,3,4:T(2,128)S(1)} %copy-done.23), channel_id=1, source_target_pairs={{0,8},{8,16},{16,24},{24,32},{32,40},{40,48},{48,56},{56,64},{64,7... | collective-permute-start | bytes 1179656 | tf_op jit(solution)/shard_map/ppermute | solution.py:19
  59.9 13.2 %collective-permute-start = (f32[4,6,4,4,1,2,128]{6,5,0,1,2,3,4:T(2,128)S(1)}, f32[4,6,4,4,1,2,128]{6,5,0,1,2,3,4:T(2,128)S(1)}, u32[]{:S(2)}, u32[]{:S(2)}) collective-permute-start(f32[4,6,4,4,1,2,128]{6,5,0,1,2,3,4:T(2,128)S(1)} %copy-done.22), channel_id=1, source_target_pairs={{8,0},{16,8},{24,16},{32,24},{40,32},{48,40},{56,48},{64,56},{72,6... | collective-permute-start | bytes 1179656 | tf_op jit(solution)/shard_map/ppermute | solution.py:20
  73.9 1.5 pad_subtract_fusion.6
  79.4 4.0 %scatter-add.84 = f32[4,3,4,4,4,1,2,128]{7,3,6,4,2,0,5,1:T(4,128)S(1)} dynamic-update-slice(f32[4,3,4,4,4,1,2,128]{7,3,6,4,2,0,5,1:T(4,128)S(1)} %copy_dynamic-update-slice_fusion.3, f32[4,3,4,1,4,1,2,128]{7,3,6,4,2,0,5,1:T(1,128)S(1)} %copy.512, s32[]{:T(128)} %constant.525.clone.1, s32[]{:T(128)} %constant.525.clone.1, s32[]{:T(128)} %constant.525.clone.1, s32[]{:T(128)} %constant.526.clone.1, ...) | dynamic-update-slice | bytes 393220 | tf_op jit(solution)/shard_map/scatter-add | solution.py:134
  84.1 4.0 %scatter-add.85 = f32[4,3,4,4,4,1,2,128]{7,3,6,4,2,0,5,1:T(4,128)S(1)} dynamic-update-slice(f32[4,3,4,4,4,1,2,128]{7,3,6,4,2,0,5,1:T(4,128)S(1)} %scatter-add.84, f32[4,3,4,1,4,1,2,128]{7,3,6,4,2,0,5,1:T(1,128)S(1)} %copy.515, s32[]{:T(128)} %constant.525.clone.1, s32[]{:T(128)} %constant.525.clone.1, s32[]{:T(128)} %constant.525.clone.1, s32[]{:T(128)} %constant.525.clone.1, ...) | dynamic-update-slice | bytes 393220 | tf_op jit(solution)/shard_map/scatter-add | solution.py:135
  97.2 1.9 collective-permute-start.7
  99.5 4.3 %collective-permute-start.6 = (f32[4,6,4,4,1,1,128]{6,5,2,0,1,3,4:T(1,128)S(1)}, f32[4,6,4,4,1,1,128]{6,5,2,0,1,3,4:T(1,128)S(1)}, u32[]{:S(2)}, u32[]{:S(2)}) collective-permute-start(f32[4,6,4,4,1,1,128]{6,5,2,0,1,3,4:T(1,128)S(1)} %get-tuple-element.397), channel_id=1, source_target_pairs={{1,0},{2,1},{3,2},{4,3},{5,4},{6,5},{7,6},{9,8},{10,9},{11,10},{12... | collective-permute-start | bytes 589832 | tf_op jit(solution)/shard_map/ppermute | solution.py:20
  104.3 3.6 %collective-permute-start.4 = (f32[4,6,4,4,1,2,128]{6,5,0,1,3,2,4:T(2,128)S(1)}, f32[4,6,4,4,1,2,128]{6,5,0,1,3,2,4:T(2,128)S(1)}, u32[]{:S(2)}, u32[]{:S(2)}) collective-permute-start(f32[4,6,4,4,1,2,128]{6,5,0,1,3,2,4:T(2,128)S(1)} %bitcast.544), channel_id=1, source_target_pairs={{8,0},{16,8},{24,16},{32,24},{40,32},{48,40},{56,48},{64,56},{72,6... | collective-permute-start | bytes 1179656 | tf_op jit(solution)/shard_map/ppermute | solution.py:20
  107.8 4.5 %collective-permute-start.5 = (f32[4,6,4,4,1,2,128]{6,5,0,1,3,2,4:T(2,128)S(1)}, f32[4,6,4,4,1,2,128]{6,5,0,1,3,2,4:T(2,128)S(1)}, u32[]{:S(2)}, u32[]{:S(2)}) collective-permute-start(f32[4,6,4,4,1,2,128]{6,5,0,1,3,2,4:T(2,128)S(1)} %bitcast.541), channel_id=1, source_target_pairs={{0,8},{8,16},{16,24},{24,32},{32,40},{40,48},{48,56},{56,64},{64,7... | collective-permute-start | bytes 1179656 | tf_op jit(solution)/shard_map/ppermute | solution.py:19
  113.4 1.9 collective-permute-done.6
  116.9 3.3 %collective-permute-done.4 = f32[4,6,4,4,1,2,128]{6,5,0,1,3,2,4:T(2,128)S(1)} collective-permute-done((f32[4,6,4,4,1,2,128]{6,5,0,1,3,2,4:T(2,128)S(1)}, f32[4,6,4,4,1,2,128]{6,5,0,1,3,2,4:T(2,128)S(1)}, u32[]{:S(2)}, u32[]{:S(2)}) %collective-permute-start.4) | collective-permute-done | bytes 393248 | tf_op jit(solution)/shard_map/ppermute | solution.py:20
  131.9 1.9 collective-permute-start.11
  134.2 4.3 %collective-permute-start.10 = (f32[4,6,4,4,1,1,128]{6,5,2,0,1,3,4:T(1,128)S(1)}, f32[4,6,4,4,1,1,128]{6,5,2,0,1,3,4:T(1,128)S(1)}, u32[]{:S(2)}, u32[]{:S(2)}) collective-permute-start(f32[4,6,4,4,1,1,128]{6,5,2,0,1,3,4:T(1,128)S(1)} %get-tuple-element.381), channel_id=1, source_target_pairs={{1,0},{2,1},{3,2},{4,3},{5,4},{6,5},{7,6},{9,8},{10,9},{11,10},{12... | collective-permute-start | bytes 589832 | tf_op jit(solution)/shard_map/ppermute | solution.py:20
  139.0 1.9 collective-permute-start.8
  140.9 5.1 %collective-permute-start.9 = (f32[4,6,4,4,1,2,128]{6,5,0,1,3,2,4:T(2,128)S(1)}, f32[4,6,4,4,1,2,128]{6,5,0,1,3,2,4:T(2,128)S(1)}, u32[]{:S(2)}, u32[]{:S(2)}) collective-permute-start(f32[4,6,4,4,1,2,128]{6,5,0,1,3,2,4:T(2,128)S(1)} %bitcast.540), channel_id=1, source_target_pairs={{0,8},{8,16},{16,24},{24,32},{32,40},{40,48},{48,56},{56,64},{64,7... | collective-permute-start | bytes 1179656 | tf_op jit(solution)/shard_map/ppermute | solution.py:19
  147.1 2.2 %collective-permute-done.10 = f32[4,6,4,4,1,1,128]{6,5,2,0,1,3,4:T(1,128)S(1)} collective-permute-done((f32[4,6,4,4,1,1,128]{6,5,2,0,1,3,4:T(1,128)S(1)}, f32[4,6,4,4,1,1,128]{6,5,2,0,1,3,4:T(1,128)S(1)}, u32[]{:S(2)}, u32[]{:S(2)}) %collective-permute-start.10) | collective-permute-done | bytes 196640 | tf_op jit(solution)/shard_map/ppermute | solution.py:20
  149.3 1.5 pad_subtract_fusion.2
  151.2 2.6 %collective-permute-done.8 = f32[4,6,4,4,1,2,128]{6,5,0,1,3,2,4:T(2,128)S(1)} collective-permute-done((f32[4,6,4,4,1,2,128]{6,5,0,1,3,2,4:T(2,128)S(1)}, f32[4,6,4,4,1,2,128]{6,5,0,1,3,2,4:T(2,128)S(1)}, u32[]{:S(2)}, u32[]{:S(2)}) %collective-permute-start.8) | collective-permute-done | bytes 393248 | tf_op jit(solution)/shard_map/ppermute | solution.py:20
  156.9 7.4 %scatter-add.106 = f32[4,3,4,4,4,1,2,128]{7,4,6,2,0,1,5,3:T(4,128)S(1)} dynamic-update-slice(f32[4,3,4,4,4,1,2,128]{7,4,6,2,0,1,5,3:T(4,128)S(1)} %fusion.141, f32[4,3,4,4,1,1,2,128]{7,4,6,2,0,1,5,3:T(1,128)S(1)} %bitcast.534, s32[]{:T(128)} %constant.525.clone.1, s32[]{:T(128)} %constant.525.clone.1, s32[]{:T(128)} %constant.525.clone.1, s32[]{:T(128)} %constant.525.clone.1, ...) | dynamic-update-slice | bytes 393220 | tf_op jit(solution)/shard_map/scatter-add | solution.py:134
  164.7 7.2 %scatter-add.109 = f32[4,3,4,4,4,1,2,128]{7,4,6,2,0,1,5,3:T(4,128)S(1)} dynamic-update-slice(f32[4,3,4,4,4,1,2,128]{7,4,6,2,0,1,5,3:T(4,128)S(1)} %scatter-add.106, f32[4,3,4,4,1,1,2,128]{7,4,6,2,0,1,5,3:T(1,128)S(1)} %bitcast.535, s32[]{:T(128)} %constant.525.clone.1, s32[]{:T(128)} %constant.525.clone.1, s32[]{:T(128)} %constant.525.clone.1, s32[]{:T(128)} %constant.525.clone.1, ...) | dynamic-update-slice | bytes 393220 | tf_op jit(solution)/shard_map/scatter-add | solution.py:135
  181.4 1.9 collective-permute-start.15
  183.9 4.5 %collective-permute-start.14 = (f32[4,6,4,4,1,1,128]{6,5,2,0,1,3,4:T(1,128)S(1)}, f32[4,6,4,4,1,1,128]{6,5,2,0,1,3,4:T(1,128)S(1)}, u32[]{:S(2)}, u32[]{:S(2)}) collective-permute-start(f32[4,6,4,4,1,1,128]{6,5,2,0,1,3,4:T(1,128)S(1)} %get-tuple-element.365), channel_id=1, source_target_pairs={{1,0},{2,1},{3,2},{4,3},{5,4},{6,5},{7,6},{9,8},{10,9},{11,10},{12... | collective-permute-start | bytes 589832 | tf_op jit(solution)/shard_map/ppermute | solution.py:20
  189.1 1.9 collective-permute-start.12
  191.0 5.1 %collective-permute-start.13 = (f32[4,6,4,4,1,2,128]{6,5,0,1,3,2,4:T(2,128)S(1)}, f32[4,6,4,4,1,2,128]{6,5,0,1,3,2,4:T(2,128)S(1)}, u32[]{:S(2)}, u32[]{:S(2)}) collective-permute-start(f32[4,6,4,4,1,2,128]{6,5,0,1,3,2,4:T(2,128)S(1)} %bitcast.542), channel_id=1, source_target_pairs={{0,8},{8,16},{16,24},{24,32},{32,40},{40,48},{48,56},{56,64},{64,7... | collective-permute-start | bytes 1179656 | tf_op jit(solution)/shard_map/ppermute | solution.py:19
  198.5 5.5 %collective-permute-done.12 = f32[4,6,4,4,1,2,128]{6,5,0,1,3,2,4:T(2,128)S(1)} collective-permute-done((f32[4,6,4,4,1,2,128]{6,5,0,1,3,2,4:T(2,128)S(1)}, f32[4,6,4,4,1,2,128]{6,5,0,1,3,2,4:T(2,128)S(1)}, u32[]{:S(2)}, u32[]{:S(2)}) %collective-permute-start.12) | collective-permute-done | bytes 393248 | tf_op jit(solution)/shard_map/ppermute | solution.py:20
  (272 shorter events, 73.2 us)
Async XLA Ops:
  0.0 13.2 %copy-start.21 = (f32[4,3,64,1,2,128]{5,4,3,2,1,0:T(2,128)S(1)}, f32[4,3,64,1,2,128]{5,4,3,2,1,0:T(2,128)}, u32[]{:S(2)}) copy-start(f32[4,3,64,1,2,128]{5,4,3,2,1,0:T(2,128)} %param.54) | copy-start | bytes 2359300
  2.5 17.8 %all-to-all-start = ((f32[128,1,384]{2,1,0:T(1,128)}), f32[128,1,384]{2,1,0:T(1,128)S(1)}, u32[]{:S(2)}, u32[]{:S(2)}) async-start(f32[128,1,384]{2,1,0:T(1,128)} %reshape.2771), calls=%async_computation | async-start | bytes 393216 | tf_op jit(solution)/shard_map/all_to_all | solution.py:155
  20.3 18.5 %all-to-all-start.1 = ((f32[128,1,384]{2,1,0:T(1,128)}), f32[128,1,384]{2,1,0:T(1,128)S(1)}, u32[]{:S(2)}, u32[]{:S(2)}) async-start(f32[128,1,384]{2,1,0:T(1,128)} %reshape.2773), calls=%async_computation.1 | async-start | bytes 393216 | tf_op jit(solution)/shard_map/all_to_all | solution.py:155
  37.3 4.9 %copy-start.3 = (f32[4,4,4,4,2,128]{5,4,1,0,2,3:T(2,128)S(1)}, f32[4,4,4,4,2,128]{5,4,1,0,2,3:T(2,128)}, u32[]{:S(2)}) copy-start(f32[4,4,4,4,2,128]{5,4,1,0,2,3:T(2,128)} %get-tuple-element.346) | copy-start | bytes 786436
  46.3 7.6 %copy-start.23 = (f32[4,6,4,4,1,2,128]{6,5,0,1,2,3,4:T(2,128)S(1)}, f32[4,6,4,4,1,2,128]{6,5,0,1,2,3,4:T(2,128)}, u32[]{:S(2)}) copy-start(f32[4,6,4,4,1,2,128]{6,5,0,1,2,3,4:T(2,128)} %get-tuple-element.329) | copy-start | bytes 1179652
  46.4 13.5 %copy-start.22 = (f32[4,6,4,4,1,2,128]{6,5,0,1,2,3,4:T(2,128)S(1)}, f32[4,6,4,4,1,2,128]{6,5,0,1,2,3,4:T(2,128)}, u32[]{:S(2)}) copy-start(f32[4,6,4,4,1,2,128]{6,5,0,1,2,3,4:T(2,128)} %get-tuple-element.330) | copy-start | bytes 1179652
  46.7 26.7 %copy-start = (f32[4,3,4,4,4,1,2,128]{7,3,6,4,2,0,5,1:T(4,128)}, f32[4,3,4,4,4,1,2,128]{7,3,6,4,2,0,5,1:T(4,128)S(1)}, u32[]{:S(2)}) copy-start(f32[4,3,4,4,4,1,2,128]{7,3,6,4,2,0,5,1:T(4,128)S(1)} %pad_maximum_fusion.4) | copy-start | bytes 2359300
  47.5 26.4 %collective-permute-start.3 = (f32[4,6,4,4,1,1,128]{6,5,2,0,1,3,4:T(1,128)S(1)}, f32[4,6,4,4,1,1,128]{6,5,2,0,1,3,4:T(1,128)S(1)}, u32[]{:S(2)}, u32[]{:S(2)}) collective-permute-start(f32[4,6,4,4,1,1,128]{6,5,2,0,1,3,4:T(1,128)S(1)} %get-tuple-element.408), channel_id=1, source_target_pairs={{0,1},{1,2},{2,3},{3,4},{4,5},{5,6},{6,7},{8,9},{9,10},{10,11},{11... | collective-permute-start | bytes 589832 | tf_op jit(solution)/shard_map/ppermute | solution.py:19
  51.1 22.8 %collective-permute-start.2 = (f32[4,6,4,4,1,1,128]{6,5,2,0,1,3,4:T(1,128)S(1)}, f32[4,6,4,4,1,1,128]{6,5,2,0,1,3,4:T(1,128)S(1)}, u32[]{:S(2)}, u32[]{:S(2)}) collective-permute-start(f32[4,6,4,4,1,1,128]{6,5,2,0,1,3,4:T(1,128)S(1)} %get-tuple-element.413), channel_id=1, source_target_pairs={{1,0},{2,1},{3,2},{4,3},{5,4},{6,5},{7,6},{9,8},{10,9},{11,10},{12... | collective-permute-start | bytes 589832 | tf_op jit(solution)/shard_map/ppermute | solution.py:20
  54.0 23.1 %collective-permute-start.1 = (f32[4,6,4,4,1,2,128]{6,5,0,1,2,3,4:T(2,128)S(1)}, f32[4,6,4,4,1,2,128]{6,5,0,1,2,3,4:T(2,128)S(1)}, u32[]{:S(2)}, u32[]{:S(2)}) collective-permute-start(f32[4,6,4,4,1,2,128]{6,5,0,1,2,3,4:T(2,128)S(1)} %copy-done.23), channel_id=1, source_target_pairs={{0,8},{8,16},{16,24},{24,32},{32,40},{40,48},{48,56},{56,64},{64,7... | collective-permute-start | bytes 1179656 | tf_op jit(solution)/shard_map/ppermute | solution.py:19
  59.9 17.2 %collective-permute-start = (f32[4,6,4,4,1,2,128]{6,5,0,1,2,3,4:T(2,128)S(1)}, f32[4,6,4,4,1,2,128]{6,5,0,1,2,3,4:T(2,128)S(1)}, u32[]{:S(2)}, u32[]{:S(2)}) collective-permute-start(f32[4,6,4,4,1,2,128]{6,5,0,1,2,3,4:T(2,128)S(1)} %copy-done.22), channel_id=1, source_target_pairs={{8,0},{16,8},{24,16},{32,24},{40,32},{48,40},{56,48},{64,56},{72,6... | collective-permute-start | bytes 1179656 | tf_op jit(solution)/shard_map/ppermute | solution.py:20
  78.7 4.9 %copy-start.17 = (f32[4,6,4,4,1,2,128]{6,5,2,0,1,3,4:T(2,128)S(1)}, f32[4,6,4,4,1,2,128]{6,5,2,0,1,3,4:T(2,128)}, u32[]{:S(2)}) copy-start(f32[4,6,4,4,1,2,128]{6,5,2,0,1,3,4:T(2,128)} %copy-done.16) | copy-start | bytes 1179652
  78.7 4.9 %copy-start.28 = (f32[4,1,4,4,1,2,128]{6,5,2,0,1,3,4:T(2,128)S(1)}, f32[4,1,4,4,1,2,128]{6,5,2,0,1,3,4:T(2,128)}, u32[]{:S(2)}) copy-start(f32[4,1,4,4,1,2,128]{6,5,2,0,1,3,4:T(2,128)} %get-tuple-element.406) | copy-start | bytes 196612
  78.7 4.9 %copy-start.29 = (f32[4,1,4,4,1,2,128]{6,5,2,0,1,3,4:T(2,128)S(1)}, f32[4,1,4,4,1,2,128]{6,5,2,0,1,3,4:T(2,128)}, u32[]{:S(2)}) copy-start(f32[4,1,4,4,1,2,128]{6,5,2,0,1,3,4:T(2,128)} %get-tuple-element.407) | copy-start | bytes 196612
  79.2 8.9 %copy-start.15 = (f32[4,6,4,4,1,2,128]{6,5,2,0,1,3,4:T(2,128)S(1)}, f32[4,6,4,4,1,2,128]{6,5,2,0,1,3,4:T(2,128)}, u32[]{:S(2)}) copy-start(f32[4,6,4,4,1,2,128]{6,5,2,0,1,3,4:T(2,128)} %copy-done.14) | copy-start | bytes 1179652
  79.2 8.9 %copy-start.26 = (f32[4,1,4,4,1,2,128]{6,5,2,0,1,3,4:T(2,128)S(1)}, f32[4,1,4,4,1,2,128]{6,5,2,0,1,3,4:T(2,128)}, u32[]{:S(2)}) copy-start(f32[4,1,4,4,1,2,128]{6,5,2,0,1,3,4:T(2,128)} %get-tuple-element.432) | copy-start | bytes 196612
  79.2 8.9 %copy-start.27 = (f32[4,1,4,4,1,2,128]{6,5,2,0,1,3,4:T(2,128)S(1)}, f32[4,1,4,4,1,2,128]{6,5,2,0,1,3,4:T(2,128)}, u32[]{:S(2)}) copy-start(f32[4,1,4,4,1,2,128]{6,5,2,0,1,3,4:T(2,128)} %get-tuple-element.433) | copy-start | bytes 196612
  83.8 4.7 %copy-start.13 = (f32[4,6,4,4,1,2,128]{6,5,2,0,1,3,4:T(2,128)S(1)}, f32[4,6,4,4,1,2,128]{6,5,2,0,1,3,4:T(2,128)}, u32[]{:S(2)}) copy-start(f32[4,6,4,4,1,2,128]{6,5,2,0,1,3,4:T(2,128)} %copy-done.12) | copy-start | bytes 1179652
  83.8 4.7 %copy-start.24 = (f32[4,1,4,4,1,2,128]{6,5,2,0,1,3,4:T(2,128)S(1)}, f32[4,1,4,4,1,2,128]{6,5,2,0,1,3,4:T(2,128)}, u32[]{:S(2)}) copy-start(f32[4,1,4,4,1,2,128]{6,5,2,0,1,3,4:T(2,128)} %get-tuple-element.402) | copy-start | bytes 196612
  83.8 4.7 %copy-start.25 = (f32[4,1,4,4,1,2,128]{6,5,2,0,1,3,4:T(2,128)S(1)}, f32[4,1,4,4,1,2,128]{6,5,2,0,1,3,4:T(2,128)}, u32[]{:S(2)}) copy-start(f32[4,1,4,4,1,2,128]{6,5,2,0,1,3,4:T(2,128)} %get-tuple-element.403) | copy-start | bytes 196612
  97.2 16.1 %collective-permute-start.7 = (f32[4,6,4,4,1,1,128]{6,5,2,0,1,3,4:T(1,128)S(1)}, f32[4,6,4,4,1,1,128]{6,5,2,0,1,3,4:T(1,128)S(1)}, u32[]{:S(2)}, u32[]{:S(2)}) collective-permute-start(f32[4,6,4,4,1,1,128]{6,5,2,0,1,3,4:T(1,128)S(1)} %get-tuple-element.392), channel_id=1, source_target_pairs={{0,1},{1,2},{2,3},{3,4},{4,5},{5,6},{6,7},{8,9},{9,10},{10,11},{11... | collective-permute-start | bytes 589832 | tf_op jit(solution)/shard_map/ppermute | solution.py:19
  99.5 15.8 %collective-permute-start.6 = (f32[4,6,4,4,1,1,128]{6,5,2,0,1,3,4:T(1,128)S(1)}, f32[4,6,4,4,1,1,128]{6,5,2,0,1,3,4:T(1,128)S(1)}, u32[]{:S(2)}, u32[]{:S(2)}) collective-permute-start(f32[4,6,4,4,1,1,128]{6,5,2,0,1,3,4:T(1,128)S(1)} %get-tuple-element.397), channel_id=1, source_target_pairs={{1,0},{2,1},{3,2},{4,3},{5,4},{6,5},{7,6},{9,8},{10,9},{11,10},{12... | collective-permute-start | bytes 589832 | tf_op jit(solution)/shard_map/ppermute | solution.py:20
  104.3 16.0 %collective-permute-start.4 = (f32[4,6,4,4,1,2,128]{6,5,0,1,3,2,4:T(2,128)S(1)}, f32[4,6,4,4,1,2,128]{6,5,0,1,3,2,4:T(2,128)S(1)}, u32[]{:S(2)}, u32[]{:S(2)}) collective-permute-start(f32[4,6,4,4,1,2,128]{6,5,0,1,3,2,4:T(2,128)S(1)} %bitcast.544), channel_id=1, source_target_pairs={{8,0},{16,8},{24,16},{32,24},{40,32},{48,40},{56,48},{64,56},{72,6... | collective-permute-start | bytes 1179656 | tf_op jit(solution)/shard_map/ppermute | solution.py:20
  107.8 12.7 %collective-permute-start.5 = (f32[4,6,4,4,1,2,128]{6,5,0,1,3,2,4:T(2,128)S(1)}, f32[4,6,4,4,1,2,128]{6,5,0,1,3,2,4:T(2,128)S(1)}, u32[]{:S(2)}, u32[]{:S(2)}) collective-permute-start(f32[4,6,4,4,1,2,128]{6,5,0,1,3,2,4:T(2,128)S(1)} %bitcast.541), channel_id=1, source_target_pairs={{0,8},{8,16},{16,24},{24,32},{32,40},{40,48},{48,56},{56,64},{64,7... | collective-permute-start | bytes 1179656 | tf_op jit(solution)/shard_map/ppermute | solution.py:19
  131.9 15.2 %collective-permute-start.11 = (f32[4,6,4,4,1,1,128]{6,5,2,0,1,3,4:T(1,128)S(1)}, f32[4,6,4,4,1,1,128]{6,5,2,0,1,3,4:T(1,128)S(1)}, u32[]{:S(2)}, u32[]{:S(2)}) collective-permute-start(f32[4,6,4,4,1,1,128]{6,5,2,0,1,3,4:T(1,128)S(1)} %get-tuple-element.376), channel_id=1, source_target_pairs={{0,1},{1,2},{2,3},{3,4},{4,5},{5,6},{6,7},{8,9},{9,10},{10,11},{11... | collective-permute-start | bytes 589832 | tf_op jit(solution)/shard_map/ppermute | solution.py:19
  134.2 15.2 %collective-permute-start.10 = (f32[4,6,4,4,1,1,128]{6,5,2,0,1,3,4:T(1,128)S(1)}, f32[4,6,4,4,1,1,128]{6,5,2,0,1,3,4:T(1,128)S(1)}, u32[]{:S(2)}, u32[]{:S(2)}) collective-permute-start(f32[4,6,4,4,1,1,128]{6,5,2,0,1,3,4:T(1,128)S(1)} %get-tuple-element.381), channel_id=1, source_target_pairs={{1,0},{2,1},{3,2},{4,3},{5,4},{6,5},{7,6},{9,8},{10,9},{11,10},{12... | collective-permute-start | bytes 589832 | tf_op jit(solution)/shard_map/ppermute | solution.py:20
  139.0 14.8 %collective-permute-start.8 = (f32[4,6,4,4,1,2,128]{6,5,0,1,3,2,4:T(2,128)S(1)}, f32[4,6,4,4,1,2,128]{6,5,0,1,3,2,4:T(2,128)S(1)}, u32[]{:S(2)}, u32[]{:S(2)}) collective-permute-start(f32[4,6,4,4,1,2,128]{6,5,0,1,3,2,4:T(2,128)S(1)} %bitcast.543), channel_id=1, source_target_pairs={{8,0},{16,8},{24,16},{32,24},{40,32},{48,40},{56,48},{64,56},{72,6... | collective-permute-start | bytes 1179656 | tf_op jit(solution)/shard_map/ppermute | solution.py:20
  140.9 13.1 %collective-permute-start.9 = (f32[4,6,4,4,1,2,128]{6,5,0,1,3,2,4:T(2,128)S(1)}, f32[4,6,4,4,1,2,128]{6,5,0,1,3,2,4:T(2,128)S(1)}, u32[]{:S(2)}, u32[]{:S(2)}) collective-permute-start(f32[4,6,4,4,1,2,128]{6,5,0,1,3,2,4:T(2,128)S(1)} %bitcast.540), channel_id=1, source_target_pairs={{0,8},{8,16},{16,24},{24,32},{32,40},{40,48},{48,56},{56,64},{64,7... | collective-permute-start | bytes 1179656 | tf_op jit(solution)/shard_map/ppermute | solution.py:19
  181.4 15.9 %collective-permute-start.15 = (f32[4,6,4,4,1,1,128]{6,5,2,0,1,3,4:T(1,128)S(1)}, f32[4,6,4,4,1,1,128]{6,5,2,0,1,3,4:T(1,128)S(1)}, u32[]{:S(2)}, u32[]{:S(2)}) collective-permute-start(f32[4,6,4,4,1,1,128]{6,5,2,0,1,3,4:T(1,128)S(1)} %get-tuple-element.360), channel_id=1, source_target_pairs={{0,1},{1,2},{2,3},{3,4},{4,5},{5,6},{6,7},{8,9},{9,10},{10,11},{11... | collective-permute-start | bytes 589832 | tf_op jit(solution)/shard_map/ppermute | solution.py:19
  183.9 14.0 %collective-permute-start.14 = (f32[4,6,4,4,1,1,128]{6,5,2,0,1,3,4:T(1,128)S(1)}, f32[4,6,4,4,1,1,128]{6,5,2,0,1,3,4:T(1,128)S(1)}, u32[]{:S(2)}, u32[]{:S(2)}) collective-permute-start(f32[4,6,4,4,1,1,128]{6,5,2,0,1,3,4:T(1,128)S(1)} %get-tuple-element.365), channel_id=1, source_target_pairs={{1,0},{2,1},{3,2},{4,3},{5,4},{6,5},{7,6},{9,8},{10,9},{11,10},{12... | collective-permute-start | bytes 589832 | tf_op jit(solution)/shard_map/ppermute | solution.py:20
  189.1 14.8 %collective-permute-start.12 = (f32[4,6,4,4,1,2,128]{6,5,0,1,3,2,4:T(2,128)S(1)}, f32[4,6,4,4,1,2,128]{6,5,0,1,3,2,4:T(2,128)S(1)}, u32[]{:S(2)}, u32[]{:S(2)}) collective-permute-start(f32[4,6,4,4,1,2,128]{6,5,0,1,3,2,4:T(2,128)S(1)} %bitcast.545), channel_id=1, source_target_pairs={{8,0},{16,8},{24,16},{32,24},{40,32},{48,40},{56,48},{64,56},{72,6... | collective-permute-start | bytes 1179656 | tf_op jit(solution)/shard_map/ppermute | solution.py:20
  191.0 13.2 %collective-permute-start.13 = (f32[4,6,4,4,1,2,128]{6,5,0,1,3,2,4:T(2,128)S(1)}, f32[4,6,4,4,1,2,128]{6,5,0,1,3,2,4:T(2,128)S(1)}, u32[]{:S(2)}, u32[]{:S(2)}) collective-permute-start(f32[4,6,4,4,1,2,128]{6,5,0,1,3,2,4:T(2,128)S(1)} %bitcast.542), channel_id=1, source_target_pairs={{0,8},{8,16},{16,24},{24,32},{32,40},{40,48},{48,56},{56,64},{64,7... | collective-permute-start | bytes 1179656 | tf_op jit(solution)/shard_map/ppermute | solution.py:19
  (18 other events, 35.4 us)
where the time goes:
time: 214 us; the launch traced here: 210 us
  starting transfers between devices  85.1 us (40%)
  local copies, waits for them, and re-layouts  49.2 us (23%)
  other arithmetic  34.3 us (16%)
  waiting for transfers between devices  20.7 us (10%)
  matrix products  18.7 us (9%)
  between operations  2.17 us (1%)
    ppermute x8, starting transfers between devices, padded(): after = lax.ppermute(first, axis, down)  36.5 us
    ppermute x8, starting transfers between devices, padded(): before = lax.ppermute(last, axis, up)  29.7 us
    all_to_all x2, starting transfers between devices, relayout(): lax.all_to_all(pieces, ('gx', 'gy'), split_axis=4, concat_axis=3, tiled=T...  18.9 us
    dot_general x24, matrix products, along(): jnp.einsum(forms[direction], table, block, precision=lax.Precision.HIGHEST)  18.7 us
    ppermute x8, waiting for transfers between devices, padded(): after = lax.ppermute(first, axis, down)  15.6 us
    scatter-add x9, local copies, waits for them, and re-layouts, tendency(): result = result.at[high_index].add(term_high)  13.5 us
    scatter-add x6, local copies, waits for them, and re-layouts, tendency(): result = result.at[low_index].add(term_low)  12.3 us
    sub x9, other arithmetic, tendency(): jump_low = outer_low - lower  6.67 us
  transfers between devices with their start and end apart: 18, of which 6 were waited for; matrix products, arithmetic and copies ran while one was open for 13% of the time, Pallas kernels for 0%

commit v1 on v0

v1 whole, which is shorter than its diff:
```python
import jax
import jax.numpy as jnp
import numpy as np
from jax import lax
from jax.experimental import pallas as pl
from jax.experimental.pallas import tpu as pltpu
from jax.sharding import PartitionSpec as P

STEP_SIZE = 0.025
FLUX_COEF = 3.0
KRYLOV = 4
SIDE = 4
LANES = 128
F32 = jnp.float32
VMEM_LIMIT = 24 * 1024 * 1024


def derivative_table():
    points = np.array([-1.0, -1.0 / np.sqrt(5.0), 1.0 / np.sqrt(5.0), 1.0])
    weights_bary = np.ones(4)
    for first in range(4):
        for second in range(4):
            if first != second:
                weights_bary[first] = weights_bary[first] / (points[first] - points[second])
    table = np.zeros((4, 4))
    for first in range(4):
        for second in range(4):
            if first != second:
                table[first, second] = (
                    weights_bary[second] / weights_bary[first] / (points[first] - points[second])
                )
        table[first, first] = -np.sum(table[first])
    return table.astype(np.float32).astype(np.float64)


TABLE = derivative_table()


def rows():
    return lax.broadcasted_iota(jnp.int32, (8, LANES), 0)


def lanes():
    return lax.broadcasted_iota(jnp.int32, (8, LANES), 1)


def roll_rows(value, shift):
    return pltpu.roll(value, shift % 8, 0)


def roll_lanes(value, shift):
    return pltpu.roll(value, shift % LANES, 1)


def cross(u, b):
    return [
        u[1] * b[2] - u[2] * b[1],
        u[2] * b[0] - u[0] * b[2],
        u[0] * b[1] - u[1] * b[0],
    ]


def plus(direction, b, e):
    if direction == 0:
        return [b[0], b[1] - e[2], b[2] + e[1]]
    if direction == 1:
        return [b[0] + e[2], b[1], b[2] - e[0]]
    return [b[0] - e[1], b[1] + e[0], b[2]]


def minus(direction, b, e):
    if direction == 0:
        return [b[0], b[1] + e[2], b[2] - e[1]]
    if direction == 1:
        return [b[0] - e[2], b[1], b[2] + e[0]]
    return [b[0] + e[1], b[1] - e[0], b[2]]


def speed_at(speed, a, b):
    start = (a * SIDE + b) * 8
    return [speed[i, start : start + 8, :] for i in range(3)]


def third_table(coef):
    node = rows() // 2
    parts = []
    for shift in range(SIDE):
        part = jnp.zeros((8, LANES), F32)
        for p in range(SIDE):
            part = jnp.where(node == p, F32(coef * TABLE[p, (p - shift) % SIDE]), part)
        parts.append(part)
    return parts


def weighted(row, terms):
    total = None
    for q in range(SIDE):
        if row[q] != 0.0:
            part = F32(row[q]) * terms[q]
            total = part if total is None else total + part
    return total


def volume(k, state, base, speed, elec, out, coef):
    row, lane = rows(), lanes()
    table = coef * TABLE
    third = third_table(coef)
    jump = FLUX_COEF * coef
    zero = jnp.zeros((8, LANES), F32)
    own_low = jnp.where(row < 2, F32(jump), zero)
    own_high = jnp.where(row >= 6, F32(jump), zero)
    in_low = jnp.where(lane > 0, own_low, zero)
    in_high = jnp.where(lane < LANES - 1, own_high, zero)
    odd = row % 2 == 1
    mid_low = jnp.where(odd, F32(jump), zero)
    mid_high = jnp.where(odd, zero, F32(jump))

    def along_third(value):
        total = third[0] * value
        for shift in range(1, SIDE):
            total = total + third[shift] * roll_rows(value, 2 * shift)
        return total

    for a in range(SIDE):
        for b in range(SIDE):
            field = [state[k, i, a, b] for i in range(3)]
            parts = cross(speed_at(speed, a, b), field)
            for i in range(3):
                elec[i, a, b] = parts[i]
    for a in range(SIDE):
        for b in range(SIDE):
            e = [elec[i, a, b] for i in range(3)]
            m = [state[k, i, a, b] for i in range(3)]
            total = [
                weighted(table[b], [elec[2, a, q] for q in range(SIDE)]) - along_third(e[1]),
                along_third(e[0]) - weighted(table[a], [elec[2, q, b] for q in range(SIDE)]),
                weighted(table[a], [elec[1, q, b] for q in range(SIDE)])
                - weighted(table[b], [elec[0, a, q] for q in range(SIDE)]),
            ]
            up, down = minus(2, m, e), plus(2, m, e)
            for i in range(3):
                total[i] = total[i] - (own_low * up[i] + own_high * down[i])
                total[i] = total[i] + in_low * roll_lanes(roll_rows(up[i], 2), 1)
                total[i] = total[i] + in_high * roll_lanes(roll_rows(down[i], -2), -1)
            if a == 0:
                own = minus(0, m, e)
                total = [t - F32(jump) * o for t, o in zip(total, own)]
            if a == SIDE - 1:
                own = plus(0, m, e)
                total = [t - F32(jump) * o for t, o in zip(total, own)]
            if b == 0:
                own = minus(1, m, e)
                far_b = [state[k, i, a, SIDE - 1] for i in range(3)]
                far_e = [elec[i, a, SIDE - 1] for i in range(3)]
                far = minus(1, far_b, far_e)
                total = [
                    t - F32(jump) * o + mid_low * roll_rows(f, 1)
                    for t, o, f in zip(total, own, far)
                ]
            if b == SIDE - 1:
                own = plus(1, m, e)
                far_b = [state[k, i, a, 0] for i in range(3)]
                far_e = [elec[i, a, 0] for i in range(3)]
                far = plus(1, far_b, far_e)
                total = [
                    t - F32(jump) * o + mid_high * roll_rows(f, -1)
                    for t, o, f in zip(total, own, far)
                ]
            start = base(k, a, b)
            for i in range(3):
                out[k, i, a, b] = start[i] + total[i]


def parities():
    return lax.axis_index("gx") % 2 == 1, lax.axis_index("gy") % 2 == 1


def pick(condition, yes, no):
    return jnp.where(condition, yes, no)


def pack_rows(first, second, keep_odd):
    odd = rows() % 2 == 1
    if keep_odd:
        return jnp.where(odd, second, roll_rows(first, -1))
    return jnp.where(odd, roll_rows(second, 1), first)


def send_faces(k, state, speed, px, py, x_even, x_odd, y_even, y_odd):
    def traces(direction, sign, a, b):
        m = [state[k, i, a, b] for i in range(3)]
        if speed is None:
            return m
        e = cross(speed_at(speed, a, b), m)
        return plus(direction, m, e) if sign > 0 else minus(direction, m, e)

    for b in range(SIDE):
        high = traces(0, -1, SIDE - 1, b)
        low = traces(0, 1, 0, b)
        for i in range(3):
            x_even[k, i, b] = pick(px, low[i], high[i])
            x_odd[k, i, b] = pick(px, high[i], low[i])
    for half in range(2):
        high = [traces(1, -1, 2 * half + s, SIDE - 1) for s in range(2)]
        low = [traces(1, 1, 2 * half + s, 0) for s in range(2)]
        for i in range(3):
            up = pack_rows(high[0][i], high[1][i], True)
            down = pack_rows(low[0][i], low[1][i], False)
            y_even[k, i, half] = pick(py, down, up)
            y_odd[k, i, half] = pick(py, up, down)


def receive_faces(k, pre, out, ghost_speed, px, py, x_even, x_odd, y_even, y_odd, coef):
    jump = FLUX_COEF * coef
    odd = rows() % 2 == 1
    zero = jnp.zeros((8, LANES), F32)
    mask_low = jnp.where(odd, zero, F32(jump))
    mask_high = jnp.where(odd, F32(jump), zero)
    turn = jnp.where(odd, F32(1.0), F32(-1.0))
    for b in range(SIDE):
        low = [pick(px, x_even[k, i, b], x_odd[k, i, b]) for i in range(3)]
        high = [pick(px, x_odd[k, i, b], x_even[k, i, b]) for i in range(3)]
        if ghost_speed is not None:
            u_low = [ghost_speed[i, b * 8 : b * 8 + 8, :] for i in range(3)]
            u_high = [ghost_speed[i, 32 + b * 8 : 40 + b * 8, :] for i in range(3)]
            low = minus(0, low, cross(u_low, low))
            high = plus(0, high, cross(u_high, high))
        for i in range(3):
            out[k, i, 0, b] = pre[k, i, 0, b] + F32(jump) * low[i]
            out[k, i, SIDE - 1, b] = pre[k, i, SIDE - 1, b] + F32(jump) * high[i]
    for a in (1, 2):
        for b in range(SIDE):
            for i in range(3):
                out[k, i, a, b] = pre[k, i, a, b]
    for half in range(2):
        low = [pick(py, y_even[k, i, half], y_odd[k, i, half]) for i in range(3)]
        high = [pick(py, y_odd[k, i, half], y_even[k, i, half]) for i in range(3)]
        for s in range(2):
            a = 2 * half + s
            if s == 0:
                both = [jnp.where(odd, roll_rows(h, 1), l) for l, h in zip(low, high)]
            else:
                both = [jnp.where(odd, h, roll_rows(l, -1)) for l, h in zip(low, high)]
            if ghost_speed is not None:
                u = [ghost_speed[i, 64 + a * 8 : 72 + a * 8, :] for i in range(3)]
                e = cross(u, both)
                both = [both[0] + turn * e[2], both[1], both[2] - turn * e[0]]
            for i in range(3):
                out[k, i, a, 0] = out[k, i, a, 0] + mask_low * both[i]
                out[k, i, a, SIDE - 1] = out[k, i, a, SIDE - 1] + mask_high * both[i]


ROWS = 9


def pack_kernel(velocity, out):
    wide = velocity.shape[1]
    pairs = velocity.shape[2] // 2
    lane = lax.broadcasted_iota(jnp.int32, (pairs, 64), 1)
    upper = lane % 16 >= 12

    def both(q, x):
        return [velocity[q, x, pl.ds(j, pairs, stride=2), :] for j in range(2)]

    def store(x, q, value):
        out[pl.ds(x * pairs * ROWS + q, pairs, stride=ROWS), :] = value

    for x in range(wide):
        for q in range(6):
            store(x, q, jnp.concatenate(both(q, x), axis=1))
        for q in range(3):
            even, odd = both(q, x)
            even_low, odd_low = both(q, (x - 1) % wide)
            even_high, odd_high = both(q, (x + 1) % wide)
            y_part = jnp.where(upper, pltpu.roll(odd, 1, 0), pltpu.roll(even, pairs - 1, 0))
            store(
                x,
                6 + q,
                jnp.concatenate(
                    [
                        y_part,
                        even_high[:, :16],
                        odd_high[:, :16],
                        odd_low[:, 48:],
                        even_low[:, 48:],
                    ],
                    axis=1,
                ),
            )


def faces_kernel(state, x_even, x_odd, y_even, y_odd):
    px, py = parities()

    def step(k, carry):
        send_faces(k, state, None, px, py, x_even, x_odd, y_even, y_odd)
        return carry

    lax.fori_loop(0, KRYLOV, step, 0)


def unpack_kernel(arrived, first, second, ghosts):
    for q in range(ROWS):
        block = arrived[pl.ds(q, LANES, stride=ROWS), :].T
        if q < 6:
            into = first if q < 3 else second
            into[q % 3, pl.ds(0, 64, stride=2), :] = block[:64]
            into[q % 3, pl.ds(1, 64, stride=2), :] = block[64:]
        else:
            i = q - 6
            ghosts[i, pl.ds(0, 16, stride=2), :] = block[112:]
            ghosts[i, pl.ds(1, 16, stride=2), :] = block[96:112]
            ghosts[i, pl.ds(32, 16, stride=2), :] = block[64:80]
            ghosts[i, pl.ds(33, 16, stride=2), :] = block[80:96]
            for a in range(SIDE):
                ghosts[i, pl.ds(64 + a * 8, 4, stride=2), :] = block[a * 16 + 12 : a * 16 + 16]
                ghosts[i, pl.ds(65 + a * 8, 4, stride=2), :] = block[a * 16 : a * 16 + 4]


def first_volume_kernel(state, speed, pre, elec):
    def base(k, a, b):
        return [state[k, i, a, b] for i in range(3)]

    def step(k, carry):
        volume(k, state, base, speed, elec, pre, STEP_SIZE)
        return carry

    lax.fori_loop(0, KRYLOV, step, 0)


def second_volume_kernel(state, start, speed, pre, elec):
    def base(k, a, b):
        return [F32(0.5) * (state[k, i, a, b] + start[k, i, a, b]) for i in range(3)]

    def step(k, carry):
        volume(k, state, base, speed, elec, pre, 0.5 * STEP_SIZE)
        return carry

    lax.fori_loop(0, KRYLOV, step, 0)


def finish_kernel(coef, has_ghosts, has_next, *refs):
    px, py = parities()
    pre, *arrived = refs[:5]
    refs = refs[5:]
    ghosts = speed = None
    if has_ghosts:
        ghosts, refs = refs[0], refs[1:]
    if has_next:
        speed, refs = refs[0], refs[1:]
    out, *leaving = refs

    def step(k, carry):
        receive_faces(k, pre, out, ghosts, px, py, *arrived, coef)
        if has_next:
            send_faces(k, out, speed, px, py, *leaving)
        return carry

    lax.fori_loop(0, KRYLOV, step, 0)


STATE = (KRYLOV, 3, SIDE, SIDE, 8, LANES)
X_FACE = (KRYLOV, 3, SIDE, 8, LANES)
Y_FACE = (KRYLOV, 3, SIDE // 2, 8, LANES)
SPEED = (3, 128, LANES)
GHOSTS = (3, 96, LANES)
FACES = (X_FACE, X_FACE, Y_FACE, Y_FACE)


def call(kernel, shapes, flops, *operands, scratch=()):
    whole = pl.BlockSpec(memory_space=pltpu.VMEM)
    return pl.pallas_call(
        kernel,
        out_shape=[jax.ShapeDtypeStruct(shape, F32) for shape in shapes],
        in_specs=[whole] * len(operands),
        out_specs=[whole] * len(shapes),
        scratch_shapes=[pltpu.VMEM(shape, F32) for shape in scratch],
        compiler_params=pltpu.CompilerParams(vmem_limit_bytes=VMEM_LIMIT),
        cost_estimate=pl.CostEstimate(
            flops=flops, bytes_accessed=2 * 1024 * 1024, transcendentals=0
        ),
    )(*operands)


def exchange(faces):
    received = []
    for index, face in enumerate(faces):
        axis = "gx" if index < 2 else "gy"
        count = lax.axis_size(axis)
        if index % 2 == 0:
            pairs = [(i, i ^ 1) for i in range(count)]
        else:
            pairs = [(i, ((i - 1) ^ 1) + 1) for i in range(1, count - 1)]
        received.append(lax.ppermute(face, axis, pairs))
    return received


def shards(fields, velocity):
    phases, comps, nodes, slab, wide_x, wide_y = velocity.shape
    devices = lax.axis_size("gx") * lax.axis_size("gy")
    state = fields.reshape(STATE)
    layers = jnp.transpose(velocity, (0, 1, 3, 4, 5, 2))
    layers = layers.reshape(phases * comps, wide_x, wide_y, nodes)
    (packed,) = call(pack_kernel, [(devices * ROWS, LANES)], 10**6, layers)
    packed = packed.reshape(devices, ROWS * LANES)
    moved = lax.all_to_all(packed, ("gx", "gy"), split_axis=0, concat_axis=0, tiled=True)
    moved = moved.reshape(devices * ROWS, LANES)
    arrived = exchange(call(faces_kernel, FACES, 10**6, state))
    *speeds, ghosts = call(unpack_kernel, [SPEED, SPEED, GHOSTS], 10**6, moved)
    elec = [(3, SIDE, SIDE, 8, LANES)]
    for phase in range(phases):
        speed = speeds[phase]
        (pre,) = call(first_volume_kernel, [STATE], 10**7, state, speed, scratch=elec)
        if phase == 0:
            extra = (ghosts, speed)
        else:
            extra = (speed,)

        def first_finish(*refs, has_ghosts=phase == 0):
            finish_kernel(STEP_SIZE, has_ghosts, True, *refs)

        middle, *leaving = call(first_finish, [STATE, *FACES], 10**6, pre, *arrived, *extra)
        arrived = exchange(leaving)
        (pre,) = call(second_volume_kernel, [STATE], 10**7, middle, state, speed, scratch=elec)
        has_next = phase + 1 < phases

        def second_finish(*refs, has_next=has_next):
            finish_kernel(0.5 * STEP_SIZE, False, has_next, *refs)

        extra = (speeds[phase + 1],) if has_next else ()
        shapes = [STATE, *FACES] if has_next else [STATE]
        state, *leaving = call(second_finish, shapes, 10**6, pre, *arrived, *extra)
        if has_next:
            arrived = exchange(leaving)
    return state.reshape(fields.shape)


def solution(mesh):
    return jax.shard_map(
        shards,
        mesh=mesh,
        in_specs=(
            P(None, None, None, "gx", "gy", None),
            P(None, None, None, ("gx", "gy"), None, None),
        ),
        out_specs=P(None, None, None, "gx", "gy", None),
        check_vma=False,
    )
```

time: 214 us -> 75.6 us (0.35); the launches traced: 210 us -> 74.5 us
  local copies, waits for them, and re-layouts: 49.2 us -> 1.14 us
  starting transfers between devices: 85.1 us -> 41 us
  other arithmetic: 34.3 us -> 0 us
  matrix products: 18.7 us -> 0 us
  Pallas kernels: 0 us -> 7.2 us
  waiting for transfers between devices: 20.7 us -> 25 us
    ppermute x16, starting transfers between devices: 66.3 us -> 30.3 us  [exchange(): received.append(lax.ppermute(face, axis, pairs))]
    scatter-add x15 -> x0, local copies, waits for them, and re-layouts: 25.8 us -> none  [the longest x9 13.5 us: tendency(): result = result.at[high_index].add(term_high)]
    dot_general x24 -> x0, matrix products: 18.7 us -> none  [along(): jnp.einsum(forms[direction], table, block, precision=lax.Precision.HIGHEST)]
    sub x22 -> x0, other arithmetic: 12.9 us -> none  [the longest x9 6.67 us: tendency(): jump_low = outer_low - lower]
    all_to_all x2 -> x1, starting transfers between devices: 18.9 us -> 10.7 us  [shards(): lax.all_to_all(packed, ('gx', 'gy'), split_axis=0, concat_axis=0, tiled=T...]
    slice x24 -> x0, local copies, waits for them, and re-layouts: 7.8 us -> none  [the longest x8 3.14 us: tendency(): lax.slice_in_dim(lower, 1, count, axis=elem_dim)]
    pallas_call x0 -> x11, Pallas kernels: none -> 7.2 us  [call(): pl.pallas_call(kernel, out_shape=[jax.ShapeDtypeStruct(shape, F32) for sh...]
    ppermute x16, waiting for transfers between devices: 15.6 us -> 22.5 us  [exchange(): received.append(lax.ppermute(face, axis, pairs))]
  transfers between devices with their start and end apart: 18 -> 17, of which waited for: 6 -> 7; matrix products, arithmetic and copies ran while one was open for 13% -> 0% of each run, Pallas kernels for 0% -> 6%
where the time goes in v1:
time: 75.6 us; the launch traced here: 74.5 us
  starting transfers between devices  41 us (54%)
  waiting for transfers between devices  25 us (33%)
  Pallas kernels  7.2 us (10%)
  local copies, waits for them, and re-layouts  1.14 us (2%)
    ppermute x16, starting transfers between devices, exchange(): received.append(lax.ppermute(face, axis, pairs))  30.3 us
    ppermute x16, waiting for transfers between devices, exchange(): received.append(lax.ppermute(face, axis, pairs))  22.5 us
    all_to_all x1, starting transfers between devices, shards(): lax.all_to_all(packed, ('gx', 'gy'), split_axis=0, concat_axis=0, tiled=T...  10.7 us
    pallas_call x11, Pallas kernels, call(): pl.pallas_call(kernel, out_shape=[jax.ShapeDtypeStruct(shape, F32) for sh...  7.2 us
    all_to_all x1, waiting for transfers between devices, shards(): lax.all_to_all(packed, ('gx', 'gy'), split_axis=0, concat_axis=0, tiled=T...  2.53 us
  transfers between devices with their start and end apart: 17, of which 7 were waited for; matrix products, arithmetic and copies ran while one was open for 0% of the time, Pallas kernels for 6%

profile of v1, /device:TPU:13, one launch (start us, length us, event | category | flops | bytes accessed | tf_op | source)
XLA Modules:
  0.0 74.5 jit_solution(2762410748571198257)
XLA Ops:
  0.0 1.1 %copy-done.1 = f32[2,3,64,1,16,16]{2,5,4,3,1,0:T(8,128)S(1)} copy-done((f32[2,3,64,1,16,16]{2,5,4,3,1,0:T(8,128)S(1)}, f32[2,3,64,1,16,16]{2,5,4,3,1,0:T(8,128)}, u32[]{:S(2)}) %copy-start.1) | copy-done | bytes 393240
  1.1 1.2 %shard_map.28 = f32[1152,128]{1,0:T(8,128)} custom-call(f32[6,16,16,64]{3,2,1,0:T(8,128)S(1)} %bitcast.13), custom_call_target="tpu_custom_call" | custom-call | flops 1000000 | bytes 2097152 | tf_op jit(solution)/shard_map/pallas_call | solution.py:372
  2.3 10.7 %all-to-all-start = ((f32[128,1,1152]{2,1,0:T(1,128)}), f32[128,1,1152]{2,1,0:T(1,128)S(1)}, u32[]{:S(2)}, u32[]{:S(2)}) async-start(f32[128,1,1152]{2,1,0:T(1,128)} %bitcast.3), calls=%async_computation | async-start | bytes 1179648 | tf_op jit(solution)/shard_map/all_to_all | solution.py:406
  13.1 0.4 collective-permute-start
  13.6 5.1 %collective-permute-start.1 = (f32[4,3,4,8,128]{4,3,2,1,0:T(8,128)S(1)}, f32[4,3,4,8,128]{4,3,2,1,0:T(8,128)S(1)}, u32[]{:S(2)}, u32[]{:S(2)}) collective-permute-start(f32[4,3,4,8,128]{4,3,2,1,0:T(8,128)S(1)} %get-tuple-element.29), channel_id=1, source_target_pairs={{8,16},{16,8},{24,32},{32,24},{40,48},{48,40},{56,64},{64,56},{72,... | collective-permute-start | bytes 589832 | tf_op jit(solution)/shard_map/ppermute | solution.py:394
  18.7 0.6 collective-permute-start.2
  19.3 2.7 %collective-permute-start.3 = (f32[4,3,2,8,128]{4,3,2,1,0:T(8,128)S(1)}, f32[4,3,2,8,128]{4,3,2,1,0:T(8,128)S(1)}, u32[]{:S(2)}, u32[]{:S(2)}) collective-permute-start(f32[4,3,2,8,128]{4,3,2,1,0:T(8,128)S(1)} %get-tuple-element.31), channel_id=1, source_target_pairs={{1,2},{2,1},{3,4},{4,3},{5,6},{6,5},{9,10},{10,9},{11,12},{12,11},... | collective-permute-start | bytes 294920 | tf_op jit(solution)/shard_map/ppermute | solution.py:394
  22.1 2.5 %all-to-all-done = f32[128,1,1152]{2,1,0:T(1,128)S(1)} async-done(((f32[128,1,1152]{2,1,0:T(1,128)}), f32[128,1,1152]{2,1,0:T(1,128)S(1)}, u32[]{:S(2)}, u32[]{:S(2)}) %all-to-all-start) | async-done | bytes 589856 | tf_op jit(solution)/shard_map/all_to_all | solution.py:406
  24.6 0.2 shard_map.29
  24.8 1.0 %shard_map.30.refs_0_ = f32[4,3,4,4,8,128]{5,4,3,2,1,0:T(8,128)S(1)} custom-call(f32[4,3,4,4,8,128]{5,4,3,2,1,0:T(8,128)S(1)} %bitcast.10, f32[3,128,128]{2,1,0:T(8,128)S(1)} %get-tuple-element.27.speed.refs_6_), custom_call_target="tpu_custom_call" | custom-call | flops 10000000 | bytes 2097152 | tf_op jit(solution)/shard_map/pallas_call | solution.py:372
  25.8 4.3 %collective-permute-done.2.refs_3_ = f32[4,3,2,8,128]{4,3,2,1,0:T(8,128)S(1)} collective-permute-done((f32[4,3,2,8,128]{4,3,2,1,0:T(8,128)S(1)}, f32[4,3,2,8,128]{4,3,2,1,0:T(8,128)S(1)}, u32[]{:S(2)}, u32[]{:S(2)}) %collective-permute-start.2) | collective-permute-done | bytes 98336 | tf_op jit(solution)/shard_map/ppermute | solution.py:394
  30.1 0.7 collective-permute-done.1.refs_2_
  30.8 0.3 shard_map.32
  31.2 4.7 %collective-permute-start.5 = (f32[4,3,4,8,128]{4,3,2,1,0:T(8,128)S(1)}, f32[4,3,4,8,128]{4,3,2,1,0:T(8,128)S(1)}, u32[]{:S(2)}, u32[]{:S(2)}) collective-permute-start(f32[4,3,4,8,128]{4,3,2,1,0:T(8,128)S(1)} %get-tuple-element.35), channel_id=1, source_target_pairs={{8,16},{16,8},{24,32},{32,24},{40,48},{48,40},{56,64},{64,56},{72,... | collective-permute-start | bytes 589832 | tf_op jit(solution)/shard_map/ppermute | solution.py:394
  35.9 0.1 collective-permute-start.6
  36.0 2.3 %collective-permute-start.7 = (f32[4,3,2,8,128]{4,3,2,1,0:T(8,128)S(1)}, f32[4,3,2,8,128]{4,3,2,1,0:T(8,128)S(1)}, u32[]{:S(2)}, u32[]{:S(2)}) collective-permute-start(f32[4,3,2,8,128]{4,3,2,1,0:T(8,128)S(1)} %get-tuple-element.37), channel_id=1, source_target_pairs={{1,2},{2,1},{3,4},{4,3},{5,6},{6,5},{9,10},{10,9},{11,12},{12,11},... | collective-permute-start | bytes 294920 | tf_op jit(solution)/shard_map/ppermute | solution.py:394
  38.4 1.0 %shard_map.33.refs_0_ = f32[4,3,4,4,8,128]{5,4,3,2,1,0:T(8,128)S(1)} custom-call(f32[4,3,4,4,8,128]{5,4,3,2,1,0:T(8,128)S(1)} %get-tuple-element.33.state, f32[4,3,4,4,8,128]{5,4,3,2,1,0:T(8,128)S(1)} %bitcast.11, f32[3,128,128]{2,1,0:T(8,128)S(1)} %get-tuple-element.27.speed.refs_6_), custom_call_target="tpu_custom_call" | custom-call | flops 10000000 | bytes 2097152 | tf_op jit(solution)/shard_map/pallas_call | solution.py:372
  39.4 5.6 %collective-permute-done.6.refs_3_ = f32[4,3,2,8,128]{4,3,2,1,0:T(8,128)S(1)} collective-permute-done((f32[4,3,2,8,128]{4,3,2,1,0:T(8,128)S(1)}, f32[4,3,2,8,128]{4,3,2,1,0:T(8,128)S(1)}, u32[]{:S(2)}, u32[]{:S(2)}) %collective-permute-start.6) | collective-permute-done | bytes 98336 | tf_op jit(solution)/shard_map/ppermute | solution.py:394
  45.0 0.2 shard_map.34
  45.2 0.4 collective-permute-start.8
  45.6 4.4 %collective-permute-start.9 = (f32[4,3,4,8,128]{4,3,2,1,0:T(8,128)S(1)}, f32[4,3,4,8,128]{4,3,2,1,0:T(8,128)S(1)}, u32[]{:S(2)}, u32[]{:S(2)}) collective-permute-start(f32[4,3,4,8,128]{4,3,2,1,0:T(8,128)S(1)} %get-tuple-element.41), channel_id=1, source_target_pairs={{8,16},{16,8},{24,32},{32,24},{40,48},{48,40},{56,64},{64,56},{72,... | collective-permute-start | bytes 589832 | tf_op jit(solution)/shard_map/ppermute | solution.py:394
  50.1 2.3 %collective-permute-start.11 = (f32[4,3,2,8,128]{4,3,2,1,0:T(8,128)S(1)}, f32[4,3,2,8,128]{4,3,2,1,0:T(8,128)S(1)}, u32[]{:S(2)}, u32[]{:S(2)}) collective-permute-start(f32[4,3,2,8,128]{4,3,2,1,0:T(8,128)S(1)} %get-tuple-element.43), channel_id=1, source_target_pairs={{1,2},{2,1},{3,4},{4,3},{5,6},{6,5},{9,10},{10,9},{11,12},{12,11},... | collective-permute-start | bytes 294920 | tf_op jit(solution)/shard_map/ppermute | solution.py:394
  52.4 1.0 %shard_map.35.refs_0_ = f32[4,3,4,4,8,128]{5,4,3,2,1,0:T(8,128)S(1)} custom-call(f32[4,3,4,4,8,128]{5,4,3,2,1,0:T(8,128)S(1)} %get-tuple-element.39.state.start, f32[3,128,128]{2,1,0:T(8,128)S(1)} %get-tuple-element.38.refs_5_.speed), custom_call_target="tpu_custom_call" | custom-call | flops 10000000 | bytes 2097152 | tf_op jit(solution)/shard_map/pallas_call | solution.py:372
  53.4 5.6 %collective-permute-done.10.refs_3_ = f32[4,3,2,8,128]{4,3,2,1,0:T(8,128)S(1)} collective-permute-done((f32[4,3,2,8,128]{4,3,2,1,0:T(8,128)S(1)}, f32[4,3,2,8,128]{4,3,2,1,0:T(8,128)S(1)}, u32[]{:S(2)}, u32[]{:S(2)}) %collective-permute-start.10) | collective-permute-done | bytes 98336 | tf_op jit(solution)/shard_map/ppermute | solution.py:394
  59.1 0.3 collective-permute-done.9.refs_2_
  59.4 0.2 shard_map.36
  59.6 0.1 collective-permute-start.12
  59.7 4.8 %collective-permute-start.13 = (f32[4,3,4,8,128]{4,3,2,1,0:T(8,128)S(1)}, f32[4,3,4,8,128]{4,3,2,1,0:T(8,128)S(1)}, u32[]{:S(2)}, u32[]{:S(2)}) collective-permute-start(f32[4,3,4,8,128]{4,3,2,1,0:T(8,128)S(1)} %get-tuple-element.46), channel_id=1, source_target_pairs={{8,16},{16,8},{24,32},{32,24},{40,48},{48,40},{56,64},{64,56},{72,... | collective-permute-start | bytes 589832 | tf_op jit(solution)/shard_map/ppermute | solution.py:394
  64.6 1.9 %collective-permute-start.15 = (f32[4,3,2,8,128]{4,3,2,1,0:T(8,128)S(1)}, f32[4,3,2,8,128]{4,3,2,1,0:T(8,128)S(1)}, u32[]{:S(2)}, u32[]{:S(2)}) collective-permute-start(f32[4,3,2,8,128]{4,3,2,1,0:T(8,128)S(1)} %get-tuple-element.48), channel_id=1, source_target_pairs={{1,2},{2,1},{3,4},{4,3},{5,6},{6,5},{9,10},{10,9},{11,12},{12,11},... | collective-permute-start | bytes 294920 | tf_op jit(solution)/shard_map/ppermute | solution.py:394
  66.5 1.0 %shard_map.37.refs_0_ = f32[4,3,4,4,8,128]{5,4,3,2,1,0:T(8,128)S(1)} custom-call(f32[4,3,4,4,8,128]{5,4,3,2,1,0:T(8,128)S(1)} %get-tuple-element.44.state, f32[4,3,4,4,8,128]{5,4,3,2,1,0:T(8,128)S(1)} %get-tuple-element.39.state.start, f32[3,128,128]{2,1,0:T(8,128)S(1)} %get-tuple-element.38.refs_5_.speed), custom_call_target="tpu_custom_call" | custom-call | flops 10000000 | bytes 2097152 | tf_op jit(solution)/shard_map/pallas_call | solution.py:372
  67.6 5.9 %collective-permute-done.14.refs_3_ = f32[4,3,2,8,128]{4,3,2,1,0:T(8,128)S(1)} collective-permute-done((f32[4,3,2,8,128]{4,3,2,1,0:T(8,128)S(1)}, f32[4,3,2,8,128]{4,3,2,1,0:T(8,128)S(1)}, u32[]{:S(2)}, u32[]{:S(2)}) %collective-permute-start.14) | collective-permute-done | bytes 98336 | tf_op jit(solution)/shard_map/ppermute | solution.py:394
  73.5 1.0 %shard_map.38 = f32[4,3,4,4,8,128]{5,4,3,2,1,0:T(8,128)} custom-call(f32[4,3,4,4,8,128]{5,4,3,2,1,0:T(8,128)S(1)} %shard_map.37.refs_0_, f32[4,3,4,8,128]{4,3,2,1,0:T(8,128)S(1)} %collective-permute-done.12.refs_1_, f32[4,3,4,8,128]{4,3,2,1,0:T(8,128)S(1)} %collective-permute-done.13.refs_2_, f32[4,3,2,8,128]{4,3,2,1,0:T(8,128)S(1)} %collective-permute-done.14.refs_3_, ...), custom_call_target="tpu_custom_call" | custom-call | flops 1000000 | bytes 2097152 | tf_op jit(solution)/shard_map/pallas_call | solution.py:372
  (17 shorter events, 0.4 us)
Async XLA Ops:
  0.0 1.1 %copy-start.1 = (f32[2,3,64,1,16,16]{2,5,4,3,1,0:T(8,128)S(1)}, f32[2,3,64,1,16,16]{2,5,4,3,1,0:T(8,128)}, u32[]{:S(2)}) copy-start(f32[2,3,64,1,16,16]{2,5,4,3,1,0:T(8,128)} %param.3) | copy-start | bytes 1179652
  2.3 10.7 %copy-start = (f32[4,3,64,1,2,128]{5,4,3,2,1,0:T(2,128)S(1)}, f32[4,3,64,1,2,128]{5,4,3,2,1,0:T(2,128)}, u32[]{:S(2)}) copy-start(f32[4,3,64,1,2,128]{5,4,3,2,1,0:T(2,128)} %param.2) | copy-start | bytes 2359300
  2.3 22.3 %all-to-all-start = ((f32[128,1,1152]{2,1,0:T(1,128)}), f32[128,1,1152]{2,1,0:T(1,128)S(1)}, u32[]{:S(2)}, u32[]{:S(2)}) async-start(f32[128,1,1152]{2,1,0:T(1,128)} %bitcast.3), calls=%async_computation | async-start | bytes 1179648 | tf_op jit(solution)/shard_map/all_to_all | solution.py:406
  13.1 17.0 %collective-permute-start = (f32[4,3,4,8,128]{4,3,2,1,0:T(8,128)S(1)}, f32[4,3,4,8,128]{4,3,2,1,0:T(8,128)S(1)}, u32[]{:S(2)}, u32[]{:S(2)}) collective-permute-start(f32[4,3,4,8,128]{4,3,2,1,0:T(8,128)S(1)} %get-tuple-element.28), channel_id=1, source_target_pairs={{0,8},{8,0},{16,24},{24,16},{32,40},{40,32},{48,56},{56,48},{64,72... | collective-permute-start | bytes 589832 | tf_op jit(solution)/shard_map/ppermute | solution.py:394
  13.6 17.2 %collective-permute-start.1 = (f32[4,3,4,8,128]{4,3,2,1,0:T(8,128)S(1)}, f32[4,3,4,8,128]{4,3,2,1,0:T(8,128)S(1)}, u32[]{:S(2)}, u32[]{:S(2)}) collective-permute-start(f32[4,3,4,8,128]{4,3,2,1,0:T(8,128)S(1)} %get-tuple-element.29), channel_id=1, source_target_pairs={{8,16},{16,8},{24,32},{32,24},{40,48},{48,40},{56,64},{64,56},{72,... | collective-permute-start | bytes 589832 | tf_op jit(solution)/shard_map/ppermute | solution.py:394
  18.7 11.4 %collective-permute-start.2 = (f32[4,3,2,8,128]{4,3,2,1,0:T(8,128)S(1)}, f32[4,3,2,8,128]{4,3,2,1,0:T(8,128)S(1)}, u32[]{:S(2)}, u32[]{:S(2)}) collective-permute-start(f32[4,3,2,8,128]{4,3,2,1,0:T(8,128)S(1)} %get-tuple-element.30), channel_id=1, source_target_pairs={{0,1},{1,0},{2,3},{3,2},{4,5},{5,4},{6,7},{7,6},{8,9},{9,8},{10,11... | collective-permute-start | bytes 294920 | tf_op jit(solution)/shard_map/ppermute | solution.py:394
  19.3 10.8 %collective-permute-start.3 = (f32[4,3,2,8,128]{4,3,2,1,0:T(8,128)S(1)}, f32[4,3,2,8,128]{4,3,2,1,0:T(8,128)S(1)}, u32[]{:S(2)}, u32[]{:S(2)}) collective-permute-start(f32[4,3,2,8,128]{4,3,2,1,0:T(8,128)S(1)} %get-tuple-element.31), channel_id=1, source_target_pairs={{1,2},{2,1},{3,4},{4,3},{5,6},{6,5},{9,10},{10,9},{11,12},{12,11},... | collective-permute-start | bytes 294920 | tf_op jit(solution)/shard_map/ppermute | solution.py:394
  31.1 13.9 %collective-permute-start.4 = (f32[4,3,4,8,128]{4,3,2,1,0:T(8,128)S(1)}, f32[4,3,4,8,128]{4,3,2,1,0:T(8,128)S(1)}, u32[]{:S(2)}, u32[]{:S(2)}) collective-permute-start(f32[4,3,4,8,128]{4,3,2,1,0:T(8,128)S(1)} %get-tuple-element.34), channel_id=1, source_target_pairs={{0,8},{8,0},{16,24},{24,16},{32,40},{40,32},{48,56},{56,48},{64,72... | collective-permute-start | bytes 589832 | tf_op jit(solution)/shard_map/ppermute | solution.py:394
  31.2 13.8 %collective-permute-start.5 = (f32[4,3,4,8,128]{4,3,2,1,0:T(8,128)S(1)}, f32[4,3,4,8,128]{4,3,2,1,0:T(8,128)S(1)}, u32[]{:S(2)}, u32[]{:S(2)}) collective-permute-start(f32[4,3,4,8,128]{4,3,2,1,0:T(8,128)S(1)} %get-tuple-element.35), channel_id=1, source_target_pairs={{8,16},{16,8},{24,32},{32,24},{40,48},{48,40},{56,64},{64,56},{72,... | collective-permute-start | bytes 589832 | tf_op jit(solution)/shard_map/ppermute | solution.py:394
  35.9 9.1 %collective-permute-start.6 = (f32[4,3,2,8,128]{4,3,2,1,0:T(8,128)S(1)}, f32[4,3,2,8,128]{4,3,2,1,0:T(8,128)S(1)}, u32[]{:S(2)}, u32[]{:S(2)}) collective-permute-start(f32[4,3,2,8,128]{4,3,2,1,0:T(8,128)S(1)} %get-tuple-element.36), channel_id=1, source_target_pairs={{0,1},{1,0},{2,3},{3,2},{4,5},{5,4},{6,7},{7,6},{8,9},{9,8},{10,11... | collective-permute-start | bytes 294920 | tf_op jit(solution)/shard_map/ppermute | solution.py:394
  36.0 9.0 %collective-permute-start.7 = (f32[4,3,2,8,128]{4,3,2,1,0:T(8,128)S(1)}, f32[4,3,2,8,128]{4,3,2,1,0:T(8,128)S(1)}, u32[]{:S(2)}, u32[]{:S(2)}) collective-permute-start(f32[4,3,2,8,128]{4,3,2,1,0:T(8,128)S(1)} %get-tuple-element.37), channel_id=1, source_target_pairs={{1,2},{2,1},{3,4},{4,3},{5,6},{6,5},{9,10},{10,9},{11,12},{12,11},... | collective-permute-start | bytes 294920 | tf_op jit(solution)/shard_map/ppermute | solution.py:394
  45.2 13.8 %collective-permute-start.8 = (f32[4,3,4,8,128]{4,3,2,1,0:T(8,128)S(1)}, f32[4,3,4,8,128]{4,3,2,1,0:T(8,128)S(1)}, u32[]{:S(2)}, u32[]{:S(2)}) collective-permute-start(f32[4,3,4,8,128]{4,3,2,1,0:T(8,128)S(1)} %get-tuple-element.40), channel_id=1, source_target_pairs={{0,8},{8,0},{16,24},{24,16},{32,40},{40,32},{48,56},{56,48},{64,72... | collective-permute-start | bytes 589832 | tf_op jit(solution)/shard_map/ppermute | solution.py:394
  45.6 13.7 %collective-permute-start.9 = (f32[4,3,4,8,128]{4,3,2,1,0:T(8,128)S(1)}, f32[4,3,4,8,128]{4,3,2,1,0:T(8,128)S(1)}, u32[]{:S(2)}, u32[]{:S(2)}) collective-permute-start(f32[4,3,4,8,128]{4,3,2,1,0:T(8,128)S(1)} %get-tuple-element.41), channel_id=1, source_target_pairs={{8,16},{16,8},{24,32},{32,24},{40,48},{48,40},{56,64},{64,56},{72,... | collective-permute-start | bytes 589832 | tf_op jit(solution)/shard_map/ppermute | solution.py:394
  50.0 9.1 %collective-permute-start.10 = (f32[4,3,2,8,128]{4,3,2,1,0:T(8,128)S(1)}, f32[4,3,2,8,128]{4,3,2,1,0:T(8,128)S(1)}, u32[]{:S(2)}, u32[]{:S(2)}) collective-permute-start(f32[4,3,2,8,128]{4,3,2,1,0:T(8,128)S(1)} %get-tuple-element.42), channel_id=1, source_target_pairs={{0,1},{1,0},{2,3},{3,2},{4,5},{5,4},{6,7},{7,6},{8,9},{9,8},{10,11... | collective-permute-start | bytes 294920 | tf_op jit(solution)/shard_map/ppermute | solution.py:394
  50.1 9.0 %collective-permute-start.11 = (f32[4,3,2,8,128]{4,3,2,1,0:T(8,128)S(1)}, f32[4,3,2,8,128]{4,3,2,1,0:T(8,128)S(1)}, u32[]{:S(2)}, u32[]{:S(2)}) collective-permute-start(f32[4,3,2,8,128]{4,3,2,1,0:T(8,128)S(1)} %get-tuple-element.43), channel_id=1, source_target_pairs={{1,2},{2,1},{3,4},{4,3},{5,6},{6,5},{9,10},{10,9},{11,12},{12,11},... | collective-permute-start | bytes 294920 | tf_op jit(solution)/shard_map/ppermute | solution.py:394
  59.6 13.9 %collective-permute-start.12 = (f32[4,3,4,8,128]{4,3,2,1,0:T(8,128)S(1)}, f32[4,3,4,8,128]{4,3,2,1,0:T(8,128)S(1)}, u32[]{:S(2)}, u32[]{:S(2)}) collective-permute-start(f32[4,3,4,8,128]{4,3,2,1,0:T(8,128)S(1)} %get-tuple-element.45), channel_id=1, source_target_pairs={{0,8},{8,0},{16,24},{24,16},{32,40},{40,32},{48,56},{56,48},{64,72... | collective-permute-start | bytes 589832 | tf_op jit(solution)/shard_map/ppermute | solution.py:394
  59.7 13.8 %collective-permute-start.13 = (f32[4,3,4,8,128]{4,3,2,1,0:T(8,128)S(1)}, f32[4,3,4,8,128]{4,3,2,1,0:T(8,128)S(1)}, u32[]{:S(2)}, u32[]{:S(2)}) collective-permute-start(f32[4,3,4,8,128]{4,3,2,1,0:T(8,128)S(1)} %get-tuple-element.46), channel_id=1, source_target_pairs={{8,16},{16,8},{24,32},{32,24},{40,48},{48,40},{56,64},{64,56},{72,... | collective-permute-start | bytes 589832 | tf_op jit(solution)/shard_map/ppermute | solution.py:394
  64.5 8.9 %collective-permute-start.14 = (f32[4,3,2,8,128]{4,3,2,1,0:T(8,128)S(1)}, f32[4,3,2,8,128]{4,3,2,1,0:T(8,128)S(1)}, u32[]{:S(2)}, u32[]{:S(2)}) collective-permute-start(f32[4,3,2,8,128]{4,3,2,1,0:T(8,128)S(1)} %get-tuple-element.47), channel_id=1, source_target_pairs={{0,1},{1,0},{2,3},{3,2},{4,5},{5,4},{6,7},{7,6},{8,9},{9,8},{10,11... | collective-permute-start | bytes 294920 | tf_op jit(solution)/shard_map/ppermute | solution.py:394
  64.6 8.9 %collective-permute-start.15 = (f32[4,3,2,8,128]{4,3,2,1,0:T(8,128)S(1)}, f32[4,3,2,8,128]{4,3,2,1,0:T(8,128)S(1)}, u32[]{:S(2)}, u32[]{:S(2)}) collective-permute-start(f32[4,3,2,8,128]{4,3,2,1,0:T(8,128)S(1)} %get-tuple-element.48), channel_id=1, source_target_pairs={{1,2},{2,1},{3,4},{4,3},{5,6},{6,5},{9,10},{10,9},{11,12},{12,11},... | collective-permute-start | bytes 294920 | tf_op jit(solution)/shard_map/ppermute | solution.py:394

commit v2 on v1

--- a/solution.py
+++ b/solution.py
@@ -186,7 +186,7 @@
     return jnp.where(odd, roll_rows(second, 1), first)
 
 
-def send_faces(k, state, speed, px, py, x_even, x_odd, y_even, y_odd):
+def send_faces(k, state, speed, px, py, y_even, x_odd, y_odd, x_even):
     def traces(direction, sign, a, b):
         m = [state[k, i, a, b] for i in range(3)]
         if speed is None:
@@ -210,7 +210,7 @@
             y_odd[k, i, half] = pick(py, up, down)
 
 
-def receive_faces(k, pre, out, ghost_speed, px, py, x_even, x_odd, y_even, y_odd, coef):
+def receive_faces(k, pre, out, ghost_speed, px, py, y_even, x_odd, y_odd, x_even, coef):
     jump = FLUX_COEF * coef
     odd = rows() % 2 == 1
     zero = jnp.zeros((8, LANES), F32)
@@ -289,11 +289,11 @@
             )
 
 
-def faces_kernel(state, x_even, x_odd, y_even, y_odd):
+def faces_kernel(state, y_even, x_odd, y_odd, x_even):
     px, py = parities()
 
     def step(k, carry):
-        send_faces(k, state, None, px, py, x_even, x_odd, y_even, y_odd)
+        send_faces(k, state, None, px, py, y_even, x_odd, y_odd, x_even)
         return carry
 
     lax.fori_loop(0, KRYLOV, step, 0)
@@ -364,7 +364,8 @@
 Y_FACE = (KRYLOV, 3, SIDE // 2, 8, LANES)
 SPEED = (3, 128, LANES)
 GHOSTS = (3, 96, LANES)
-FACES = (X_FACE, X_FACE, Y_FACE, Y_FACE)
+FACES = (Y_FACE, X_FACE, Y_FACE, X_FACE)
+ORDER = ('y_even', 'x_odd', 'y_odd', 'x_even')
 
 
 def call(kernel, shapes, flops, *operands, scratch=()):
@@ -382,16 +383,43 @@
     )(*operands)
 
 
-def exchange(faces):
+WAITS = (("y_even", 2 * 10**9), ("x_odd", 10**10))
+
+
+def exchange(faces, waits=WAITS):
     received = []
     for index, face in enumerate(faces):
-        axis = "gx" if index < 2 else "gy"
+        axis = "gx" if ORDER[index][0] == "x" else "gy"
         count = lax.axis_size(axis)
-        if index % 2 == 0:
+        if ORDER[index][2:] == "even":
             pairs = [(i, i ^ 1) for i in range(count)]
         else:
             pairs = [(i, ((i - 1) ^ 1) + 1) for i in range(1, count - 1)]
         received.append(lax.ppermute(face, axis, pairs))
+    return in_order(received, waits)
+
+
+def pass_kernel(arrived, *refs):
+    refs[-1][...] = arrived[...]
+
+
+def in_order(received, waits):
+    whole = pl.BlockSpec(memory_space=pltpu.VMEM)
+    before = ()
+    for name, flops in waits:
+        index = ORDER.index(name)
+        array = received[index]
+        received[index] = pl.pallas_call(
+            pass_kernel,
+            out_shape=jax.ShapeDtypeStruct(array.shape, F32),
+            in_specs=[whole] + [pl.BlockSpec(memory_space=pl.ANY)] * len(before),
+            out_specs=whole,
+            compiler_params=pltpu.CompilerParams(vmem_limit_bytes=VMEM_LIMIT),
+            cost_estimate=pl.CostEstimate(
+                flops=flops, bytes_accessed=flops // 100, transcendentals=0
+            ),
+        )(array, *before)
+        before = (received[index],)
     return received
 
 
@@ -405,7 +433,7 @@
     packed = packed.reshape(devices, ROWS * LANES)
     moved = lax.all_to_all(packed, ("gx", "gy"), split_axis=0, concat_axis=0, tiled=True)
     moved = moved.reshape(devices * ROWS, LANES)
-    arrived = exchange(call(faces_kernel, FACES, 10**6, state))
+    arrived = exchange(call(faces_kernel, FACES, 10**6, state), ())
     *speeds, ghosts = call(unpack_kernel, [SPEED, SPEED, GHOSTS], 10**6, moved)
     elec = [(3, SIDE, SIDE, 8, LANES)]
     for phase in range(phases):

time: 75.6 us -> 70.9 us (0.938)
  the two profiles are of different devices: /device:TPU:13 before, /device:TPU:3 now
where the time goes in v2:
time: 70.9 us; the launch traced here: 70.5 us
  starting transfers between devices  36.7 us (52%)
  waiting for transfers between devices  25.1 us (35%)
  Pallas kernels  7.29 us (10%)
  local copies, waits for them, and re-layouts  1.14 us (2%)
    ppermute x16, starting transfers between devices, exchange(): received.append(lax.ppermute(face, axis, pairs))  25.9 us
    ppermute x16, waiting for transfers between devices, exchange(): received.append(lax.ppermute(face, axis, pairs))  17.3 us
    all_to_all x1, starting transfers between devices, shards(): lax.all_to_all(packed, ('gx', 'gy'), split_axis=0, concat_axis=0, tiled=T...  10.8 us
    all_to_all x1, waiting for transfers between devices, shards(): lax.all_to_all(packed, ('gx', 'gy'), split_axis=0, concat_axis=0, tiled=T...  7.75 us
    pallas_call x11, Pallas kernels, call(): pl.pallas_call(kernel, out_shape=[jax.ShapeDtypeStruct(shape, F32) for sh...  7.22 us
  transfers between devices with their start and end apart: 17, of which 6 were waited for; matrix products, arithmetic and copies ran while one was open for 0% of the time, Pallas kernels for 6%

profile of v2, /device:TPU:3, one launch (start us, length us, event | category | flops | bytes accessed | tf_op | source)
XLA Modules:
  0.0 70.5 jit_solution(2265741884933887699)
XLA Ops:
  0.0 1.1 %copy-done.1 = f32[2,3,64,1,16,16]{2,5,4,3,1,0:T(8,128)S(1)} copy-done((f32[2,3,64,1,16,16]{2,5,4,3,1,0:T(8,128)S(1)}, f32[2,3,64,1,16,16]{2,5,4,3,1,0:T(8,128)}, u32[]{:S(2)}) %copy-start.1) | copy-done | bytes 393240
  1.1 1.2 %shard_map.28 = f32[1152,128]{1,0:T(8,128)} custom-call(f32[6,16,16,64]{3,2,1,0:T(8,128)S(1)} %bitcast.13), custom_call_target="tpu_custom_call" | custom-call | flops 1000000 | bytes 2097152 | tf_op jit(solution)/shard_map/pallas_call | solution.py:373
  2.3 10.8 %all-to-all-start = ((f32[128,1,1152]{2,1,0:T(1,128)}), f32[128,1,1152]{2,1,0:T(1,128)S(1)}, u32[]{:S(2)}, u32[]{:S(2)}) async-start(f32[128,1,1152]{2,1,0:T(1,128)} %bitcast.3), calls=%async_computation | async-start | bytes 1179648 | tf_op jit(solution)/shard_map/all_to_all | solution.py:434
  13.3 5.2 %collective-permute-start.1 = (f32[4,3,4,8,128]{4,3,2,1,0:T(8,128)S(1)}, f32[4,3,4,8,128]{4,3,2,1,0:T(8,128)S(1)}, u32[]{:S(2)}, u32[]{:S(2)}) collective-permute-start(f32[4,3,4,8,128]{4,3,2,1,0:T(8,128)S(1)} %get-tuple-element.29), channel_id=1, source_target_pairs={{8,16},{16,8},{24,32},{32,24},{40,48},{48,40},{56,64},{64,56},{72,... | collective-permute-start | bytes 589832 | tf_op jit(solution)/shard_map/ppermute | solution.py:398
  18.5 0.2 collective-permute-start.3
  18.7 0.6 collective-permute-start
  19.3 0.7 collective-permute-start.2
  19.9 7.7 %all-to-all-done = f32[128,1,1152]{2,1,0:T(1,128)S(1)} async-done(((f32[128,1,1152]{2,1,0:T(1,128)}), f32[128,1,1152]{2,1,0:T(1,128)S(1)}, u32[]{:S(2)}, u32[]{:S(2)}) %all-to-all-start) | async-done | bytes 589856 | tf_op jit(solution)/shard_map/all_to_all | solution.py:434
  27.7 0.2 shard_map.29
  27.9 1.0 %shard_map.30.refs_0_ = f32[4,3,4,4,8,128]{5,4,3,2,1,0:T(8,128)S(1)} custom-call(f32[4,3,4,4,8,128]{5,4,3,2,1,0:T(8,128)S(1)} %bitcast.10, f32[3,128,128]{2,1,0:T(8,128)S(1)} %get-tuple-element.27.speed.refs_6_), custom_call_target="tpu_custom_call" | custom-call | flops 10000000 | bytes 2097152 | tf_op jit(solution)/shard_map/pallas_call | solution.py:373
  28.9 0.7 %collective-permute-done.refs_1_ = f32[4,3,2,8,128]{4,3,2,1,0:T(8,128)S(1)} collective-permute-done((f32[4,3,2,8,128]{4,3,2,1,0:T(8,128)S(1)}, f32[4,3,2,8,128]{4,3,2,1,0:T(8,128)S(1)}, u32[]{:S(2)}, u32[]{:S(2)}) %collective-permute-start) | collective-permute-done | bytes 98336 | tf_op jit(solution)/shard_map/ppermute | solution.py:398
  29.7 2.2 %collective-permute-done.1.refs_2_ = f32[4,3,4,8,128]{4,3,2,1,0:T(8,128)S(1)} collective-permute-done((f32[4,3,4,8,128]{4,3,2,1,0:T(8,128)S(1)}, f32[4,3,4,8,128]{4,3,2,1,0:T(8,128)S(1)}, u32[]{:S(2)}, u32[]{:S(2)}) %collective-permute-start.1) | collective-permute-done | bytes 196640 | tf_op jit(solution)/shard_map/ppermute | solution.py:398
  31.8 0.3 shard_map.32
  32.1 0.1 collective-permute-start.4
  32.2 5.3 %collective-permute-start.5 = (f32[4,3,4,8,128]{4,3,2,1,0:T(8,128)S(1)}, f32[4,3,4,8,128]{4,3,2,1,0:T(8,128)S(1)}, u32[]{:S(2)}, u32[]{:S(2)}) collective-permute-start(f32[4,3,4,8,128]{4,3,2,1,0:T(8,128)S(1)} %get-tuple-element.35), channel_id=1, source_target_pairs={{8,16},{16,8},{24,32},{32,24},{40,48},{48,40},{56,64},{64,56},{72,... | collective-permute-start | bytes 589832 | tf_op jit(solution)/shard_map/ppermute | solution.py:398
  37.5 0.7 collective-permute-start.6
  38.3 1.0 %shard_map.33.refs_0_ = f32[4,3,4,4,8,128]{5,4,3,2,1,0:T(8,128)S(1)} custom-call(f32[4,3,4,4,8,128]{5,4,3,2,1,0:T(8,128)S(1)} %get-tuple-element.33.state, f32[4,3,4,4,8,128]{5,4,3,2,1,0:T(8,128)S(1)} %bitcast.11, f32[3,128,128]{2,1,0:T(8,128)S(1)} %get-tuple-element.27.speed.refs_6_), custom_call_target="tpu_custom_call" | custom-call | flops 10000000 | bytes 2097152 | tf_op jit(solution)/shard_map/pallas_call | solution.py:373
  39.3 3.8 %collective-permute-done.5.arrived = f32[4,3,4,8,128]{4,3,2,1,0:T(8,128)S(1)} collective-permute-done((f32[4,3,4,8,128]{4,3,2,1,0:T(8,128)S(1)}, f32[4,3,4,8,128]{4,3,2,1,0:T(8,128)S(1)}, u32[]{:S(2)}, u32[]{:S(2)}) %collective-permute-start.5) | collective-permute-done | bytes 196640 | tf_op jit(solution)/shard_map/ppermute | solution.py:398
  43.2 0.2 shard_map.36
  43.4 0.1 collective-permute-start.8
  43.5 5.9 %collective-permute-start.9 = (f32[4,3,4,8,128]{4,3,2,1,0:T(8,128)S(1)}, f32[4,3,4,8,128]{4,3,2,1,0:T(8,128)S(1)}, u32[]{:S(2)}, u32[]{:S(2)}) collective-permute-start(f32[4,3,4,8,128]{4,3,2,1,0:T(8,128)S(1)} %get-tuple-element.41), channel_id=1, source_target_pairs={{8,16},{16,8},{24,32},{32,24},{40,48},{48,40},{56,64},{64,56},{72,... | collective-permute-start | bytes 589832 | tf_op jit(solution)/shard_map/ppermute | solution.py:398
  49.4 0.7 collective-permute-start.10
  50.1 0.1 collective-permute-start.11
  50.2 1.0 %shard_map.37.refs_0_ = f32[4,3,4,4,8,128]{5,4,3,2,1,0:T(8,128)S(1)} custom-call(f32[4,3,4,4,8,128]{5,4,3,2,1,0:T(8,128)S(1)} %get-tuple-element.39.state.start, f32[3,128,128]{2,1,0:T(8,128)S(1)} %get-tuple-element.38.refs_5_.speed), custom_call_target="tpu_custom_call" | custom-call | flops 10000000 | bytes 2097152 | tf_op jit(solution)/shard_map/pallas_call | solution.py:373
  51.2 3.9 %collective-permute-done.9.arrived = f32[4,3,4,8,128]{4,3,2,1,0:T(8,128)S(1)} collective-permute-done((f32[4,3,4,8,128]{4,3,2,1,0:T(8,128)S(1)}, f32[4,3,4,8,128]{4,3,2,1,0:T(8,128)S(1)}, u32[]{:S(2)}, u32[]{:S(2)}) %collective-permute-start.9) | collective-permute-done | bytes 196640 | tf_op jit(solution)/shard_map/ppermute | solution.py:398
  55.1 0.2 shard_map.40
  55.4 1.7 %collective-permute-start.12 = (f32[4,3,2,8,128]{4,3,2,1,0:T(8,128)S(1)}, f32[4,3,2,8,128]{4,3,2,1,0:T(8,128)S(1)}, u32[]{:S(2)}, u32[]{:S(2)}) collective-permute-start(f32[4,3,2,8,128]{4,3,2,1,0:T(8,128)S(1)} %get-tuple-element.45), channel_id=1, source_target_pairs={{0,1},{1,0},{2,3},{3,2},{4,5},{5,4},{6,7},{7,6},{8,9},{9,8},{10,11... | collective-permute-start | bytes 294920 | tf_op jit(solution)/shard_map/ppermute | solution.py:398
  57.1 3.9 %collective-permute-start.13 = (f32[4,3,4,8,128]{4,3,2,1,0:T(8,128)S(1)}, f32[4,3,4,8,128]{4,3,2,1,0:T(8,128)S(1)}, u32[]{:S(2)}, u32[]{:S(2)}) collective-permute-start(f32[4,3,4,8,128]{4,3,2,1,0:T(8,128)S(1)} %get-tuple-element.46), channel_id=1, source_target_pairs={{8,16},{16,8},{24,32},{32,24},{40,48},{48,40},{56,64},{64,56},{72,... | collective-permute-start | bytes 589832 | tf_op jit(solution)/shard_map/ppermute | solution.py:398
  61.0 0.7 collective-permute-start.14
  61.8 1.0 %shard_map.41.refs_0_ = f32[4,3,4,4,8,128]{5,4,3,2,1,0:T(8,128)S(1)} custom-call(f32[4,3,4,4,8,128]{5,4,3,2,1,0:T(8,128)S(1)} %get-tuple-element.44.state, f32[4,3,4,4,8,128]{5,4,3,2,1,0:T(8,128)S(1)} %get-tuple-element.39.state.start, f32[3,128,128]{2,1,0:T(8,128)S(1)} %get-tuple-element.38.refs_5_.speed), custom_call_target="tpu_custom_call" | custom-call | flops 10000000 | bytes 2097152 | tf_op jit(solution)/shard_map/pallas_call | solution.py:373
  62.9 6.6 %collective-permute-done.13.arrived = f32[4,3,4,8,128]{4,3,2,1,0:T(8,128)S(1)} collective-permute-done((f32[4,3,4,8,128]{4,3,2,1,0:T(8,128)S(1)}, f32[4,3,4,8,128]{4,3,2,1,0:T(8,128)S(1)}, u32[]{:S(2)}, u32[]{:S(2)}) %collective-permute-start.13) | collective-permute-done | bytes 196640 | tf_op jit(solution)/shard_map/ppermute | solution.py:398
  69.5 1.0 %shard_map.44 = f32[4,3,4,4,8,128]{5,4,3,2,1,0:T(8,128)} custom-call(f32[4,3,4,4,8,128]{5,4,3,2,1,0:T(8,128)S(1)} %shard_map.41.refs_0_, f32[4,3,2,8,128]{4,3,2,1,0:T(8,128)S(1)} %shard_map.42.refs_0_.refs_1_, f32[4,3,4,8,128]{4,3,2,1,0:T(8,128)S(1)} %shard_map.43.refs_2_, f32[4,3,2,8,128]{4,3,2,1,0:T(8,128)S(1)} %collective-permute-done.14.refs_3_, ...), custom_call_target="tpu_custom_call" | custom-call | flops 1000000 | bytes 2097152 | tf_op jit(solution)/shard_map/pallas_call | solution.py:373
  (23 shorter events, 0.3 us)
Async XLA Ops:
  0.0 1.1 %copy-start.1 = (f32[2,3,64,1,16,16]{2,5,4,3,1,0:T(8,128)S(1)}, f32[2,3,64,1,16,16]{2,5,4,3,1,0:T(8,128)}, u32[]{:S(2)}) copy-start(f32[2,3,64,1,16,16]{2,5,4,3,1,0:T(8,128)} %param.3) | copy-start | bytes 1179652
  2.3 10.9 %copy-start = (f32[4,3,64,1,2,128]{5,4,3,2,1,0:T(2,128)S(1)}, f32[4,3,64,1,2,128]{5,4,3,2,1,0:T(2,128)}, u32[]{:S(2)}) copy-start(f32[4,3,64,1,2,128]{5,4,3,2,1,0:T(2,128)} %param.2) | copy-start | bytes 2359300
  2.3 25.4 %all-to-all-start = ((f32[128,1,1152]{2,1,0:T(1,128)}), f32[128,1,1152]{2,1,0:T(1,128)S(1)}, u32[]{:S(2)}, u32[]{:S(2)}) async-start(f32[128,1,1152]{2,1,0:T(1,128)} %bitcast.3), calls=%async_computation | async-start | bytes 1179648 | tf_op jit(solution)/shard_map/all_to_all | solution.py:434
  13.3 18.6 %collective-permute-start.1 = (f32[4,3,4,8,128]{4,3,2,1,0:T(8,128)S(1)}, f32[4,3,4,8,128]{4,3,2,1,0:T(8,128)S(1)}, u32[]{:S(2)}, u32[]{:S(2)}) collective-permute-start(f32[4,3,4,8,128]{4,3,2,1,0:T(8,128)S(1)} %get-tuple-element.29), channel_id=1, source_target_pairs={{8,16},{16,8},{24,32},{32,24},{40,48},{48,40},{56,64},{64,56},{72,... | collective-permute-start | bytes 589832 | tf_op jit(solution)/shard_map/ppermute | solution.py:398
  18.5 13.3 %collective-permute-start.3 = (f32[4,3,4,8,128]{4,3,2,1,0:T(8,128)S(1)}, f32[4,3,4,8,128]{4,3,2,1,0:T(8,128)S(1)}, u32[]{:S(2)}, u32[]{:S(2)}) collective-permute-start(f32[4,3,4,8,128]{4,3,2,1,0:T(8,128)S(1)} %get-tuple-element.31), channel_id=1, source_target_pairs={{0,8},{8,0},{16,24},{24,16},{32,40},{40,32},{48,56},{56,48},{64,72... | collective-permute-start | bytes 589832 | tf_op jit(solution)/shard_map/ppermute | solution.py:398
  18.7 10.9 %collective-permute-start = (f32[4,3,2,8,128]{4,3,2,1,0:T(8,128)S(1)}, f32[4,3,2,8,128]{4,3,2,1,0:T(8,128)S(1)}, u32[]{:S(2)}, u32[]{:S(2)}) collective-permute-start(f32[4,3,2,8,128]{4,3,2,1,0:T(8,128)S(1)} %get-tuple-element.28), channel_id=1, source_target_pairs={{0,1},{1,0},{2,3},{3,2},{4,5},{5,4},{6,7},{7,6},{8,9},{9,8},{10,11... | collective-permute-start | bytes 294920 | tf_op jit(solution)/shard_map/ppermute | solution.py:398
  19.3 10.4 %collective-permute-start.2 = (f32[4,3,2,8,128]{4,3,2,1,0:T(8,128)S(1)}, f32[4,3,2,8,128]{4,3,2,1,0:T(8,128)S(1)}, u32[]{:S(2)}, u32[]{:S(2)}) collective-permute-start(f32[4,3,2,8,128]{4,3,2,1,0:T(8,128)S(1)} %get-tuple-element.30), channel_id=1, source_target_pairs={{1,2},{2,1},{3,4},{4,3},{5,6},{6,5},{9,10},{10,9},{11,12},{12,11},... | collective-permute-start | bytes 294920 | tf_op jit(solution)/shard_map/ppermute | solution.py:398
  32.1 7.2 %collective-permute-start.4 = (f32[4,3,2,8,128]{4,3,2,1,0:T(8,128)S(1)}, f32[4,3,2,8,128]{4,3,2,1,0:T(8,128)S(1)}, u32[]{:S(2)}, u32[]{:S(2)}) collective-permute-start(f32[4,3,2,8,128]{4,3,2,1,0:T(8,128)S(1)} %get-tuple-element.34), channel_id=1, source_target_pairs={{0,1},{1,0},{2,3},{3,2},{4,5},{5,4},{6,7},{7,6},{8,9},{9,8},{10,11... | collective-permute-start | bytes 294920 | tf_op jit(solution)/shard_map/ppermute | solution.py:398
  32.2 10.9 %collective-permute-start.5 = (f32[4,3,4,8,128]{4,3,2,1,0:T(8,128)S(1)}, f32[4,3,4,8,128]{4,3,2,1,0:T(8,128)S(1)}, u32[]{:S(2)}, u32[]{:S(2)}) collective-permute-start(f32[4,3,4,8,128]{4,3,2,1,0:T(8,128)S(1)} %get-tuple-element.35), channel_id=1, source_target_pairs={{8,16},{16,8},{24,32},{32,24},{40,48},{48,40},{56,64},{64,56},{72,... | collective-permute-start | bytes 589832 | tf_op jit(solution)/shard_map/ppermute | solution.py:398
  37.5 5.7 %collective-permute-start.6 = (f32[4,3,2,8,128]{4,3,2,1,0:T(8,128)S(1)}, f32[4,3,2,8,128]{4,3,2,1,0:T(8,128)S(1)}, u32[]{:S(2)}, u32[]{:S(2)}) collective-permute-start(f32[4,3,2,8,128]{4,3,2,1,0:T(8,128)S(1)} %get-tuple-element.36), channel_id=1, source_target_pairs={{1,2},{2,1},{3,4},{4,3},{5,6},{6,5},{9,10},{10,9},{11,12},{12,11},... | collective-permute-start | bytes 294920 | tf_op jit(solution)/shard_map/ppermute | solution.py:398
  38.2 5.0 %collective-permute-start.7 = (f32[4,3,4,8,128]{4,3,2,1,0:T(8,128)S(1)}, f32[4,3,4,8,128]{4,3,2,1,0:T(8,128)S(1)}, u32[]{:S(2)}, u32[]{:S(2)}) collective-permute-start(f32[4,3,4,8,128]{4,3,2,1,0:T(8,128)S(1)} %get-tuple-element.37), channel_id=1, source_target_pairs={{0,8},{8,0},{16,24},{24,16},{32,40},{40,32},{48,56},{56,48},{64,72... | collective-permute-start | bytes 589832 | tf_op jit(solution)/shard_map/ppermute | solution.py:398
  43.4 7.7 %collective-permute-start.8 = (f32[4,3,2,8,128]{4,3,2,1,0:T(8,128)S(1)}, f32[4,3,2,8,128]{4,3,2,1,0:T(8,128)S(1)}, u32[]{:S(2)}, u32[]{:S(2)}) collective-permute-start(f32[4,3,2,8,128]{4,3,2,1,0:T(8,128)S(1)} %get-tuple-element.40), channel_id=1, source_target_pairs={{0,1},{1,0},{2,3},{3,2},{4,5},{5,4},{6,7},{7,6},{8,9},{9,8},{10,11... | collective-permute-start | bytes 294920 | tf_op jit(solution)/shard_map/ppermute | solution.py:398
  43.5 11.6 %collective-permute-start.9 = (f32[4,3,4,8,128]{4,3,2,1,0:T(8,128)S(1)}, f32[4,3,4,8,128]{4,3,2,1,0:T(8,128)S(1)}, u32[]{:S(2)}, u32[]{:S(2)}) collective-permute-start(f32[4,3,4,8,128]{4,3,2,1,0:T(8,128)S(1)} %get-tuple-element.41), channel_id=1, source_target_pairs={{8,16},{16,8},{24,32},{32,24},{40,48},{48,40},{56,64},{64,56},{72,... | collective-permute-start | bytes 589832 | tf_op jit(solution)/shard_map/ppermute | solution.py:398
  49.4 5.7 %collective-permute-start.10 = (f32[4,3,2,8,128]{4,3,2,1,0:T(8,128)S(1)}, f32[4,3,2,8,128]{4,3,2,1,0:T(8,128)S(1)}, u32[]{:S(2)}, u32[]{:S(2)}) collective-permute-start(f32[4,3,2,8,128]{4,3,2,1,0:T(8,128)S(1)} %get-tuple-element.42), channel_id=1, source_target_pairs={{1,2},{2,1},{3,4},{4,3},{5,6},{6,5},{9,10},{10,9},{11,12},{12,11},... | collective-permute-start | bytes 294920 | tf_op jit(solution)/shard_map/ppermute | solution.py:398
  50.1 5.1 %collective-permute-start.11 = (f32[4,3,4,8,128]{4,3,2,1,0:T(8,128)S(1)}, f32[4,3,4,8,128]{4,3,2,1,0:T(8,128)S(1)}, u32[]{:S(2)}, u32[]{:S(2)}) collective-permute-start(f32[4,3,4,8,128]{4,3,2,1,0:T(8,128)S(1)} %get-tuple-element.43), channel_id=1, source_target_pairs={{0,8},{8,0},{16,24},{24,16},{32,40},{40,32},{48,56},{56,48},{64,72... | collective-permute-start | bytes 589832 | tf_op jit(solution)/shard_map/ppermute | solution.py:398
  55.4 7.5 %collective-permute-start.12 = (f32[4,3,2,8,128]{4,3,2,1,0:T(8,128)S(1)}, f32[4,3,2,8,128]{4,3,2,1,0:T(8,128)S(1)}, u32[]{:S(2)}, u32[]{:S(2)}) collective-permute-start(f32[4,3,2,8,128]{4,3,2,1,0:T(8,128)S(1)} %get-tuple-element.45), channel_id=1, source_target_pairs={{0,1},{1,0},{2,3},{3,2},{4,5},{5,4},{6,7},{7,6},{8,9},{9,8},{10,11... | collective-permute-start | bytes 294920 | tf_op jit(solution)/shard_map/ppermute | solution.py:398
  57.1 12.4 %collective-permute-start.13 = (f32[4,3,4,8,128]{4,3,2,1,0:T(8,128)S(1)}, f32[4,3,4,8,128]{4,3,2,1,0:T(8,128)S(1)}, u32[]{:S(2)}, u32[]{:S(2)}) collective-permute-start(f32[4,3,4,8,128]{4,3,2,1,0:T(8,128)S(1)} %get-tuple-element.46), channel_id=1, source_target_pairs={{8,16},{16,8},{24,32},{32,24},{40,48},{48,40},{56,64},{64,56},{72,... | collective-permute-start | bytes 589832 | tf_op jit(solution)/shard_map/ppermute | solution.py:398
  61.0 8.5 %collective-permute-start.14 = (f32[4,3,2,8,128]{4,3,2,1,0:T(8,128)S(1)}, f32[4,3,2,8,128]{4,3,2,1,0:T(8,128)S(1)}, u32[]{:S(2)}, u32[]{:S(2)}) collective-permute-start(f32[4,3,2,8,128]{4,3,2,1,0:T(8,128)S(1)} %get-tuple-element.47), channel_id=1, source_target_pairs={{1,2},{2,1},{3,4},{4,3},{5,6},{6,5},{9,10},{10,9},{11,12},{12,11},... | collective-permute-start | bytes 294920 | tf_op jit(solution)/shard_map/ppermute | solution.py:398
  61.7 7.8 %collective-permute-start.15 = (f32[4,3,4,8,128]{4,3,2,1,0:T(8,128)S(1)}, f32[4,3,4,8,128]{4,3,2,1,0:T(8,128)S(1)}, u32[]{:S(2)}, u32[]{:S(2)}) collective-permute-start(f32[4,3,4,8,128]{4,3,2,1,0:T(8,128)S(1)} %get-tuple-element.48), channel_id=1, source_target_pairs={{0,8},{8,0},{16,24},{24,16},{32,40},{40,32},{48,56},{56,48},{64,72... | collective-permute-start | bytes 589832 | tf_op jit(solution)/shard_map/ppermute | solution.py:398

commit v3 on v2

--- a/solution.py
+++ b/solution.py
@@ -186,7 +186,35 @@
     return jnp.where(odd, roll_rows(second, 1), first)
 
 
-def send_faces(k, state, speed, px, py, y_even, x_odd, y_odd, x_even):
+class Form:
+    def __init__(self, short):
+        self.short = short
+        self.x_count, self.y_count = (10, 5) if short else (12, 6)
+
+    def shapes(self):
+        x = (KRYLOV, self.x_count, 8, LANES)
+        y = (KRYLOV, self.y_count, 8, LANES)
+        return [y if name[0] == "y" else x for name in ORDER]
+
+    def x_slot(self, i, b):
+        if not self.short:
+            return i * SIDE + b
+        if i > 0:
+            return (i - 1) * SIDE + b
+        return {0: 8, SIDE - 1: 9}.get(b)
+
+    def y_slots(self):
+        pairs = [(i, 2 * half, 2 * half + 1) for i in range(3) for half in range(2)]
+        if self.short:
+            pairs = [p for p in pairs if p[0] != 1] + [(1, 0, SIDE - 1)]
+        return pairs
+
+
+ORDER = ("y_even", "x_odd", "y_odd", "x_even")
+FULL, SHORT = Form(False), Form(True)
+
+
+def send_faces(k, form, state, speed, px, py, y_even, x_odd, y_odd, x_even):
     def traces(direction, sign, a, b):
         m = [state[k, i, a, b] for i in range(3)]
         if speed is None:
@@ -198,19 +226,48 @@
         high = traces(0, -1, SIDE - 1, b)
         low = traces(0, 1, 0, b)
         for i in range(3):
-            x_even[k, i, b] = pick(px, low[i], high[i])
-            x_odd[k, i, b] = pick(px, high[i], low[i])
-    for half in range(2):
-        high = [traces(1, -1, 2 * half + s, SIDE - 1) for s in range(2)]
-        low = [traces(1, 1, 2 * half + s, 0) for s in range(2)]
-        for i in range(3):
-            up = pack_rows(high[0][i], high[1][i], True)
-            down = pack_rows(low[0][i], low[1][i], False)
-            y_even[k, i, half] = pick(py, down, up)
-            y_odd[k, i, half] = pick(py, up, down)
-
-
-def receive_faces(k, pre, out, ghost_speed, px, py, y_even, x_odd, y_odd, x_even, coef):
+            slot = form.x_slot(i, b)
+            if slot is not None:
+                x_even[k, slot] = pick(px, low[i], high[i])
+                x_odd[k, slot] = pick(px, high[i], low[i])
+    high = [traces(1, -1, a, SIDE - 1) for a in range(SIDE)]
+    low = [traces(1, 1, a, 0) for a in range(SIDE)]
+    for slot, (i, first, second) in enumerate(form.y_slots()):
+        up = pack_rows(high[first][i], high[second][i], True)
+        down = pack_rows(low[first][i], low[second][i], False)
+        y_even[k, slot] = pick(py, down, up)
+        y_odd[k, slot] = pick(py, up, down)
+
+
+class Arrived:
+    def __init__(self, form, faces, inner, px, py):
+        self.form, self.inner, self.px, self.py = form, inner, px, py
+        self.y_even, self.x_odd, self.y_odd, self.x_even = faces
+
+    def x(self, k, side, i, b):
+        slot = self.form.x_slot(i, b)
+        if slot is None:
+            return self.inner[0][k, side, b - 1]
+        even, odd = self.x_even[k, slot], self.x_odd[k, slot]
+        return pick(self.px, even, odd) if side == 0 else pick(self.px, odd, even)
+
+    def y(self, k, i, a):
+        odd_row = rows() % 2 == 1
+        for slot, (comp, first, second) in enumerate(self.form.y_slots()):
+            if comp == i and a in (first, second):
+                even, odd = self.y_even[k, slot], self.y_odd[k, slot]
+                low, high = pick(self.py, even, odd), pick(self.py, odd, even)
+                if a == first:
+                    return jnp.where(odd_row, roll_rows(high, 1), low)
+                return jnp.where(odd_row, high, roll_rows(low, -1))
+        return self.inner[1][k, a - 1]
+
+
+def ghost_at(ghost_speed, place):
+    return [ghost_speed[i, place * 8 : place * 8 + 8, :] for i in range(3)]
+
+
+def receive_faces(k, pre, out, ghost_speed, arrived, coef):
     jump = FLUX_COEF * coef
     odd = rows() % 2 == 1
     zero = jnp.zeros((8, LANES), F32)
@@ -218,13 +275,11 @@
     mask_high = jnp.where(odd, F32(jump), zero)
     turn = jnp.where(odd, F32(1.0), F32(-1.0))
     for b in range(SIDE):
-        low = [pick(px, x_even[k, i, b], x_odd[k, i, b]) for i in range(3)]
-        high = [pick(px, x_odd[k, i, b], x_even[k, i, b]) for i in range(3)]
+        low = [arrived.x(k, 0, i, b) for i in range(3)]
+        high = [arrived.x(k, 1, i, b) for i in range(3)]
         if ghost_speed is not None:
-            u_low = [ghost_speed[i, b * 8 : b * 8 + 8, :] for i in range(3)]
-            u_high = [ghost_speed[i, 32 + b * 8 : 40 + b * 8, :] for i in range(3)]
-            low = minus(0, low, cross(u_low, low))
-            high = plus(0, high, cross(u_high, high))
+            low = minus(0, low, cross(ghost_at(ghost_speed, b), low))
+            high = plus(0, high, cross(ghost_at(ghost_speed, SIDE + b), high))
         for i in range(3):
             out[k, i, 0, b] = pre[k, i, 0, b] + F32(jump) * low[i]
             out[k, i, SIDE - 1, b] = pre[k, i, SIDE - 1, b] + F32(jump) * high[i]
@@ -232,22 +287,67 @@
         for b in range(SIDE):
             for i in range(3):
                 out[k, i, a, b] = pre[k, i, a, b]
-    for half in range(2):
-        low = [pick(py, y_even[k, i, half], y_odd[k, i, half]) for i in range(3)]
-        high = [pick(py, y_odd[k, i, half], y_even[k, i, half]) for i in range(3)]
-        for s in range(2):
-            a = 2 * half + s
-            if s == 0:
-                both = [jnp.where(odd, roll_rows(h, 1), l) for l, h in zip(low, high)]
-            else:
-                both = [jnp.where(odd, h, roll_rows(l, -1)) for l, h in zip(low, high)]
-            if ghost_speed is not None:
-                u = [ghost_speed[i, 64 + a * 8 : 72 + a * 8, :] for i in range(3)]
-                e = cross(u, both)
-                both = [both[0] + turn * e[2], both[1], both[2] - turn * e[0]]
-            for i in range(3):
-                out[k, i, a, 0] = out[k, i, a, 0] + mask_low * both[i]
-                out[k, i, a, SIDE - 1] = out[k, i, a, SIDE - 1] + mask_high * both[i]
+    for a in range(SIDE):
+        both = [arrived.y(k, i, a) for i in range(3)]
+        if ghost_speed is not None:
+            e = cross(ghost_at(ghost_speed, 2 * SIDE + a), both)
+            both = [both[0] + turn * e[2], both[1], both[2] - turn * e[0]]
+        for i in range(3):
+            out[k, i, a, 0] = out[k, i, a, 0] + mask_low * both[i]
+            out[k, i, a, SIDE - 1] = out[k, i, a, SIDE - 1] + mask_high * both[i]
+
+
+def inside(k, state, now, before, ghost_speed, inner_x, inner_y, coef):
+    row, lane = rows(), lanes()
+    table = coef * TABLE
+    third = third_table(coef)
+    jump = FLUX_COEF * coef
+    zero = jnp.zeros((8, LANES), F32)
+    own_low = jnp.where(row < 2, F32(jump), zero)
+    own_high = jnp.where(row >= 6, F32(jump), zero)
+    in_low = jnp.where(lane > 0, own_low, zero)
+    in_high = jnp.where(lane < LANES - 1, own_high, zero)
+    odd = row % 2 == 1
+    at_x, at_y = lax.axis_index("gx"), lax.axis_index("gy")
+    last_x, last_y = lax.axis_size("gx") - 1, lax.axis_size("gy") - 1
+
+    def along_third(value):
+        total = third[0] * value
+        for shift in range(1, SIDE):
+            total = total + third[shift] * roll_rows(value, 2 * shift)
+        return total
+
+    def ends(up, down):
+        total = in_low * roll_lanes(roll_rows(up, 2), 1) - own_low * up
+        return total + in_high * roll_lanes(roll_rows(down, -2), -1) - own_high * down
+
+    def start(value, old):
+        return value if old is None else F32(0.5) * (value + old)
+
+    for side in range(2):
+        there = at_x > 0 if side == 0 else at_x < last_x
+        m = [[now.x(k, side, i, b) for i in range(3)] for b in range(SIDE)]
+        e = [cross(ghost_at(ghost_speed, side * SIDE + b), m[b]) for b in range(SIDE)]
+        for b in (1, 2):
+            own = m[b][0]
+            total = weighted(table[b], [e[q][2] for q in range(SIDE)]) - along_third(e[b][1])
+            total = total + ends(own + e[b][1], own - e[b][1])
+            total = total + F32(jump) * (state[k, 0, (SIDE - 1) * side, b] - own)
+            old = None if before is None else before.x(k, side, 0, b)
+            inner_x[k, side, b - 1] = pick(there, start(own, old) + total, zero)
+    m = [[now.y(k, i, a) for i in range(3)] for a in range(SIDE)]
+    e = [cross(ghost_at(ghost_speed, 2 * SIDE + a), m[a]) for a in range(SIDE)]
+    for a in (1, 2):
+        own = m[a][1]
+        total = along_third(e[a][0]) - weighted(table[a], [e[q][2] for q in range(SIDE)])
+        total = total + ends(own - e[a][0], own + e[a][0])
+        mine = jnp.where(odd, state[k, 1, a, SIDE - 1], state[k, 1, a, 0])
+        total = total + F32(jump) * (mine - own)
+        old = None if before is None else before.y(k, 1, a)
+        value = start(own, old) + total
+        low = pick(at_y > 0, value, zero)
+        high = pick(at_y < last_y, value, zero)
+        inner_y[k, a - 1] = jnp.where(odd, high, low)
 
 
 ROWS = 9
@@ -289,11 +389,11 @@
             )
 
 
-def faces_kernel(state, y_even, x_odd, y_odd, x_even):
+def faces_kernel(state, *faces):
     px, py = parities()
 
     def step(k, carry):
-        send_faces(k, state, None, px, py, y_even, x_odd, y_odd, x_even)
+        send_faces(k, FULL, state, None, px, py, *faces)
         return carry
 
     lax.fori_loop(0, KRYLOV, step, 0)
@@ -339,33 +439,53 @@
     lax.fori_loop(0, KRYLOV, step, 0)
 
 
-def finish_kernel(coef, has_ghosts, has_next, *refs):
+def inside_kernel(coef, forms, *refs):
     px, py = parities()
-    pre, *arrived = refs[:5]
-    refs = refs[5:]
-    ghosts = speed = None
+    state, ghost_speed, *refs, inner_x, inner_y = refs
+    stages = []
+    for form in forms:
+        faces, refs = refs[:4], refs[4:]
+        inner = None
+        if form.short:
+            inner, refs = refs[:2], refs[2:]
+        stages.append(Arrived(form, faces, inner, px, py))
+    now = stages[0]
+    before = stages[1] if len(stages) > 1 else None
+
+    def step(k, carry):
+        inside(k, state, now, before, ghost_speed, inner_x, inner_y, coef)
+        return carry
+
+    lax.fori_loop(0, KRYLOV, step, 0)
+
+
+def finish_kernel(coef, form, has_ghosts, next_form, next_speed, *refs):
+    px, py = parities()
+    pre, *refs = refs
+    faces, refs = refs[:4], refs[4:]
+    inner = ghosts = speed = None
+    if form.short:
+        inner, refs = refs[:2], refs[2:]
     if has_ghosts:
-        ghosts, refs = refs[0], refs[1:]
-    if has_next:
-        speed, refs = refs[0], refs[1:]
+        ghosts, *refs = refs
+    if next_speed:
+        speed, *refs = refs
     out, *leaving = refs
+    arrived = Arrived(form, faces, inner, px, py)
 
     def step(k, carry):
-        receive_faces(k, pre, out, ghosts, px, py, *arrived, coef)
-        if has_next:
-            send_faces(k, out, speed, px, py, *leaving)
+        receive_faces(k, pre, out, ghosts, arrived, coef)
+        if next_form is not None:
+            send_faces(k, next_form, out, speed, px, py, *leaving)
         return carry
 
     lax.fori_loop(0, KRYLOV, step, 0)
 
 
 STATE = (KRYLOV, 3, SIDE, SIDE, 8, LANES)
-X_FACE = (KRYLOV, 3, SIDE, 8, LANES)
-Y_FACE = (KRYLOV, 3, SIDE // 2, 8, LANES)
+INNER = [(KRYLOV, 2, 2, 8, LANES), (KRYLOV, 2, 8, LANES)]
 SPEED = (3, 128, LANES)
 GHOSTS = (3, 96, LANES)
-FACES = (Y_FACE, X_FACE, Y_FACE, X_FACE)
-ORDER = ('y_even', 'x_odd', 'y_odd', 'x_even')
 
 
 def call(kernel, shapes, flops, *operands, scratch=()):
@@ -383,7 +503,7 @@
     )(*operands)
 
 
-WAITS = (("y_even", 2 * 10**9), ("x_odd", 10**10))
+WAITS = (("y_even", 15 * 10**8), ("x_odd", 10**10))
 
 
 def exchange(faces, waits=WAITS):
@@ -433,33 +553,41 @@
     packed = packed.reshape(devices, ROWS * LANES)
     moved = lax.all_to_all(packed, ("gx", "gy"), split_axis=0, concat_axis=0, tiled=True)
     moved = moved.reshape(devices * ROWS, LANES)
-    arrived = exchange(call(faces_kernel, FACES, 10**6, state), ())
+    arrived = exchange(call(faces_kernel, FULL.shapes(), 10**6, state), ())
     *speeds, ghosts = call(unpack_kernel, [SPEED, SPEED, GHOSTS], 10**6, moved)
     elec = [(3, SIDE, SIDE, 8, LANES)]
-    for phase in range(phases):
-        speed = speeds[phase]
-        (pre,) = call(first_volume_kernel, [STATE], 10**7, state, speed, scratch=elec)
-        if phase == 0:
-            extra = (ghosts, speed)
-        else:
-            extra = (speed,)
-
-        def first_finish(*refs, has_ghosts=phase == 0):
-            finish_kernel(STEP_SIZE, has_ghosts, True, *refs)
-
-        middle, *leaving = call(first_finish, [STATE, *FACES], 10**6, pre, *arrived, *extra)
-        arrived = exchange(leaving)
-        (pre,) = call(second_volume_kernel, [STATE], 10**7, middle, state, speed, scratch=elec)
-        has_next = phase + 1 < phases
-
-        def second_finish(*refs, has_next=has_next):
-            finish_kernel(0.5 * STEP_SIZE, False, has_next, *refs)
-
-        extra = (speeds[phase + 1],) if has_next else ()
-        shapes = [STATE, *FACES] if has_next else [STATE]
-        state, *leaving = call(second_finish, shapes, 10**6, pre, *arrived, *extra)
-        if has_next:
-            arrived = exchange(leaving)
+
+    def finish(coef, form, ghosts, next_form, speed, pre, *arrived):
+        def kernel(*refs):
+            finish_kernel(
+                coef, form, ghosts is not None, next_form, speed is not None, *refs
+            )
+
+        extra = [array for array in (ghosts, speed) if array is not None]
+        shapes = [STATE] if next_form is None else [STATE, *next_form.shapes()]
+        return call(kernel, shapes, 10**6, pre, *arrived, *extra)
+
+    def inner(coef, forms, state, *arrived):
+        def kernel(*refs):
+            inside_kernel(coef, forms, *refs)
+
+        return call(kernel, INNER, 10**7, state, ghosts, *arrived)
+
+    whole, half = STEP_SIZE, 0.5 * STEP_SIZE
+    (pre,) = call(first_volume_kernel, [STATE], 10**7, state, speeds[0], scratch=elec)
+    middle, *leaving = finish(whole, FULL, ghosts, SHORT, None, pre, *arrived)
+    one = list(arrived)
+    two = exchange(leaving)
+    two += inner(whole, [FULL], state, *one)
+    (pre,) = call(second_volume_kernel, [STATE], 10**7, middle, state, speeds[0], scratch=elec)
+    state, *leaving = finish(half, SHORT, ghosts, SHORT, speeds[1], pre, *two)
+    three = exchange(leaving)
+    three += inner(half, [SHORT, FULL], middle, *two, *one)
+    (pre,) = call(first_volume_kernel, [STATE], 10**7, state, speeds[1], scratch=elec)
+    middle, *leaving = finish(whole, SHORT, None, FULL, speeds[1], pre, *three)
+    four = exchange(leaving)
+    (pre,) = call(second_volume_kernel, [STATE], 10**7, middle, state, speeds[1], scratch=elec)
+    (state,) = finish(half, FULL, None, None, None, pre, *four)
     return state.reshape(fields.shape)
 
 

time: 70.9 us -> 68.9 us (0.972)
  the two profiles are of different devices: /device:TPU:3 before, /device:TPU:13 now
where the time goes in v3:
time: 68.9 us; the launch traced here: 68.5 us
  starting transfers between devices  42.6 us (62%)
  waiting for transfers between devices  16.6 us (24%)
  Pallas kernels  8.01 us (12%)
  local copies, waits for them, and re-layouts  1.14 us (2%)
    ppermute x16, starting transfers between devices, exchange(): received.append(lax.ppermute(face, axis, pairs))  31.9 us
    ppermute x16, waiting for transfers between devices, exchange(): received.append(lax.ppermute(face, axis, pairs))  14 us
    all_to_all x1, starting transfers between devices, shards(): lax.all_to_all(packed, ('gx', 'gy'), split_axis=0, concat_axis=0, tiled=T...  10.7 us
    pallas_call x13, Pallas kernels, call(): pl.pallas_call(kernel, out_shape=[jax.ShapeDtypeStruct(shape, F32) for sh...  7.95 us
    all_to_all x1, waiting for transfers between devices, shards(): lax.all_to_all(packed, ('gx', 'gy'), split_axis=0, concat_axis=0, tiled=T...  2.62 us
  transfers between devices with their start and end apart: 17, of which 8 were waited for; matrix products, arithmetic and copies ran while one was open for 0% of the time, Pallas kernels for 8%

profile of v3, /device:TPU:13, one launch (start us, length us, event | category | flops | bytes accessed | tf_op | source)
XLA Modules:
  0.0 68.5 jit_solution(1589192458778389731)
XLA Ops:
  0.0 1.1 %copy-done.1 = f32[2,3,64,1,16,16]{2,5,4,3,1,0:T(8,128)S(1)} copy-done((f32[2,3,64,1,16,16]{2,5,4,3,1,0:T(8,128)S(1)}, f32[2,3,64,1,16,16]{2,5,4,3,1,0:T(8,128)}, u32[]{:S(2)}) %copy-start.1) | copy-done | bytes 393240
  1.1 1.2 %shard_map.28 = f32[1152,128]{1,0:T(8,128)} custom-call(f32[6,16,16,64]{3,2,1,0:T(8,128)S(1)} %bitcast.14), custom_call_target="tpu_custom_call" | custom-call | flops 1000000 | bytes 2097152 | tf_op jit(solution)/shard_map/pallas_call | solution.py:493
  2.3 10.7 %all-to-all-start = ((f32[128,1,1152]{2,1,0:T(1,128)}), f32[128,1,1152]{2,1,0:T(1,128)S(1)}, u32[]{:S(2)}, u32[]{:S(2)}) async-start(f32[128,1,1152]{2,1,0:T(1,128)} %bitcast.3), calls=%async_computation | async-start | bytes 1179648 | tf_op jit(solution)/shard_map/all_to_all | solution.py:554
  13.1 5.3 %collective-permute-start.1 = (f32[4,12,8,128]{3,2,1,0:T(8,128)S(1)}, f32[4,12,8,128]{3,2,1,0:T(8,128)S(1)}, u32[]{:S(2)}, u32[]{:S(2)}) collective-permute-start(f32[4,12,8,128]{3,2,1,0:T(8,128)S(1)} %get-tuple-element.33), channel_id=1, source_target_pairs={{8,16},{16,8},{24,32},{32,24},{40,48},{48,40},{56,64},{64,56},{72,... | collective-permute-start | bytes 589832 | tf_op jit(solution)/shard_map/ppermute | solution.py:518
  18.7 0.6 collective-permute-start
  19.2 2.7 %collective-permute-start.2 = (f32[4,6,8,128]{3,2,1,0:T(8,128)S(1)}, f32[4,6,8,128]{3,2,1,0:T(8,128)S(1)}, u32[]{:S(2)}, u32[]{:S(2)}) collective-permute-start(f32[4,6,8,128]{3,2,1,0:T(8,128)S(1)} %get-tuple-element.34), channel_id=1, source_target_pairs={{1,2},{2,1},{3,4},{4,3},{5,6},{6,5},{9,10},{10,9},{11,12},{12,11},... | collective-permute-start | bytes 294920 | tf_op jit(solution)/shard_map/ppermute | solution.py:518
  22.0 2.6 %all-to-all-done = f32[128,1,1152]{2,1,0:T(1,128)S(1)} async-done(((f32[128,1,1152]{2,1,0:T(1,128)}), f32[128,1,1152]{2,1,0:T(1,128)S(1)}, u32[]{:S(2)}, u32[]{:S(2)}) %all-to-all-start) | async-done | bytes 589856 | tf_op jit(solution)/shard_map/all_to_all | solution.py:554
  24.6 0.2 shard_map.29
  24.8 1.0 %shard_map.30.refs_0_ = f32[4,3,4,4,8,128]{5,4,3,2,1,0:T(8,128)S(1)} custom-call(f32[4,3,4,4,8,128]{5,4,3,2,1,0:T(8,128)S(1)} %bitcast.10, f32[3,128,128]{2,1,0:T(8,128)S(1)} %get-tuple-element.31.speed), custom_call_target="tpu_custom_call" | custom-call | flops 10000000 | bytes 2097152 | tf_op jit(solution)/shard_map/pallas_call | solution.py:493
  25.8 4.3 %collective-permute-done.refs_1_.refs_2_.refs_8_ = f32[4,6,8,128]{3,2,1,0:T(8,128)S(1)} collective-permute-done((f32[4,6,8,128]{3,2,1,0:T(8,128)S(1)}, f32[4,6,8,128]{3,2,1,0:T(8,128)S(1)}, u32[]{:S(2)}, u32[]{:S(2)}) %collective-permute-start) | collective-permute-done | bytes 98336 | tf_op jit(solution)/shard_map/ppermute | solution.py:518
  30.1 0.7 %collective-permute-done.1.refs_2_.refs_3_.refs_9_ = f32[4,12,8,128]{3,2,1,0:T(8,128)S(1)} collective-permute-done((f32[4,12,8,128]{3,2,1,0:T(8,128)S(1)}, f32[4,12,8,128]{3,2,1,0:T(8,128)S(1)}, u32[]{:S(2)}, u32[]{:S(2)}) %collective-permute-start.1) | collective-permute-done | bytes 196640 | tf_op jit(solution)/shard_map/ppermute | solution.py:518
  31.0 0.5 collective-permute-start.4
  31.5 4.9 %collective-permute-start.5 = (f32[4,10,8,128]{3,2,1,0:T(8,128)S(1)}, f32[4,10,8,128]{3,2,1,0:T(8,128)S(1)}, u32[]{:S(2)}, u32[]{:S(2)}) collective-permute-start(f32[4,10,8,128]{3,2,1,0:T(8,128)S(1)} %get-tuple-element.39), channel_id=1, source_target_pairs={{8,16},{16,8},{24,32},{32,24},{40,48},{48,40},{56,64},{64,56},{72,... | collective-permute-start | bytes 491528 | tf_op jit(solution)/shard_map/ppermute | solution.py:518
  36.4 1.9 %collective-permute-start.6 = (f32[4,5,8,128]{3,2,1,0:T(8,128)S(1)}, f32[4,5,8,128]{3,2,1,0:T(8,128)S(1)}, u32[]{:S(2)}, u32[]{:S(2)}) collective-permute-start(f32[4,5,8,128]{3,2,1,0:T(8,128)S(1)} %get-tuple-element.40), channel_id=1, source_target_pairs={{1,2},{2,1},{3,4},{4,3},{5,6},{6,5},{9,10},{10,9},{11,12},{12,11},... | collective-permute-start | bytes 245768 | tf_op jit(solution)/shard_map/ppermute | solution.py:518
  38.4 1.0 %shard_map.33.refs_0_ = f32[4,3,4,4,8,128]{5,4,3,2,1,0:T(8,128)S(1)} custom-call(f32[4,3,4,4,8,128]{5,4,3,2,1,0:T(8,128)S(1)} %get-tuple-element.37.state.refs_0_, f32[4,3,4,4,8,128]{5,4,3,2,1,0:T(8,128)S(1)} %bitcast.11, f32[3,128,128]{2,1,0:T(8,128)S(1)} %get-tuple-element.31.speed), custom_call_target="tpu_custom_call" | custom-call | flops 10000000 | bytes 2097152 | tf_op jit(solution)/shard_map/pallas_call | solution.py:493
  39.5 0.4 shard_map.36
  39.9 1.1 %collective-permute-done.5.arrived = f32[4,10,8,128]{3,2,1,0:T(8,128)S(1)} collective-permute-done((f32[4,10,8,128]{3,2,1,0:T(8,128)S(1)}, f32[4,10,8,128]{3,2,1,0:T(8,128)S(1)}, u32[]{:S(2)}, u32[]{:S(2)}) %collective-permute-start.5) | collective-permute-done | bytes 163872 | tf_op jit(solution)/shard_map/ppermute | solution.py:518
  41.0 1.5 %collective-permute-done.6.refs_3_.refs_4_ = f32[4,5,8,128]{3,2,1,0:T(8,128)S(1)} collective-permute-done((f32[4,5,8,128]{3,2,1,0:T(8,128)S(1)}, f32[4,5,8,128]{3,2,1,0:T(8,128)S(1)}, u32[]{:S(2)}, u32[]{:S(2)}) %collective-permute-start.6) | collective-permute-done | bytes 81952 | tf_op jit(solution)/shard_map/ppermute | solution.py:518
  42.5 0.3 shard_map.37
  42.8 0.7 %collective-permute-start.8 = (f32[4,5,8,128]{3,2,1,0:T(8,128)S(1)}, f32[4,5,8,128]{3,2,1,0:T(8,128)S(1)}, u32[]{:S(2)}, u32[]{:S(2)}) collective-permute-start(f32[4,5,8,128]{3,2,1,0:T(8,128)S(1)} %get-tuple-element.46), channel_id=1, source_target_pairs={{0,1},{1,0},{2,3},{3,2},{4,5},{5,4},{6,7},{7,6},{8,9},{9,8},{10,11... | collective-permute-start | bytes 245768 | tf_op jit(solution)/shard_map/ppermute | solution.py:518
  43.5 4.6 %collective-permute-start.9 = (f32[4,10,8,128]{3,2,1,0:T(8,128)S(1)}, f32[4,10,8,128]{3,2,1,0:T(8,128)S(1)}, u32[]{:S(2)}, u32[]{:S(2)}) collective-permute-start(f32[4,10,8,128]{3,2,1,0:T(8,128)S(1)} %get-tuple-element.47), channel_id=1, source_target_pairs={{8,16},{16,8},{24,32},{32,24},{40,48},{48,40},{56,64},{64,56},{72,... | collective-permute-start | bytes 491528 | tf_op jit(solution)/shard_map/ppermute | solution.py:518
  48.1 2.7 %collective-permute-start.10 = (f32[4,5,8,128]{3,2,1,0:T(8,128)S(1)}, f32[4,5,8,128]{3,2,1,0:T(8,128)S(1)}, u32[]{:S(2)}, u32[]{:S(2)}) collective-permute-start(f32[4,5,8,128]{3,2,1,0:T(8,128)S(1)} %get-tuple-element.48), channel_id=1, source_target_pairs={{1,2},{2,1},{3,4},{4,3},{5,6},{6,5},{9,10},{10,9},{11,12},{12,11},... | collective-permute-start | bytes 245768 | tf_op jit(solution)/shard_map/ppermute | solution.py:518
  50.9 1.0 %shard_map.38.refs_0_ = f32[4,3,4,4,8,128]{5,4,3,2,1,0:T(8,128)S(1)} custom-call(f32[4,3,4,4,8,128]{5,4,3,2,1,0:T(8,128)S(1)} %get-tuple-element.45.state.start, f32[3,128,128]{2,1,0:T(8,128)S(1)} %get-tuple-element.44.refs_8_.speed.refs_7_), custom_call_target="tpu_custom_call" | custom-call | flops 10000000 | bytes 2097152 | tf_op jit(solution)/shard_map/pallas_call | solution.py:493
  51.9 0.4 shard_map.41
  52.3 0.7 %collective-permute-done.9.arrived = f32[4,10,8,128]{3,2,1,0:T(8,128)S(1)} collective-permute-done((f32[4,10,8,128]{3,2,1,0:T(8,128)S(1)}, f32[4,10,8,128]{3,2,1,0:T(8,128)S(1)}, u32[]{:S(2)}, u32[]{:S(2)}) %collective-permute-start.9) | collective-permute-done | bytes 163872 | tf_op jit(solution)/shard_map/ppermute | solution.py:518
  53.1 1.1 %collective-permute-done.10.refs_3_ = f32[4,5,8,128]{3,2,1,0:T(8,128)S(1)} collective-permute-done((f32[4,5,8,128]{3,2,1,0:T(8,128)S(1)}, f32[4,5,8,128]{3,2,1,0:T(8,128)S(1)}, u32[]{:S(2)}, u32[]{:S(2)}) %collective-permute-start.10) | collective-permute-done | bytes 81952 | tf_op jit(solution)/shard_map/ppermute | solution.py:518
  54.4 1.6 %collective-permute-start.12 = (f32[4,6,8,128]{3,2,1,0:T(8,128)S(1)}, f32[4,6,8,128]{3,2,1,0:T(8,128)S(1)}, u32[]{:S(2)}, u32[]{:S(2)}) collective-permute-start(f32[4,6,8,128]{3,2,1,0:T(8,128)S(1)} %get-tuple-element.53), channel_id=1, source_target_pairs={{0,1},{1,0},{2,3},{3,2},{4,5},{5,4},{6,7},{7,6},{8,9},{9,8},{10,11... | collective-permute-start | bytes 294920 | tf_op jit(solution)/shard_map/ppermute | solution.py:518
  56.0 3.9 %collective-permute-start.13 = (f32[4,12,8,128]{3,2,1,0:T(8,128)S(1)}, f32[4,12,8,128]{3,2,1,0:T(8,128)S(1)}, u32[]{:S(2)}, u32[]{:S(2)}) collective-permute-start(f32[4,12,8,128]{3,2,1,0:T(8,128)S(1)} %get-tuple-element.54), channel_id=1, source_target_pairs={{8,16},{16,8},{24,32},{32,24},{40,48},{48,40},{56,64},{64,56},{72,... | collective-permute-start | bytes 589832 | tf_op jit(solution)/shard_map/ppermute | solution.py:518
  59.9 1.9 %collective-permute-start.14 = (f32[4,6,8,128]{3,2,1,0:T(8,128)S(1)}, f32[4,6,8,128]{3,2,1,0:T(8,128)S(1)}, u32[]{:S(2)}, u32[]{:S(2)}) collective-permute-start(f32[4,6,8,128]{3,2,1,0:T(8,128)S(1)} %get-tuple-element.55), channel_id=1, source_target_pairs={{1,2},{2,1},{3,4},{4,3},{5,6},{6,5},{9,10},{10,9},{11,12},{12,11},... | collective-permute-start | bytes 294920 | tf_op jit(solution)/shard_map/ppermute | solution.py:518
  61.9 1.0 %shard_map.43.refs_0_ = f32[4,3,4,4,8,128]{5,4,3,2,1,0:T(8,128)S(1)} custom-call(f32[4,3,4,4,8,128]{5,4,3,2,1,0:T(8,128)S(1)} %get-tuple-element.52.state, f32[4,3,4,4,8,128]{5,4,3,2,1,0:T(8,128)S(1)} %get-tuple-element.45.state.start, f32[3,128,128]{2,1,0:T(8,128)S(1)} %get-tuple-element.44.refs_8_.speed.refs_7_), custom_call_target="tpu_custom_call" | custom-call | flops 10000000 | bytes 2097152 | tf_op jit(solution)/shard_map/pallas_call | solution.py:493
  63.0 4.5 %collective-permute-done.13.arrived = f32[4,12,8,128]{3,2,1,0:T(8,128)S(1)} collective-permute-done((f32[4,12,8,128]{3,2,1,0:T(8,128)S(1)}, f32[4,12,8,128]{3,2,1,0:T(8,128)S(1)}, u32[]{:S(2)}, u32[]{:S(2)}) %collective-permute-start.13) | collective-permute-done | bytes 196640 | tf_op jit(solution)/shard_map/ppermute | solution.py:518
  67.5 1.0 %shard_map.46 = f32[4,3,4,4,8,128]{5,4,3,2,1,0:T(8,128)} custom-call(f32[4,3,4,4,8,128]{5,4,3,2,1,0:T(8,128)S(1)} %shard_map.43.refs_0_, f32[4,6,8,128]{3,2,1,0:T(8,128)S(1)} %shard_map.44.refs_0_.refs_1_, f32[4,12,8,128]{3,2,1,0:T(8,128)S(1)} %shard_map.45.refs_2_, f32[4,6,8,128]{3,2,1,0:T(8,128)S(1)} %collective-permute-done.14.refs_3_, ...), custom_call_target="tpu_custom_call" | custom-call | flops 1000000 | bytes 2097152 | tf_op jit(solution)/shard_map/pallas_call | solution.py:493
  (25 shorter events, 1.0 us)
Async XLA Ops:
  0.0 1.1 %copy-start.1 = (f32[2,3,64,1,16,16]{2,5,4,3,1,0:T(8,128)S(1)}, f32[2,3,64,1,16,16]{2,5,4,3,1,0:T(8,128)}, u32[]{:S(2)}) copy-start(f32[2,3,64,1,16,16]{2,5,4,3,1,0:T(8,128)} %param.3) | copy-start | bytes 1179652
  2.3 10.7 %copy-start = (f32[4,3,64,1,2,128]{5,4,3,2,1,0:T(2,128)S(1)}, f32[4,3,64,1,2,128]{5,4,3,2,1,0:T(2,128)}, u32[]{:S(2)}) copy-start(f32[4,3,64,1,2,128]{5,4,3,2,1,0:T(2,128)} %param.2) | copy-start | bytes 2359300
  2.3 22.3 %all-to-all-start = ((f32[128,1,1152]{2,1,0:T(1,128)}), f32[128,1,1152]{2,1,0:T(1,128)S(1)}, u32[]{:S(2)}, u32[]{:S(2)}) async-start(f32[128,1,1152]{2,1,0:T(1,128)} %bitcast.3), calls=%async_computation | async-start | bytes 1179648 | tf_op jit(solution)/shard_map/all_to_all | solution.py:554
  13.1 17.7 %collective-permute-start.1 = (f32[4,12,8,128]{3,2,1,0:T(8,128)S(1)}, f32[4,12,8,128]{3,2,1,0:T(8,128)S(1)}, u32[]{:S(2)}, u32[]{:S(2)}) collective-permute-start(f32[4,12,8,128]{3,2,1,0:T(8,128)S(1)} %get-tuple-element.33), channel_id=1, source_target_pairs={{8,16},{16,8},{24,32},{32,24},{40,48},{48,40},{56,64},{64,56},{72,... | collective-permute-start | bytes 589832 | tf_op jit(solution)/shard_map/ppermute | solution.py:518
  18.5 12.4 %collective-permute-start.3 = (f32[4,12,8,128]{3,2,1,0:T(8,128)S(1)}, f32[4,12,8,128]{3,2,1,0:T(8,128)S(1)}, u32[]{:S(2)}, u32[]{:S(2)}) collective-permute-start(f32[4,12,8,128]{3,2,1,0:T(8,128)S(1)} %get-tuple-element.35), channel_id=1, source_target_pairs={{0,8},{8,0},{16,24},{24,16},{32,40},{40,32},{48,56},{56,48},{64,72... | collective-permute-start | bytes 589832 | tf_op jit(solution)/shard_map/ppermute | solution.py:518
  18.7 11.4 %collective-permute-start = (f32[4,6,8,128]{3,2,1,0:T(8,128)S(1)}, f32[4,6,8,128]{3,2,1,0:T(8,128)S(1)}, u32[]{:S(2)}, u32[]{:S(2)}) collective-permute-start(f32[4,6,8,128]{3,2,1,0:T(8,128)S(1)} %get-tuple-element.32), channel_id=1, source_target_pairs={{0,1},{1,0},{2,3},{3,2},{4,5},{5,4},{6,7},{7,6},{8,9},{9,8},{10,11... | collective-permute-start | bytes 294920 | tf_op jit(solution)/shard_map/ppermute | solution.py:518
  19.2 10.9 %collective-permute-start.2 = (f32[4,6,8,128]{3,2,1,0:T(8,128)S(1)}, f32[4,6,8,128]{3,2,1,0:T(8,128)S(1)}, u32[]{:S(2)}, u32[]{:S(2)}) collective-permute-start(f32[4,6,8,128]{3,2,1,0:T(8,128)S(1)} %get-tuple-element.34), channel_id=1, source_target_pairs={{1,2},{2,1},{3,4},{4,3},{5,6},{6,5},{9,10},{10,9},{11,12},{12,11},... | collective-permute-start | bytes 294920 | tf_op jit(solution)/shard_map/ppermute | solution.py:518
  31.0 8.8 %collective-permute-start.4 = (f32[4,5,8,128]{3,2,1,0:T(8,128)S(1)}, f32[4,5,8,128]{3,2,1,0:T(8,128)S(1)}, u32[]{:S(2)}, u32[]{:S(2)}) collective-permute-start(f32[4,5,8,128]{3,2,1,0:T(8,128)S(1)} %get-tuple-element.38), channel_id=1, source_target_pairs={{0,1},{1,0},{2,3},{3,2},{4,5},{5,4},{6,7},{7,6},{8,9},{9,8},{10,11... | collective-permute-start | bytes 245768 | tf_op jit(solution)/shard_map/ppermute | solution.py:518
  31.5 9.5 %collective-permute-start.5 = (f32[4,10,8,128]{3,2,1,0:T(8,128)S(1)}, f32[4,10,8,128]{3,2,1,0:T(8,128)S(1)}, u32[]{:S(2)}, u32[]{:S(2)}) collective-permute-start(f32[4,10,8,128]{3,2,1,0:T(8,128)S(1)} %get-tuple-element.39), channel_id=1, source_target_pairs={{8,16},{16,8},{24,32},{32,24},{40,48},{48,40},{56,64},{64,56},{72,... | collective-permute-start | bytes 491528 | tf_op jit(solution)/shard_map/ppermute | solution.py:518
  36.4 6.1 %collective-permute-start.6 = (f32[4,5,8,128]{3,2,1,0:T(8,128)S(1)}, f32[4,5,8,128]{3,2,1,0:T(8,128)S(1)}, u32[]{:S(2)}, u32[]{:S(2)}) collective-permute-start(f32[4,5,8,128]{3,2,1,0:T(8,128)S(1)} %get-tuple-element.40), channel_id=1, source_target_pairs={{1,2},{2,1},{3,4},{4,3},{5,6},{6,5},{9,10},{10,9},{11,12},{12,11},... | collective-permute-start | bytes 245768 | tf_op jit(solution)/shard_map/ppermute | solution.py:518
  38.3 4.2 %collective-permute-start.7 = (f32[4,10,8,128]{3,2,1,0:T(8,128)S(1)}, f32[4,10,8,128]{3,2,1,0:T(8,128)S(1)}, u32[]{:S(2)}, u32[]{:S(2)}) collective-permute-start(f32[4,10,8,128]{3,2,1,0:T(8,128)S(1)} %get-tuple-element.41), channel_id=1, source_target_pairs={{0,8},{8,0},{16,24},{24,16},{32,40},{40,32},{48,56},{56,48},{64,72... | collective-permute-start | bytes 491528 | tf_op jit(solution)/shard_map/ppermute | solution.py:518
  42.8 9.5 %collective-permute-start.8 = (f32[4,5,8,128]{3,2,1,0:T(8,128)S(1)}, f32[4,5,8,128]{3,2,1,0:T(8,128)S(1)}, u32[]{:S(2)}, u32[]{:S(2)}) collective-permute-start(f32[4,5,8,128]{3,2,1,0:T(8,128)S(1)} %get-tuple-element.46), channel_id=1, source_target_pairs={{0,1},{1,0},{2,3},{3,2},{4,5},{5,4},{6,7},{7,6},{8,9},{9,8},{10,11... | collective-permute-start | bytes 245768 | tf_op jit(solution)/shard_map/ppermute | solution.py:518
  43.5 9.6 %collective-permute-start.9 = (f32[4,10,8,128]{3,2,1,0:T(8,128)S(1)}, f32[4,10,8,128]{3,2,1,0:T(8,128)S(1)}, u32[]{:S(2)}, u32[]{:S(2)}) collective-permute-start(f32[4,10,8,128]{3,2,1,0:T(8,128)S(1)} %get-tuple-element.47), channel_id=1, source_target_pairs={{8,16},{16,8},{24,32},{32,24},{40,48},{48,40},{56,64},{64,56},{72,... | collective-permute-start | bytes 491528 | tf_op jit(solution)/shard_map/ppermute | solution.py:518
  48.1 6.1 %collective-permute-start.10 = (f32[4,5,8,128]{3,2,1,0:T(8,128)S(1)}, f32[4,5,8,128]{3,2,1,0:T(8,128)S(1)}, u32[]{:S(2)}, u32[]{:S(2)}) collective-permute-start(f32[4,5,8,128]{3,2,1,0:T(8,128)S(1)} %get-tuple-element.48), channel_id=1, source_target_pairs={{1,2},{2,1},{3,4},{4,3},{5,6},{6,5},{9,10},{10,9},{11,12},{12,11},... | collective-permute-start | bytes 245768 | tf_op jit(solution)/shard_map/ppermute | solution.py:518
  50.8 3.4 %collective-permute-start.11 = (f32[4,10,8,128]{3,2,1,0:T(8,128)S(1)}, f32[4,10,8,128]{3,2,1,0:T(8,128)S(1)}, u32[]{:S(2)}, u32[]{:S(2)}) collective-permute-start(f32[4,10,8,128]{3,2,1,0:T(8,128)S(1)} %get-tuple-element.49), channel_id=1, source_target_pairs={{0,8},{8,0},{16,24},{24,16},{32,40},{40,32},{48,56},{56,48},{64,72... | collective-permute-start | bytes 491528 | tf_op jit(solution)/shard_map/ppermute | solution.py:518
  54.4 8.6 %collective-permute-start.12 = (f32[4,6,8,128]{3,2,1,0:T(8,128)S(1)}, f32[4,6,8,128]{3,2,1,0:T(8,128)S(1)}, u32[]{:S(2)}, u32[]{:S(2)}) collective-permute-start(f32[4,6,8,128]{3,2,1,0:T(8,128)S(1)} %get-tuple-element.53), channel_id=1, source_target_pairs={{0,1},{1,0},{2,3},{3,2},{4,5},{5,4},{6,7},{7,6},{8,9},{9,8},{10,11... | collective-permute-start | bytes 294920 | tf_op jit(solution)/shard_map/ppermute | solution.py:518
  56.0 11.4 %collective-permute-start.13 = (f32[4,12,8,128]{3,2,1,0:T(8,128)S(1)}, f32[4,12,8,128]{3,2,1,0:T(8,128)S(1)}, u32[]{:S(2)}, u32[]{:S(2)}) collective-permute-start(f32[4,12,8,128]{3,2,1,0:T(8,128)S(1)} %get-tuple-element.54), channel_id=1, source_target_pairs={{8,16},{16,8},{24,32},{32,24},{40,48},{48,40},{56,64},{64,56},{72,... | collective-permute-start | bytes 589832 | tf_op jit(solution)/shard_map/ppermute | solution.py:518
  59.9 7.6 %collective-permute-start.14 = (f32[4,6,8,128]{3,2,1,0:T(8,128)S(1)}, f32[4,6,8,128]{3,2,1,0:T(8,128)S(1)}, u32[]{:S(2)}, u32[]{:S(2)}) collective-permute-start(f32[4,6,8,128]{3,2,1,0:T(8,128)S(1)} %get-tuple-element.55), channel_id=1, source_target_pairs={{1,2},{2,1},{3,4},{4,3},{5,6},{6,5},{9,10},{10,9},{11,12},{12,11},... | collective-permute-start | bytes 294920 | tf_op jit(solution)/shard_map/ppermute | solution.py:518
  61.8 5.7 %collective-permute-start.15 = (f32[4,12,8,128]{3,2,1,0:T(8,128)S(1)}, f32[4,12,8,128]{3,2,1,0:T(8,128)S(1)}, u32[]{:S(2)}, u32[]{:S(2)}) collective-permute-start(f32[4,12,8,128]{3,2,1,0:T(8,128)S(1)} %get-tuple-element.56), channel_id=1, source_target_pairs={{0,8},{8,0},{16,24},{24,16},{32,40},{40,32},{48,56},{56,48},{64,72... | collective-permute-start | bytes 589832 | tf_op jit(solution)/shard_map/ppermute | solution.py:518

commit v4 on v3

--- a/solution.py
+++ b/solution.py
@@ -101,25 +101,38 @@
     return total
 
 
-def volume(k, state, base, speed, elec, out, coef):
-    row, lane = rows(), lanes()
-    table = coef * TABLE
-    third = third_table(coef)
-    jump = FLUX_COEF * coef
-    zero = jnp.zeros((8, LANES), F32)
-    own_low = jnp.where(row < 2, F32(jump), zero)
-    own_high = jnp.where(row >= 6, F32(jump), zero)
-    in_low = jnp.where(lane > 0, own_low, zero)
-    in_high = jnp.where(lane < LANES - 1, own_high, zero)
-    odd = row % 2 == 1
-    mid_low = jnp.where(odd, F32(jump), zero)
-    mid_high = jnp.where(odd, zero, F32(jump))
-
-    def along_third(value):
-        total = third[0] * value
+class Weights:
+    def __init__(self, coef):
+        row, lane = rows(), lanes()
+        self.table = coef * TABLE
+        self.third = third_table(coef)
+        self.jump = F32(FLUX_COEF * coef)
+        zero = jnp.zeros((8, LANES), F32)
+        self.low = row < 4
+        low, high = row < 2, row >= 6
+        self.own = jnp.where(low | high, self.jump, zero)
+        far = (low & (lane > 0)) | (high & (lane < LANES - 1))
+        self.other = jnp.where(far, self.jump, zero)
+        self.odd = row % 2 == 1
+        self.mid_low = jnp.where(self.odd, self.jump, zero)
+        self.mid_high = jnp.where(self.odd, zero, self.jump)
+
+    def along_third(self, value):
+        total = self.third[0] * value
         for shift in range(1, SIDE):
-            total = total + third[shift] * roll_rows(value, 2 * shift)
+            total = total + self.third[shift] * roll_rows(value, 2 * shift)
         return total
+
+    def ends(self, up, down):
+        below, above = roll_lanes(roll_rows(up, 2), 1), roll_lanes(roll_rows(down, -2), -1)
+        own = up if up is down else jnp.where(self.low, up, down)
+        return self.other * jnp.where(self.low, below, above) - self.own * own
+
+
+def volume(k, state, base, speed, elec, out, weights):
+    table, jump = weights.table, weights.jump
+    mid_low, mid_high = weights.mid_low, weights.mid_high
+    along_third = weights.along_third
 
     for a in range(SIDE):
         for b in range(SIDE):
@@ -139,22 +152,20 @@
             ]
             up, down = minus(2, m, e), plus(2, m, e)
             for i in range(3):
-                total[i] = total[i] - (own_low * up[i] + own_high * down[i])
-                total[i] = total[i] + in_low * roll_lanes(roll_rows(up[i], 2), 1)
-                total[i] = total[i] + in_high * roll_lanes(roll_rows(down[i], -2), -1)
+                total[i] = total[i] + weights.ends(up[i], down[i])
             if a == 0:
                 own = minus(0, m, e)
-                total = [t - F32(jump) * o for t, o in zip(total, own)]
+                total = [t - jump * o for t, o in zip(total, own)]
             if a == SIDE - 1:
                 own = plus(0, m, e)
-                total = [t - F32(jump) * o for t, o in zip(total, own)]
+                total = [t - jump * o for t, o in zip(total, own)]
             if b == 0:
                 own = minus(1, m, e)
                 far_b = [state[k, i, a, SIDE - 1] for i in range(3)]
                 far_e = [elec[i, a, SIDE - 1] for i in range(3)]
                 far = minus(1, far_b, far_e)
                 total = [
-                    t - F32(jump) * o + mid_low * roll_rows(f, 1)
+                    t - jump * o + mid_low * roll_rows(f, 1)
                     for t, o, f in zip(total, own, far)
                 ]
             if b == SIDE - 1:
@@ -163,7 +174,7 @@
                 far_e = [elec[i, a, 0] for i in range(3)]
                 far = plus(1, far_b, far_e)
                 total = [
-                    t - F32(jump) * o + mid_high * roll_rows(f, -1)
+                    t - jump * o + mid_high * roll_rows(f, -1)
                     for t, o, f in zip(total, own, far)
                 ]
             start = base(k, a, b)
@@ -297,29 +308,12 @@
             out[k, i, a, SIDE - 1] = out[k, i, a, SIDE - 1] + mask_high * both[i]
 
 
-def inside(k, state, now, before, ghost_speed, inner_x, inner_y, coef):
-    row, lane = rows(), lanes()
-    table = coef * TABLE
-    third = third_table(coef)
-    jump = FLUX_COEF * coef
+def inside(k, state, now, before, ghost_speed, inner_x, inner_y, weights):
+    table, jump, odd = weights.table, weights.jump, weights.odd
+    along_third, ends = weights.along_third, weights.ends
     zero = jnp.zeros((8, LANES), F32)
-    own_low = jnp.where(row < 2, F32(jump), zero)
-    own_high = jnp.where(row >= 6, F32(jump), zero)
-    in_low = jnp.where(lane > 0, own_low, zero)
-    in_high = jnp.where(lane < LANES - 1, own_high, zero)
-    odd = row % 2 == 1
     at_x, at_y = lax.axis_index("gx"), lax.axis_index("gy")
     last_x, last_y = lax.axis_size("gx") - 1, lax.axis_size("gy") - 1
-
-    def along_third(value):
-        total = third[0] * value
-        for shift in range(1, SIDE):
-            total = total + third[shift] * roll_rows(value, 2 * shift)
-        return total
-
-    def ends(up, down):
-        total = in_low * roll_lanes(roll_rows(up, 2), 1) - own_low * up
-        return total + in_high * roll_lanes(roll_rows(down, -2), -1) - own_high * down
 
     def start(value, old):
         return value if old is None else F32(0.5) * (value + old)
@@ -332,7 +326,7 @@
             own = m[b][0]
             total = weighted(table[b], [e[q][2] for q in range(SIDE)]) - along_third(e[b][1])
             total = total + ends(own + e[b][1], own - e[b][1])
-            total = total + F32(jump) * (state[k, 0, (SIDE - 1) * side, b] - own)
+            total = total + jump * (state[k, 0, (SIDE - 1) * side, b] - own)
             old = None if before is None else before.x(k, side, 0, b)
             inner_x[k, side, b - 1] = pick(there, start(own, old) + total, zero)
     m = [[now.y(k, i, a) for i in range(3)] for a in range(SIDE)]
@@ -342,7 +336,7 @@
         total = along_third(e[a][0]) - weighted(table[a], [e[q][2] for q in range(SIDE)])
         total = total + ends(own - e[a][0], own + e[a][0])
         mine = jnp.where(odd, state[k, 1, a, SIDE - 1], state[k, 1, a, 0])
-        total = total + F32(jump) * (mine - own)
+        total = total + jump * (mine - own)
         old = None if before is None else before.y(k, 1, a)
         value = start(own, old) + total
         low = pick(at_y > 0, value, zero)
@@ -418,25 +412,29 @@
 
 
 def first_volume_kernel(state, speed, pre, elec):
+    weights = Weights(STEP_SIZE)
+
     def base(k, a, b):
         return [state[k, i, a, b] for i in range(3)]
 
     def step(k, carry):
-        volume(k, state, base, speed, elec, pre, STEP_SIZE)
+        volume(k, state, base, speed, elec, pre, weights)
         return carry
 
-    lax.fori_loop(0, KRYLOV, step, 0)
+    lax.fori_loop(0, KRYLOV, step, 0, unroll=True)
 
 
 def second_volume_kernel(state, start, speed, pre, elec):
+    weights = Weights(0.5 * STEP_SIZE)
+
     def base(k, a, b):
         return [F32(0.5) * (state[k, i, a, b] + start[k, i, a, b]) for i in range(3)]
 
     def step(k, carry):
-        volume(k, state, base, speed, elec, pre, 0.5 * STEP_SIZE)
+        volume(k, state, base, speed, elec, pre, weights)
         return carry
 
-    lax.fori_loop(0, KRYLOV, step, 0)
+    lax.fori_loop(0, KRYLOV, step, 0, unroll=True)
 
 
 def inside_kernel(coef, forms, *refs):
@@ -451,9 +449,10 @@
         stages.append(Arrived(form, faces, inner, px, py))
     now = stages[0]
     before = stages[1] if len(stages) > 1 else None
+    weights = Weights(coef)
 
     def step(k, carry):
-        inside(k, state, now, before, ghost_speed, inner_x, inner_y, coef)
+        inside(k, state, now, before, ghost_speed, inner_x, inner_y, weights)
         return carry
 
     lax.fori_loop(0, KRYLOV, step, 0)
@@ -480,6 +479,21 @@
         return carry
 
     lax.fori_loop(0, KRYLOV, step, 0)
+
+
+def last_kernel(coef, pre, *refs):
+    *faces, result, out, written = refs
+    px, py = parities()
+    arrived = Arrived(FULL, faces, None, px, py)
+
+    def copy(k):
+        return pltpu.make_async_copy(out.at[k], result.at[k], written.at[k])
+
+    for k in range(KRYLOV):
+        receive_faces(k, pre, out, None, arrived, coef)
+        copy(k).start()
+    for k in range(KRYLOV):
+        copy(k).wait()
 
 
 STATE = (KRYLOV, 3, SIDE, SIDE, 8, LANES)
@@ -587,7 +601,19 @@
     middle, *leaving = finish(whole, SHORT, None, FULL, speeds[1], pre, *three)
     four = exchange(leaving)
     (pre,) = call(second_volume_kernel, [STATE], 10**7, middle, state, speeds[1], scratch=elec)
-    (state,) = finish(half, FULL, None, None, None, pre, *four)
+
+    def last(*refs):
+        last_kernel(half, *refs)
+
+    state = pl.pallas_call(
+        last,
+        out_shape=jax.ShapeDtypeStruct(STATE, F32),
+        in_specs=[pl.BlockSpec(memory_space=pltpu.VMEM)] * 5,
+        out_specs=pl.BlockSpec(memory_space=pltpu.HBM),
+        scratch_shapes=[pltpu.VMEM(STATE, F32), pltpu.SemaphoreType.DMA((KRYLOV,))],
+        compiler_params=pltpu.CompilerParams(vmem_limit_bytes=VMEM_LIMIT),
+        cost_estimate=pl.CostEstimate(flops=10**6, bytes_accessed=2 * 10**6, transcendentals=0),
+    )(pre, *four)
     return state.reshape(fields.shape)
 
 

time: 68.9 us -> 68.7 us (level)
    pallas_call x13 -> x12, Pallas kernels: 7.95 us -> 6.52 us  [call(): pl.pallas_call(kernel, out_shape=[jax.ShapeDtypeStruct(shape, F32) for sh...]
    pallas_call x0 -> x1, Pallas kernels: none -> 0.95 us  [shards(): pl.pallas_call(last, out_shape=jax.ShapeDtypeStruct(STATE, F32), in_specs...]
  transfers between devices with their start and end apart: 17 -> 17, of which waited for: 8 -> 8; matrix products, arithmetic and copies ran while one was open for 0% -> 0% of each run, Pallas kernels for 8% -> 7%
where the time goes in v4:
time: 68.7 us; the launch traced here: 68.4 us
  starting transfers between devices  42.6 us (62%)
  waiting for transfers between devices  16.9 us (25%)
  Pallas kernels  7.53 us (11%)
  local copies, waits for them, and re-layouts  1.14 us (2%)
    ppermute x16, starting transfers between devices, exchange(): received.append(lax.ppermute(face, axis, pairs))  31.9 us
    ppermute x16, waiting for transfers between devices, exchange(): received.append(lax.ppermute(face, axis, pairs))  14.3 us
    all_to_all x1, starting transfers between devices, shards(): lax.all_to_all(packed, ('gx', 'gy'), split_axis=0, concat_axis=0, tiled=T...  10.7 us
    pallas_call x12, Pallas kernels, call(): pl.pallas_call(kernel, out_shape=[jax.ShapeDtypeStruct(shape, F32) for sh...  6.52 us
    all_to_all x1, waiting for transfers between devices, shards(): lax.all_to_all(packed, ('gx', 'gy'), split_axis=0, concat_axis=0, tiled=T...  2.62 us
  transfers between devices with their start and end apart: 17, of which 8 were waited for; matrix products, arithmetic and copies ran while one was open for 0% of the time, Pallas kernels for 7%

profile of v4, /device:TPU:13, one launch (start us, length us, event | category | flops | bytes accessed | tf_op | source)
XLA Modules:
  0.0 68.4 jit_solution(16060313706008497301)
XLA Ops:
  0.0 1.1 %copy-done.1 = f32[2,3,64,1,16,16]{2,5,4,3,1,0:T(8,128)S(1)} copy-done((f32[2,3,64,1,16,16]{2,5,4,3,1,0:T(8,128)S(1)}, f32[2,3,64,1,16,16]{2,5,4,3,1,0:T(8,128)}, u32[]{:S(2)}) %copy-start.1) | copy-done | bytes 393240
  1.1 1.2 %shard_map.28 = f32[1152,128]{1,0:T(8,128)} custom-call(f32[6,16,16,64]{3,2,1,0:T(8,128)S(1)} %bitcast.14), custom_call_target="tpu_custom_call" | custom-call | flops 1000000 | bytes 2097152 | tf_op jit(solution)/shard_map/pallas_call | solution.py:507
  2.3 10.7 %all-to-all-start = ((f32[128,1,1152]{2,1,0:T(1,128)}), f32[128,1,1152]{2,1,0:T(1,128)S(1)}, u32[]{:S(2)}, u32[]{:S(2)}) async-start(f32[128,1,1152]{2,1,0:T(1,128)} %bitcast.3), calls=%async_computation | async-start | bytes 1179648 | tf_op jit(solution)/shard_map/all_to_all | solution.py:568
  13.1 5.3 %collective-permute-start.1 = (f32[4,12,8,128]{3,2,1,0:T(8,128)S(1)}, f32[4,12,8,128]{3,2,1,0:T(8,128)S(1)}, u32[]{:S(2)}, u32[]{:S(2)}) collective-permute-start(f32[4,12,8,128]{3,2,1,0:T(8,128)S(1)} %get-tuple-element.33), channel_id=1, source_target_pairs={{8,16},{16,8},{24,32},{32,24},{40,48},{48,40},{56,64},{64,56},{72,... | collective-permute-start | bytes 589832 | tf_op jit(solution)/shard_map/ppermute | solution.py:532
  18.7 0.6 collective-permute-start
  19.2 2.7 %collective-permute-start.2 = (f32[4,6,8,128]{3,2,1,0:T(8,128)S(1)}, f32[4,6,8,128]{3,2,1,0:T(8,128)S(1)}, u32[]{:S(2)}, u32[]{:S(2)}) collective-permute-start(f32[4,6,8,128]{3,2,1,0:T(8,128)S(1)} %get-tuple-element.34), channel_id=1, source_target_pairs={{1,2},{2,1},{3,4},{4,3},{5,6},{6,5},{9,10},{10,9},{11,12},{12,11},... | collective-permute-start | bytes 294920 | tf_op jit(solution)/shard_map/ppermute | solution.py:532
  22.0 2.6 %all-to-all-done = f32[128,1,1152]{2,1,0:T(1,128)S(1)} async-done(((f32[128,1,1152]{2,1,0:T(1,128)}), f32[128,1,1152]{2,1,0:T(1,128)S(1)}, u32[]{:S(2)}, u32[]{:S(2)}) %all-to-all-start) | async-done | bytes 589856 | tf_op jit(solution)/shard_map/all_to_all | solution.py:568
  24.6 0.2 shard_map.29
  24.8 0.9 %shard_map.30.refs_0_ = f32[4,3,4,4,8,128]{5,4,3,2,1,0:T(8,128)S(1)} custom-call(f32[4,3,4,4,8,128]{5,4,3,2,1,0:T(8,128)S(1)} %bitcast.10, f32[3,128,128]{2,1,0:T(8,128)S(1)} %get-tuple-element.31.speed), custom_call_target="tpu_custom_call" | custom-call | flops 10000000 | bytes 2097152 | tf_op jit(solution)/shard_map/pallas_call | solution.py:507
  25.7 4.4 %collective-permute-done.refs_1_.refs_2_.refs_8_ = f32[4,6,8,128]{3,2,1,0:T(8,128)S(1)} collective-permute-done((f32[4,6,8,128]{3,2,1,0:T(8,128)S(1)}, f32[4,6,8,128]{3,2,1,0:T(8,128)S(1)}, u32[]{:S(2)}, u32[]{:S(2)}) %collective-permute-start) | collective-permute-done | bytes 98336 | tf_op jit(solution)/shard_map/ppermute | solution.py:532
  30.1 0.7 %collective-permute-done.1.refs_2_.refs_3_.refs_9_ = f32[4,12,8,128]{3,2,1,0:T(8,128)S(1)} collective-permute-done((f32[4,12,8,128]{3,2,1,0:T(8,128)S(1)}, f32[4,12,8,128]{3,2,1,0:T(8,128)S(1)}, u32[]{:S(2)}, u32[]{:S(2)}) %collective-permute-start.1) | collective-permute-done | bytes 196640 | tf_op jit(solution)/shard_map/ppermute | solution.py:532
  31.0 0.5 collective-permute-start.4
  31.5 4.9 %collective-permute-start.5 = (f32[4,10,8,128]{3,2,1,0:T(8,128)S(1)}, f32[4,10,8,128]{3,2,1,0:T(8,128)S(1)}, u32[]{:S(2)}, u32[]{:S(2)}) collective-permute-start(f32[4,10,8,128]{3,2,1,0:T(8,128)S(1)} %get-tuple-element.39), channel_id=1, source_target_pairs={{8,16},{16,8},{24,32},{32,24},{40,48},{48,40},{56,64},{64,56},{72,... | collective-permute-start | bytes 491528 | tf_op jit(solution)/shard_map/ppermute | solution.py:532
  36.4 1.9 %collective-permute-start.6 = (f32[4,5,8,128]{3,2,1,0:T(8,128)S(1)}, f32[4,5,8,128]{3,2,1,0:T(8,128)S(1)}, u32[]{:S(2)}, u32[]{:S(2)}) collective-permute-start(f32[4,5,8,128]{3,2,1,0:T(8,128)S(1)} %get-tuple-element.40), channel_id=1, source_target_pairs={{1,2},{2,1},{3,4},{4,3},{5,6},{6,5},{9,10},{10,9},{11,12},{12,11},... | collective-permute-start | bytes 245768 | tf_op jit(solution)/shard_map/ppermute | solution.py:532
  38.4 0.9 %shard_map.33.refs_0_ = f32[4,3,4,4,8,128]{5,4,3,2,1,0:T(8,128)S(1)} custom-call(f32[4,3,4,4,8,128]{5,4,3,2,1,0:T(8,128)S(1)} %get-tuple-element.37.state.refs_0_, f32[4,3,4,4,8,128]{5,4,3,2,1,0:T(8,128)S(1)} %bitcast.11, f32[3,128,128]{2,1,0:T(8,128)S(1)} %get-tuple-element.31.speed), custom_call_target="tpu_custom_call" | custom-call | flops 10000000 | bytes 2097152 | tf_op jit(solution)/shard_map/pallas_call | solution.py:507
  39.4 0.4 shard_map.36
  39.8 1.2 %collective-permute-done.5.arrived = f32[4,10,8,128]{3,2,1,0:T(8,128)S(1)} collective-permute-done((f32[4,10,8,128]{3,2,1,0:T(8,128)S(1)}, f32[4,10,8,128]{3,2,1,0:T(8,128)S(1)}, u32[]{:S(2)}, u32[]{:S(2)}) %collective-permute-start.5) | collective-permute-done | bytes 163872 | tf_op jit(solution)/shard_map/ppermute | solution.py:532
  41.0 1.5 %collective-permute-done.6.refs_3_.refs_4_ = f32[4,5,8,128]{3,2,1,0:T(8,128)S(1)} collective-permute-done((f32[4,5,8,128]{3,2,1,0:T(8,128)S(1)}, f32[4,5,8,128]{3,2,1,0:T(8,128)S(1)}, u32[]{:S(2)}, u32[]{:S(2)}) %collective-permute-start.6) | collective-permute-done | bytes 81952 | tf_op jit(solution)/shard_map/ppermute | solution.py:532
  42.5 0.3 shard_map.37
  42.8 0.7 %collective-permute-start.8 = (f32[4,5,8,128]{3,2,1,0:T(8,128)S(1)}, f32[4,5,8,128]{3,2,1,0:T(8,128)S(1)}, u32[]{:S(2)}, u32[]{:S(2)}) collective-permute-start(f32[4,5,8,128]{3,2,1,0:T(8,128)S(1)} %get-tuple-element.46), channel_id=1, source_target_pairs={{0,1},{1,0},{2,3},{3,2},{4,5},{5,4},{6,7},{7,6},{8,9},{9,8},{10,11... | collective-permute-start | bytes 245768 | tf_op jit(solution)/shard_map/ppermute | solution.py:532
  43.5 4.6 %collective-permute-start.9 = (f32[4,10,8,128]{3,2,1,0:T(8,128)S(1)}, f32[4,10,8,128]{3,2,1,0:T(8,128)S(1)}, u32[]{:S(2)}, u32[]{:S(2)}) collective-permute-start(f32[4,10,8,128]{3,2,1,0:T(8,128)S(1)} %get-tuple-element.47), channel_id=1, source_target_pairs={{8,16},{16,8},{24,32},{32,24},{40,48},{48,40},{56,64},{64,56},{72,... | collective-permute-start | bytes 491528 | tf_op jit(solution)/shard_map/ppermute | solution.py:532
  48.1 2.7 %collective-permute-start.10 = (f32[4,5,8,128]{3,2,1,0:T(8,128)S(1)}, f32[4,5,8,128]{3,2,1,0:T(8,128)S(1)}, u32[]{:S(2)}, u32[]{:S(2)}) collective-permute-start(f32[4,5,8,128]{3,2,1,0:T(8,128)S(1)} %get-tuple-element.48), channel_id=1, source_target_pairs={{1,2},{2,1},{3,4},{4,3},{5,6},{6,5},{9,10},{10,9},{11,12},{12,11},... | collective-permute-start | bytes 245768 | tf_op jit(solution)/shard_map/ppermute | solution.py:532
  50.9 0.9 %shard_map.38.refs_0_ = f32[4,3,4,4,8,128]{5,4,3,2,1,0:T(8,128)S(1)} custom-call(f32[4,3,4,4,8,128]{5,4,3,2,1,0:T(8,128)S(1)} %get-tuple-element.45.state.start, f32[3,128,128]{2,1,0:T(8,128)S(1)} %get-tuple-element.44.refs_8_.speed.refs_7_), custom_call_target="tpu_custom_call" | custom-call | flops 10000000 | bytes 2097152 | tf_op jit(solution)/shard_map/pallas_call | solution.py:507
  51.8 0.4 shard_map.41
  52.2 0.8 %collective-permute-done.9.arrived = f32[4,10,8,128]{3,2,1,0:T(8,128)S(1)} collective-permute-done((f32[4,10,8,128]{3,2,1,0:T(8,128)S(1)}, f32[4,10,8,128]{3,2,1,0:T(8,128)S(1)}, u32[]{:S(2)}, u32[]{:S(2)}) %collective-permute-start.9) | collective-permute-done | bytes 163872 | tf_op jit(solution)/shard_map/ppermute | solution.py:532
  53.0 1.2 %collective-permute-done.10.refs_3_ = f32[4,5,8,128]{3,2,1,0:T(8,128)S(1)} collective-permute-done((f32[4,5,8,128]{3,2,1,0:T(8,128)S(1)}, f32[4,5,8,128]{3,2,1,0:T(8,128)S(1)}, u32[]{:S(2)}, u32[]{:S(2)}) %collective-permute-start.10) | collective-permute-done | bytes 81952 | tf_op jit(solution)/shard_map/ppermute | solution.py:532
  54.4 1.6 %collective-permute-start.12 = (f32[4,6,8,128]{3,2,1,0:T(8,128)S(1)}, f32[4,6,8,128]{3,2,1,0:T(8,128)S(1)}, u32[]{:S(2)}, u32[]{:S(2)}) collective-permute-start(f32[4,6,8,128]{3,2,1,0:T(8,128)S(1)} %get-tuple-element.53), channel_id=1, source_target_pairs={{0,1},{1,0},{2,3},{3,2},{4,5},{5,4},{6,7},{7,6},{8,9},{9,8},{10,11... | collective-permute-start | bytes 294920 | tf_op jit(solution)/shard_map/ppermute | solution.py:532
  56.0 3.9 %collective-permute-start.13 = (f32[4,12,8,128]{3,2,1,0:T(8,128)S(1)}, f32[4,12,8,128]{3,2,1,0:T(8,128)S(1)}, u32[]{:S(2)}, u32[]{:S(2)}) collective-permute-start(f32[4,12,8,128]{3,2,1,0:T(8,128)S(1)} %get-tuple-element.54), channel_id=1, source_target_pairs={{8,16},{16,8},{24,32},{32,24},{40,48},{48,40},{56,64},{64,56},{72,... | collective-permute-start | bytes 589832 | tf_op jit(solution)/shard_map/ppermute | solution.py:532
  59.9 1.9 %collective-permute-start.14 = (f32[4,6,8,128]{3,2,1,0:T(8,128)S(1)}, f32[4,6,8,128]{3,2,1,0:T(8,128)S(1)}, u32[]{:S(2)}, u32[]{:S(2)}) collective-permute-start(f32[4,6,8,128]{3,2,1,0:T(8,128)S(1)} %get-tuple-element.55), channel_id=1, source_target_pairs={{1,2},{2,1},{3,4},{4,3},{5,6},{6,5},{9,10},{10,9},{11,12},{12,11},... | collective-permute-start | bytes 294920 | tf_op jit(solution)/shard_map/ppermute | solution.py:532
  61.9 0.9 %shard_map.43.refs_0_ = f32[4,3,4,4,8,128]{5,4,3,2,1,0:T(8,128)S(1)} custom-call(f32[4,3,4,4,8,128]{5,4,3,2,1,0:T(8,128)S(1)} %get-tuple-element.52.state, f32[4,3,4,4,8,128]{5,4,3,2,1,0:T(8,128)S(1)} %get-tuple-element.45.state.start, f32[3,128,128]{2,1,0:T(8,128)S(1)} %get-tuple-element.44.refs_8_.speed.refs_7_), custom_call_target="tpu_custom_call" | custom-call | flops 10000000 | bytes 2097152 | tf_op jit(solution)/shard_map/pallas_call | solution.py:507
  62.9 4.5 %collective-permute-done.13.arrived = f32[4,12,8,128]{3,2,1,0:T(8,128)S(1)} collective-permute-done((f32[4,12,8,128]{3,2,1,0:T(8,128)S(1)}, f32[4,12,8,128]{3,2,1,0:T(8,128)S(1)}, u32[]{:S(2)}, u32[]{:S(2)}) %collective-permute-start.13) | collective-permute-done | bytes 196640 | tf_op jit(solution)/shard_map/ppermute | solution.py:532
  67.4 0.9 %shard_map.46 = f32[4,3,4,4,8,128]{5,4,3,2,1,0:T(8,128)} custom-call(f32[4,3,4,4,8,128]{5,4,3,2,1,0:T(8,128)S(1)} %shard_map.43.refs_0_, f32[4,6,8,128]{3,2,1,0:T(8,128)S(1)} %shard_map.44.refs_0_.refs_1_, f32[4,12,8,128]{3,2,1,0:T(8,128)S(1)} %shard_map.45.refs_2_, f32[4,6,8,128]{3,2,1,0:T(8,128)S(1)} %collective-permute-done.14.refs_3_, ...), custom_call_target="tpu_custom_call" | custom-call | flops 1000000 | bytes 2000000 | tf_op jit(solution)/shard_map/pallas_call | solution.py:608
  (25 shorter events, 1.0 us)
Async XLA Ops:
  0.0 1.1 %copy-start.1 = (f32[2,3,64,1,16,16]{2,5,4,3,1,0:T(8,128)S(1)}, f32[2,3,64,1,16,16]{2,5,4,3,1,0:T(8,128)}, u32[]{:S(2)}) copy-start(f32[2,3,64,1,16,16]{2,5,4,3,1,0:T(8,128)} %param.3) | copy-start | bytes 1179652
  2.3 10.7 %copy-start = (f32[4,3,64,1,2,128]{5,4,3,2,1,0:T(2,128)S(1)}, f32[4,3,64,1,2,128]{5,4,3,2,1,0:T(2,128)}, u32[]{:S(2)}) copy-start(f32[4,3,64,1,2,128]{5,4,3,2,1,0:T(2,128)} %param.2) | copy-start | bytes 2359300
  2.3 22.3 %all-to-all-start = ((f32[128,1,1152]{2,1,0:T(1,128)}), f32[128,1,1152]{2,1,0:T(1,128)S(1)}, u32[]{:S(2)}, u32[]{:S(2)}) async-start(f32[128,1,1152]{2,1,0:T(1,128)} %bitcast.3), calls=%async_computation | async-start | bytes 1179648 | tf_op jit(solution)/shard_map/all_to_all | solution.py:568
  13.1 17.7 %collective-permute-start.1 = (f32[4,12,8,128]{3,2,1,0:T(8,128)S(1)}, f32[4,12,8,128]{3,2,1,0:T(8,128)S(1)}, u32[]{:S(2)}, u32[]{:S(2)}) collective-permute-start(f32[4,12,8,128]{3,2,1,0:T(8,128)S(1)} %get-tuple-element.33), channel_id=1, source_target_pairs={{8,16},{16,8},{24,32},{32,24},{40,48},{48,40},{56,64},{64,56},{72,... | collective-permute-start | bytes 589832 | tf_op jit(solution)/shard_map/ppermute | solution.py:532
  18.5 12.4 %collective-permute-start.3 = (f32[4,12,8,128]{3,2,1,0:T(8,128)S(1)}, f32[4,12,8,128]{3,2,1,0:T(8,128)S(1)}, u32[]{:S(2)}, u32[]{:S(2)}) collective-permute-start(f32[4,12,8,128]{3,2,1,0:T(8,128)S(1)} %get-tuple-element.35), channel_id=1, source_target_pairs={{0,8},{8,0},{16,24},{24,16},{32,40},{40,32},{48,56},{56,48},{64,72... | collective-permute-start | bytes 589832 | tf_op jit(solution)/shard_map/ppermute | solution.py:532
  18.7 11.4 %collective-permute-start = (f32[4,6,8,128]{3,2,1,0:T(8,128)S(1)}, f32[4,6,8,128]{3,2,1,0:T(8,128)S(1)}, u32[]{:S(2)}, u32[]{:S(2)}) collective-permute-start(f32[4,6,8,128]{3,2,1,0:T(8,128)S(1)} %get-tuple-element.32), channel_id=1, source_target_pairs={{0,1},{1,0},{2,3},{3,2},{4,5},{5,4},{6,7},{7,6},{8,9},{9,8},{10,11... | collective-permute-start | bytes 294920 | tf_op jit(solution)/shard_map/ppermute | solution.py:532
  19.2 10.9 %collective-permute-start.2 = (f32[4,6,8,128]{3,2,1,0:T(8,128)S(1)}, f32[4,6,8,128]{3,2,1,0:T(8,128)S(1)}, u32[]{:S(2)}, u32[]{:S(2)}) collective-permute-start(f32[4,6,8,128]{3,2,1,0:T(8,128)S(1)} %get-tuple-element.34), channel_id=1, source_target_pairs={{1,2},{2,1},{3,4},{4,3},{5,6},{6,5},{9,10},{10,9},{11,12},{12,11},... | collective-permute-start | bytes 294920 | tf_op jit(solution)/shard_map/ppermute | solution.py:532
  31.0 8.7 %collective-permute-start.4 = (f32[4,5,8,128]{3,2,1,0:T(8,128)S(1)}, f32[4,5,8,128]{3,2,1,0:T(8,128)S(1)}, u32[]{:S(2)}, u32[]{:S(2)}) collective-permute-start(f32[4,5,8,128]{3,2,1,0:T(8,128)S(1)} %get-tuple-element.38), channel_id=1, source_target_pairs={{0,1},{1,0},{2,3},{3,2},{4,5},{5,4},{6,7},{7,6},{8,9},{9,8},{10,11... | collective-permute-start | bytes 245768 | tf_op jit(solution)/shard_map/ppermute | solution.py:532
  31.5 9.5 %collective-permute-start.5 = (f32[4,10,8,128]{3,2,1,0:T(8,128)S(1)}, f32[4,10,8,128]{3,2,1,0:T(8,128)S(1)}, u32[]{:S(2)}, u32[]{:S(2)}) collective-permute-start(f32[4,10,8,128]{3,2,1,0:T(8,128)S(1)} %get-tuple-element.39), channel_id=1, source_target_pairs={{8,16},{16,8},{24,32},{32,24},{40,48},{48,40},{56,64},{64,56},{72,... | collective-permute-start | bytes 491528 | tf_op jit(solution)/shard_map/ppermute | solution.py:532
  36.4 6.1 %collective-permute-start.6 = (f32[4,5,8,128]{3,2,1,0:T(8,128)S(1)}, f32[4,5,8,128]{3,2,1,0:T(8,128)S(1)}, u32[]{:S(2)}, u32[]{:S(2)}) collective-permute-start(f32[4,5,8,128]{3,2,1,0:T(8,128)S(1)} %get-tuple-element.40), channel_id=1, source_target_pairs={{1,2},{2,1},{3,4},{4,3},{5,6},{6,5},{9,10},{10,9},{11,12},{12,11},... | collective-permute-start | bytes 245768 | tf_op jit(solution)/shard_map/ppermute | solution.py:532
  38.3 4.2 %collective-permute-start.7 = (f32[4,10,8,128]{3,2,1,0:T(8,128)S(1)}, f32[4,10,8,128]{3,2,1,0:T(8,128)S(1)}, u32[]{:S(2)}, u32[]{:S(2)}) collective-permute-start(f32[4,10,8,128]{3,2,1,0:T(8,128)S(1)} %get-tuple-element.41), channel_id=1, source_target_pairs={{0,8},{8,0},{16,24},{24,16},{32,40},{40,32},{48,56},{56,48},{64,72... | collective-permute-start | bytes 491528 | tf_op jit(solution)/shard_map/ppermute | solution.py:532
  42.8 9.4 %collective-permute-start.8 = (f32[4,5,8,128]{3,2,1,0:T(8,128)S(1)}, f32[4,5,8,128]{3,2,1,0:T(8,128)S(1)}, u32[]{:S(2)}, u32[]{:S(2)}) collective-permute-start(f32[4,5,8,128]{3,2,1,0:T(8,128)S(1)} %get-tuple-element.46), channel_id=1, source_target_pairs={{0,1},{1,0},{2,3},{3,2},{4,5},{5,4},{6,7},{7,6},{8,9},{9,8},{10,11... | collective-permute-start | bytes 245768 | tf_op jit(solution)/shard_map/ppermute | solution.py:532
  43.5 9.5 %collective-permute-start.9 = (f32[4,10,8,128]{3,2,1,0:T(8,128)S(1)}, f32[4,10,8,128]{3,2,1,0:T(8,128)S(1)}, u32[]{:S(2)}, u32[]{:S(2)}) collective-permute-start(f32[4,10,8,128]{3,2,1,0:T(8,128)S(1)} %get-tuple-element.47), channel_id=1, source_target_pairs={{8,16},{16,8},{24,32},{32,24},{40,48},{48,40},{56,64},{64,56},{72,... | collective-permute-start | bytes 491528 | tf_op jit(solution)/shard_map/ppermute | solution.py:532
  48.1 6.1 %collective-permute-start.10 = (f32[4,5,8,128]{3,2,1,0:T(8,128)S(1)}, f32[4,5,8,128]{3,2,1,0:T(8,128)S(1)}, u32[]{:S(2)}, u32[]{:S(2)}) collective-permute-start(f32[4,5,8,128]{3,2,1,0:T(8,128)S(1)} %get-tuple-element.48), channel_id=1, source_target_pairs={{1,2},{2,1},{3,4},{4,3},{5,6},{6,5},{9,10},{10,9},{11,12},{12,11},... | collective-permute-start | bytes 245768 | tf_op jit(solution)/shard_map/ppermute | solution.py:532
  50.8 3.4 %collective-permute-start.11 = (f32[4,10,8,128]{3,2,1,0:T(8,128)S(1)}, f32[4,10,8,128]{3,2,1,0:T(8,128)S(1)}, u32[]{:S(2)}, u32[]{:S(2)}) collective-permute-start(f32[4,10,8,128]{3,2,1,0:T(8,128)S(1)} %get-tuple-element.49), channel_id=1, source_target_pairs={{0,8},{8,0},{16,24},{24,16},{32,40},{40,32},{48,56},{56,48},{64,72... | collective-permute-start | bytes 491528 | tf_op jit(solution)/shard_map/ppermute | solution.py:532
  54.4 8.5 %collective-permute-start.12 = (f32[4,6,8,128]{3,2,1,0:T(8,128)S(1)}, f32[4,6,8,128]{3,2,1,0:T(8,128)S(1)}, u32[]{:S(2)}, u32[]{:S(2)}) collective-permute-start(f32[4,6,8,128]{3,2,1,0:T(8,128)S(1)} %get-tuple-element.53), channel_id=1, source_target_pairs={{0,1},{1,0},{2,3},{3,2},{4,5},{5,4},{6,7},{7,6},{8,9},{9,8},{10,11... | collective-permute-start | bytes 294920 | tf_op jit(solution)/shard_map/ppermute | solution.py:532
  56.0 11.3 %collective-permute-start.13 = (f32[4,12,8,128]{3,2,1,0:T(8,128)S(1)}, f32[4,12,8,128]{3,2,1,0:T(8,128)S(1)}, u32[]{:S(2)}, u32[]{:S(2)}) collective-permute-start(f32[4,12,8,128]{3,2,1,0:T(8,128)S(1)} %get-tuple-element.54), channel_id=1, source_target_pairs={{8,16},{16,8},{24,32},{32,24},{40,48},{48,40},{56,64},{64,56},{72,... | collective-permute-start | bytes 589832 | tf_op jit(solution)/shard_map/ppermute | solution.py:532
  59.9 7.5 %collective-permute-start.14 = (f32[4,6,8,128]{3,2,1,0:T(8,128)S(1)}, f32[4,6,8,128]{3,2,1,0:T(8,128)S(1)}, u32[]{:S(2)}, u32[]{:S(2)}) collective-permute-start(f32[4,6,8,128]{3,2,1,0:T(8,128)S(1)} %get-tuple-element.55), channel_id=1, source_target_pairs={{1,2},{2,1},{3,4},{4,3},{5,6},{6,5},{9,10},{10,9},{11,12},{12,11},... | collective-permute-start | bytes 294920 | tf_op jit(solution)/shard_map/ppermute | solution.py:532
  61.8 5.6 %collective-permute-start.15 = (f32[4,12,8,128]{3,2,1,0:T(8,128)S(1)}, f32[4,12,8,128]{3,2,1,0:T(8,128)S(1)}, u32[]{:S(2)}, u32[]{:S(2)}) collective-permute-start(f32[4,12,8,128]{3,2,1,0:T(8,128)S(1)} %get-tuple-element.56), channel_id=1, source_target_pairs={{0,8},{8,0},{16,24},{24,16},{32,40},{40,32},{48,56},{56,48},{64,72... | collective-permute-start | bytes 589832 | tf_op jit(solution)/shard_map/ppermute | solution.py:532

commit v5 on v3

--- a/solution.py
+++ b/solution.py
@@ -239,6 +239,23 @@
         y_odd[k, slot] = pick(py, up, down)
 
 
+class Ghosts:
+    def __init__(self, here, partner, px):
+        self.here, self.partner, self.px = here, partner, px
+
+    def x(self, side, b):
+        part = pl.ds(b * 8, 8)
+        values = []
+        for i in range(3):
+            even, odd = self.partner[i, part, :], self.here[i, part, :]
+            values.append(pick(self.px, even, odd) if side == 0 else pick(self.px, odd, even))
+        return values
+
+    def y(self, a):
+        start = (SIDE + a) * 8
+        return [self.here[i, start : start + 8, :] for i in range(3)]
+
+
 class Arrived:
     def __init__(self, form, faces, inner, px, py):
         self.form, self.inner, self.px, self.py = form, inner, px, py
@@ -263,11 +280,7 @@
         return self.inner[1][k, a - 1]
 
 
-def ghost_at(ghost_speed, place):
-    return [ghost_speed[i, place * 8 : place * 8 + 8, :] for i in range(3)]
-
-
-def receive_faces(k, pre, out, ghost_speed, arrived, coef):
+def receive_faces(k, pre, out, ghosts, arrived, coef):
     jump = FLUX_COEF * coef
     odd = rows() % 2 == 1
     zero = jnp.zeros((8, LANES), F32)
@@ -277,9 +290,9 @@
     for b in range(SIDE):
         low = [arrived.x(k, 0, i, b) for i in range(3)]
         high = [arrived.x(k, 1, i, b) for i in range(3)]
-        if ghost_speed is not None:
-            low = minus(0, low, cross(ghost_at(ghost_speed, b), low))
-            high = plus(0, high, cross(ghost_at(ghost_speed, SIDE + b), high))
+        if ghosts is not None:
+            low = minus(0, low, cross(ghosts.x(0, b), low))
+            high = plus(0, high, cross(ghosts.x(1, b), high))
         for i in range(3):
             out[k, i, 0, b] = pre[k, i, 0, b] + F32(jump) * low[i]
             out[k, i, SIDE - 1, b] = pre[k, i, SIDE - 1, b] + F32(jump) * high[i]
@@ -289,15 +302,15 @@
                 out[k, i, a, b] = pre[k, i, a, b]
     for a in range(SIDE):
         both = [arrived.y(k, i, a) for i in range(3)]
-        if ghost_speed is not None:
-            e = cross(ghost_at(ghost_speed, 2 * SIDE + a), both)
+        if ghosts is not None:
+            e = cross(ghosts.y(a), both)
             both = [both[0] + turn * e[2], both[1], both[2] - turn * e[0]]
         for i in range(3):
             out[k, i, a, 0] = out[k, i, a, 0] + mask_low * both[i]
             out[k, i, a, SIDE - 1] = out[k, i, a, SIDE - 1] + mask_high * both[i]
 
 
-def inside(k, state, now, before, ghost_speed, inner_x, inner_y, coef):
+def inside(k, state, now, before, ghosts, inner_x, inner_y, coef):
     row, lane = rows(), lanes()
     table = coef * TABLE
     third = third_table(coef)
@@ -327,7 +340,7 @@
     for side in range(2):
         there = at_x > 0 if side == 0 else at_x < last_x
         m = [[now.x(k, side, i, b) for i in range(3)] for b in range(SIDE)]
-        e = [cross(ghost_at(ghost_speed, side * SIDE + b), m[b]) for b in range(SIDE)]
+        e = [cross(ghosts.x(side, b), m[b]) for b in range(SIDE)]
         for b in (1, 2):
             own = m[b][0]
             total = weighted(table[b], [e[q][2] for q in range(SIDE)]) - along_third(e[b][1])
@@ -336,7 +349,7 @@
             old = None if before is None else before.x(k, side, 0, b)
             inner_x[k, side, b - 1] = pick(there, start(own, old) + total, zero)
     m = [[now.y(k, i, a) for i in range(3)] for a in range(SIDE)]
-    e = [cross(ghost_at(ghost_speed, 2 * SIDE + a), m[a]) for a in range(SIDE)]
+    e = [cross(ghosts.y(a), m[a]) for a in range(SIDE)]
     for a in (1, 2):
         own = m[a][1]
         total = along_third(e[a][0]) - weighted(table[a], [e[q][2] for q in range(SIDE)])
@@ -350,14 +363,15 @@
         inner_y[k, a - 1] = jnp.where(odd, high, low)
 
 
-ROWS = 9
+ROWS = 8
 
 
 def pack_kernel(velocity, out):
     wide = velocity.shape[1]
     pairs = velocity.shape[2] // 2
-    lane = lax.broadcasted_iota(jnp.int32, (pairs, 64), 1)
-    upper = lane % 16 >= 12
+    upper = lax.broadcasted_iota(jnp.int32, (pairs, 64), 1) % 16 >= 12
+    lane = lax.broadcasted_iota(jnp.int32, (pairs, LANES), 1)
+    inner = (lane % 16 >= 4) & (lane % 16 < 12)
 
     def both(q, x):
         return [velocity[q, x, pl.ds(j, pairs, stride=2), :] for j in range(2)]
@@ -368,25 +382,18 @@
     for x in range(wide):
         for q in range(6):
             store(x, q, jnp.concatenate(both(q, x), axis=1))
+        beside, nodes = (max(x - 1, 0), 48) if x % 2 == 0 else (min(x + 1, wide - 1), 0)
+        y_part = []
         for q in range(3):
             even, odd = both(q, x)
-            even_low, odd_low = both(q, (x - 1) % wide)
-            even_high, odd_high = both(q, (x + 1) % wide)
-            y_part = jnp.where(upper, pltpu.roll(odd, 1, 0), pltpu.roll(even, pairs - 1, 0))
-            store(
-                x,
-                6 + q,
-                jnp.concatenate(
-                    [
-                        y_part,
-                        even_high[:, :16],
-                        odd_high[:, :16],
-                        odd_low[:, 48:],
-                        even_low[:, 48:],
-                    ],
-                    axis=1,
-                ),
-            )
+            y_part.append(jnp.where(upper, pltpu.roll(odd, 1, 0), pltpu.roll(even, pairs - 1, 0)))
+        third = jnp.concatenate(both(2, beside), axis=1)
+        row = jnp.concatenate(y_part[:2], axis=1)
+        row = jnp.where(inner, pltpu.roll(third, 24, 1), row)
+        row = jnp.where(inner & (lane % 64 // 16 == nodes // 16), third, row)
+        store(x, 6, row)
+        pieces = [v[:, nodes : nodes + 16] for q in range(2) for v in both(q, beside)]
+        store(x, 7, jnp.concatenate([y_part[2], *pieces], axis=1))
 
 
 def faces_kernel(state, *faces):
@@ -399,22 +406,34 @@
     lax.fori_loop(0, KRYLOV, step, 0)
 
 
-def unpack_kernel(arrived, first, second, ghosts):
-    for q in range(ROWS):
-        block = arrived[pl.ds(q, LANES, stride=ROWS), :].T
-        if q < 6:
-            into = first if q < 3 else second
-            into[q % 3, pl.ds(0, 64, stride=2), :] = block[:64]
-            into[q % 3, pl.ds(1, 64, stride=2), :] = block[64:]
-        else:
-            i = q - 6
-            ghosts[i, pl.ds(0, 16, stride=2), :] = block[112:]
-            ghosts[i, pl.ds(1, 16, stride=2), :] = block[96:112]
-            ghosts[i, pl.ds(32, 16, stride=2), :] = block[64:80]
-            ghosts[i, pl.ds(33, 16, stride=2), :] = block[80:96]
-            for a in range(SIDE):
-                ghosts[i, pl.ds(64 + a * 8, 4, stride=2), :] = block[a * 16 + 12 : a * 16 + 16]
-                ghosts[i, pl.ds(65 + a * 8, 4, stride=2), :] = block[a * 16 : a * 16 + 4]
+def unpack_kernel(arrived, first, second, here, partner):
+    px, _ = parities()
+    blocks = [arrived[pl.ds(q, LANES, stride=ROWS), :].T for q in range(ROWS)]
+    for q in range(6):
+        into = first if q < 3 else second
+        into[q % 3, pl.ds(0, 64, stride=2), :] = blocks[q][:64]
+        into[q % 3, pl.ds(1, 64, stride=2), :] = blocks[q][64:]
+    for i in range(3):
+        block = blocks[6][64 * i : 64 * i + 64] if i < 2 else blocks[7][:64]
+        for a in range(SIDE):
+            low, high = block[a * 16 + 12 : a * 16 + 16], block[a * 16 : a * 16 + 4]
+            here[i, pl.ds(32 + a * 8, 4, stride=2), :] = low
+            here[i, pl.ds(33 + a * 8, 4, stride=2), :] = high
+    for i in range(2):
+        for j in range(2):
+            start = 64 + 32 * i + 16 * j
+            here[i, pl.ds(j, 16, stride=2), :] = blocks[7][start : start + 16]
+    for j in range(2):
+        for b in range(SIDE):
+            shift = 4 * b if b in (1, 2) else 4 * b + 24
+            places = [(group * 16 + 64 * j + shift) % LANES for group in (3, 0)]
+            low, high = [blocks[6][place : place + 4] for place in places]
+            here[2, pl.ds(b * 8 + j, 4, stride=2), :] = pick(px, high, low)
+    for i in range(3):
+        for b in range(SIDE):
+            low = first[i, b * 8 : b * 8 + 8, :]
+            high = first[i, 96 + b * 8 : 104 + b * 8, :]
+            partner[i, b * 8 : b * 8 + 8, :] = pick(px, low, high)
 
 
 def first_volume_kernel(state, speed, pre, elec):
@@ -441,7 +460,8 @@
 
 def inside_kernel(coef, forms, *refs):
     px, py = parities()
-    state, ghost_speed, *refs, inner_x, inner_y = refs
+    state, here, partner, *refs, inner_x, inner_y = refs
+    ghosts = Ghosts(here, partner, px)
     stages = []
     for form in forms:
         faces, refs = refs[:4], refs[4:]
@@ -453,7 +473,7 @@
     before = stages[1] if len(stages) > 1 else None
 
     def step(k, carry):
-        inside(k, state, now, before, ghost_speed, inner_x, inner_y, coef)
+        inside(k, state, now, before, ghosts, inner_x, inner_y, coef)
         return carry
 
     lax.fori_loop(0, KRYLOV, step, 0)
@@ -467,7 +487,8 @@
     if form.short:
         inner, refs = refs[:2], refs[2:]
     if has_ghosts:
-        ghosts, *refs = refs
+        here, partner, *refs = refs
+        ghosts = Ghosts(here, partner, px)
     if next_speed:
         speed, *refs = refs
     out, *leaving = refs
@@ -485,7 +506,8 @@
 STATE = (KRYLOV, 3, SIDE, SIDE, 8, LANES)
 INNER = [(KRYLOV, 2, 2, 8, LANES), (KRYLOV, 2, 8, LANES)]
 SPEED = (3, 128, LANES)
-GHOSTS = (3, 96, LANES)
+GHOSTS = (3, 64, LANES)
+PARTNER = (3, 32, LANES)
 
 
 def call(kernel, shapes, flops, *operands, scratch=()):
@@ -554,7 +576,11 @@
     moved = lax.all_to_all(packed, ("gx", "gy"), split_axis=0, concat_axis=0, tiled=True)
     moved = moved.reshape(devices * ROWS, LANES)
     arrived = exchange(call(faces_kernel, FULL.shapes(), 10**6, state), ())
-    *speeds, ghosts = call(unpack_kernel, [SPEED, SPEED, GHOSTS], 10**6, moved)
+    shapes = [SPEED, SPEED, GHOSTS, PARTNER]
+    *speeds, here, leaving = call(unpack_kernel, shapes, 10**6, moved)
+    count = lax.axis_size("gx")
+    partner = lax.ppermute(leaving, "gx", [(i, i ^ 1) for i in range(count)])
+    ghosts = (here, partner)
     elec = [(3, SIDE, SIDE, 8, LANES)]
 
     def finish(coef, form, ghosts, next_form, speed, pre, *arrived):
@@ -563,7 +589,8 @@
                 coef, form, ghosts is not None, next_form, speed is not None, *refs
             )
 
-        extra = [array for array in (ghosts, speed) if array is not None]
+        extra = [] if ghosts is None else [*ghosts]
+        extra += [] if speed is None else [speed]
         shapes = [STATE] if next_form is None else [STATE, *next_form.shapes()]
         return call(kernel, shapes, 10**6, pre, *arrived, *extra)
 
@@ -571,7 +598,7 @@
         def kernel(*refs):
             inside_kernel(coef, forms, *refs)
 
-        return call(kernel, INNER, 10**7, state, ghosts, *arrived)
+        return call(kernel, INNER, 10**7, state, *ghosts, *arrived)
 
     whole, half = STEP_SIZE, 0.5 * STEP_SIZE
     (pre,) = call(first_volume_kernel, [STATE], 10**7, state, speeds[0], scratch=elec)

time: 68.9 us -> 69 us (level)
  waiting for transfers between devices: 16.6 us -> 15.6 us
  starting transfers between devices: 42.6 us -> 43.4 us
    ppermute x0 -> x1, starting transfers between devices: none -> 0.97 us  [shards(): partner = lax.ppermute(leaving, 'gx', [(i, i ^ 1) for i in range(count)])]
    all_to_all x1, waiting for transfers between devices: 2.62 us -> 1.89 us  [shards(): lax.all_to_all(packed, ('gx', 'gy'), split_axis=0, concat_axis=0, tiled=T...]
  transfers between devices with their start and end apart: 17 -> 18, of which waited for: 8 -> 8; matrix products, arithmetic and copies ran while one was open for 0% -> 0% of each run, Pallas kernels for 8% -> 7%
where the time goes in v5:
time: 69 us; the launch traced here: 68.7 us
  starting transfers between devices  43.4 us (63%)
  waiting for transfers between devices  15.6 us (23%)
  Pallas kernels  8.2 us (12%)
  local copies, waits for them, and re-layouts  1.14 us (2%)
    ppermute x16, starting transfers between devices, exchange(): received.append(lax.ppermute(face, axis, pairs))  31.8 us
    ppermute x16, waiting for transfers between devices, exchange(): received.append(lax.ppermute(face, axis, pairs))  13.7 us
    all_to_all x1, starting transfers between devices, shards(): lax.all_to_all(packed, ('gx', 'gy'), split_axis=0, concat_axis=0, tiled=T...  10.7 us
    pallas_call x13, Pallas kernels, call(): pl.pallas_call(kernel, out_shape=[jax.ShapeDtypeStruct(shape, F32) for sh...  8.14 us
    all_to_all x1, waiting for transfers between devices, shards(): lax.all_to_all(packed, ('gx', 'gy'), split_axis=0, concat_axis=0, tiled=T...  1.89 us
  transfers between devices with their start and end apart: 18, of which 8 were waited for; matrix products, arithmetic and copies ran while one was open for 0% of the time, Pallas kernels for 7%

profile of v5, /device:TPU:13, one launch (start us, length us, event | category | flops | bytes accessed | tf_op | source)
XLA Modules:
  0.0 68.7 jit_solution(10345704396947257555)
XLA Ops:
  0.0 1.1 %copy-done.1 = f32[2,3,64,1,16,16]{2,5,4,3,1,0:T(8,128)S(1)} copy-done((f32[2,3,64,1,16,16]{2,5,4,3,1,0:T(8,128)S(1)}, f32[2,3,64,1,16,16]{2,5,4,3,1,0:T(8,128)}, u32[]{:S(2)}) %copy-start.1) | copy-done | bytes 393240
  1.1 1.4 %shard_map.28 = f32[1024,128]{1,0:T(8,128)} custom-call(f32[6,16,16,64]{3,2,1,0:T(8,128)S(1)} %bitcast.14), custom_call_target="tpu_custom_call" | custom-call | flops 1000000 | bytes 2097152 | tf_op jit(solution)/shard_map/pallas_call | solution.py:515
  2.5 10.7 %all-to-all-start = ((f32[128,1,1024]{2,1,0:T(1,128)}), f32[128,1,1024]{2,1,0:T(1,128)S(1)}, u32[]{:S(2)}, u32[]{:S(2)}) async-start(f32[128,1,1024]{2,1,0:T(1,128)} %bitcast.3), calls=%async_computation | async-start | bytes 1048576 | tf_op jit(solution)/shard_map/all_to_all | solution.py:576
  13.3 5.3 %collective-permute-start.1 = (f32[4,12,8,128]{3,2,1,0:T(8,128)S(1)}, f32[4,12,8,128]{3,2,1,0:T(8,128)S(1)}, u32[]{:S(2)}, u32[]{:S(2)}) collective-permute-start(f32[4,12,8,128]{3,2,1,0:T(8,128)S(1)} %get-tuple-element.34), channel_id=1, source_target_pairs={{8,16},{16,8},{24,32},{32,24},{40,48},{48,40},{56,64},{64,56},{72,... | collective-permute-start | bytes 589832 | tf_op jit(solution)/shard_map/ppermute | solution.py:540
  18.9 0.6 collective-permute-start
  19.4 2.7 %collective-permute-start.2 = (f32[4,6,8,128]{3,2,1,0:T(8,128)S(1)}, f32[4,6,8,128]{3,2,1,0:T(8,128)S(1)}, u32[]{:S(2)}, u32[]{:S(2)}) collective-permute-start(f32[4,6,8,128]{3,2,1,0:T(8,128)S(1)} %get-tuple-element.35), channel_id=1, source_target_pairs={{1,2},{2,1},{3,4},{4,3},{5,6},{6,5},{9,10},{10,9},{11,12},{12,11},... | collective-permute-start | bytes 294920 | tf_op jit(solution)/shard_map/ppermute | solution.py:540
  22.2 1.9 %all-to-all-done = f32[128,1,1024]{2,1,0:T(1,128)S(1)} async-done(((f32[128,1,1024]{2,1,0:T(1,128)}), f32[128,1,1024]{2,1,0:T(1,128)S(1)}, u32[]{:S(2)}, u32[]{:S(2)}) %all-to-all-start) | async-done | bytes 524320 | tf_op jit(solution)/shard_map/all_to_all | solution.py:576
  24.3 1.0 %collective-permute-start.4 = (f32[3,32,128]{2,1,0:T(8,128)S(1)}, f32[3,32,128]{2,1,0:T(8,128)S(1)}, u32[]{:S(2)}, u32[]{:S(2)}) collective-permute-start(f32[3,32,128]{2,1,0:T(8,128)S(1)} %get-tuple-element.38), channel_id=1, source_target_pairs={{0,8},{8,0},{16,24},{24,16},{32,40},{40,32},{48,56},{56,48},{64,72... | collective-permute-start | bytes 147464 | tf_op jit(solution)/shard_map/ppermute | solution.py:582
  25.2 1.0 %shard_map.30.refs_0_ = f32[4,3,4,4,8,128]{5,4,3,2,1,0:T(8,128)S(1)} custom-call(f32[4,3,4,4,8,128]{5,4,3,2,1,0:T(8,128)S(1)} %bitcast.10, f32[3,128,128]{2,1,0:T(8,128)S(1)} %get-tuple-element.32.speed), custom_call_target="tpu_custom_call" | custom-call | flops 10000000 | bytes 2097152 | tf_op jit(solution)/shard_map/pallas_call | solution.py:515
  26.2 3.5 %collective-permute-done.refs_1_.refs_3_.refs_9_ = f32[4,6,8,128]{3,2,1,0:T(8,128)S(1)} collective-permute-done((f32[4,6,8,128]{3,2,1,0:T(8,128)S(1)}, f32[4,6,8,128]{3,2,1,0:T(8,128)S(1)}, u32[]{:S(2)}, u32[]{:S(2)}) %collective-permute-start) | collective-permute-done | bytes 98336 | tf_op jit(solution)/shard_map/ppermute | solution.py:540
  29.7 0.7 %collective-permute-done.1.refs_2_.refs_4_.refs_10_ = f32[4,12,8,128]{3,2,1,0:T(8,128)S(1)} collective-permute-done((f32[4,12,8,128]{3,2,1,0:T(8,128)S(1)}, f32[4,12,8,128]{3,2,1,0:T(8,128)S(1)}, u32[]{:S(2)}, u32[]{:S(2)}) %collective-permute-start.1) | collective-permute-done | bytes 196640 | tf_op jit(solution)/shard_map/ppermute | solution.py:540
  30.6 0.6 collective-permute-start.5
  31.2 4.8 %collective-permute-start.6 = (f32[4,10,8,128]{3,2,1,0:T(8,128)S(1)}, f32[4,10,8,128]{3,2,1,0:T(8,128)S(1)}, u32[]{:S(2)}, u32[]{:S(2)}) collective-permute-start(f32[4,10,8,128]{3,2,1,0:T(8,128)S(1)} %get-tuple-element.41), channel_id=1, source_target_pairs={{8,16},{16,8},{24,32},{32,24},{40,48},{48,40},{56,64},{64,56},{72,... | collective-permute-start | bytes 491528 | tf_op jit(solution)/shard_map/ppermute | solution.py:540
  36.0 1.9 %collective-permute-start.7 = (f32[4,5,8,128]{3,2,1,0:T(8,128)S(1)}, f32[4,5,8,128]{3,2,1,0:T(8,128)S(1)}, u32[]{:S(2)}, u32[]{:S(2)}) collective-permute-start(f32[4,5,8,128]{3,2,1,0:T(8,128)S(1)} %get-tuple-element.42), channel_id=1, source_target_pairs={{1,2},{2,1},{3,4},{4,3},{5,6},{6,5},{9,10},{10,9},{11,12},{12,11},... | collective-permute-start | bytes 245768 | tf_op jit(solution)/shard_map/ppermute | solution.py:540
  38.0 1.0 %shard_map.33.refs_0_ = f32[4,3,4,4,8,128]{5,4,3,2,1,0:T(8,128)S(1)} custom-call(f32[4,3,4,4,8,128]{5,4,3,2,1,0:T(8,128)S(1)} %get-tuple-element.39.state.refs_0_, f32[4,3,4,4,8,128]{5,4,3,2,1,0:T(8,128)S(1)} %bitcast.11, f32[3,128,128]{2,1,0:T(8,128)S(1)} %get-tuple-element.32.speed), custom_call_target="tpu_custom_call" | custom-call | flops 10000000 | bytes 2097152 | tf_op jit(solution)/shard_map/pallas_call | solution.py:515
  39.0 0.4 shard_map.36
  39.5 1.5 %collective-permute-done.6.arrived = f32[4,10,8,128]{3,2,1,0:T(8,128)S(1)} collective-permute-done((f32[4,10,8,128]{3,2,1,0:T(8,128)S(1)}, f32[4,10,8,128]{3,2,1,0:T(8,128)S(1)}, u32[]{:S(2)}, u32[]{:S(2)}) %collective-permute-start.6) | collective-permute-done | bytes 163872 | tf_op jit(solution)/shard_map/ppermute | solution.py:540
  41.0 1.1 %collective-permute-done.7.refs_3_.refs_5_ = f32[4,5,8,128]{3,2,1,0:T(8,128)S(1)} collective-permute-done((f32[4,5,8,128]{3,2,1,0:T(8,128)S(1)}, f32[4,5,8,128]{3,2,1,0:T(8,128)S(1)}, u32[]{:S(2)}, u32[]{:S(2)}) %collective-permute-start.7) | collective-permute-done | bytes 81952 | tf_op jit(solution)/shard_map/ppermute | solution.py:540
  42.1 0.3 shard_map.37
  42.3 0.8 %collective-permute-start.9 = (f32[4,5,8,128]{3,2,1,0:T(8,128)S(1)}, f32[4,5,8,128]{3,2,1,0:T(8,128)S(1)}, u32[]{:S(2)}, u32[]{:S(2)}) collective-permute-start(f32[4,5,8,128]{3,2,1,0:T(8,128)S(1)} %get-tuple-element.48), channel_id=1, source_target_pairs={{0,1},{1,0},{2,3},{3,2},{4,5},{5,4},{6,7},{7,6},{8,9},{9,8},{10,11... | collective-permute-start | bytes 245768 | tf_op jit(solution)/shard_map/ppermute | solution.py:540
  43.1 4.6 %collective-permute-start.10 = (f32[4,10,8,128]{3,2,1,0:T(8,128)S(1)}, f32[4,10,8,128]{3,2,1,0:T(8,128)S(1)}, u32[]{:S(2)}, u32[]{:S(2)}) collective-permute-start(f32[4,10,8,128]{3,2,1,0:T(8,128)S(1)} %get-tuple-element.49), channel_id=1, source_target_pairs={{8,16},{16,8},{24,32},{32,24},{40,48},{48,40},{56,64},{64,56},{72,... | collective-permute-start | bytes 491528 | tf_op jit(solution)/shard_map/ppermute | solution.py:540
  47.7 2.7 %collective-permute-start.11 = (f32[4,5,8,128]{3,2,1,0:T(8,128)S(1)}, f32[4,5,8,128]{3,2,1,0:T(8,128)S(1)}, u32[]{:S(2)}, u32[]{:S(2)}) collective-permute-start(f32[4,5,8,128]{3,2,1,0:T(8,128)S(1)} %get-tuple-element.50), channel_id=1, source_target_pairs={{1,2},{2,1},{3,4},{4,3},{5,6},{6,5},{9,10},{10,9},{11,12},{12,11},... | collective-permute-start | bytes 245768 | tf_op jit(solution)/shard_map/ppermute | solution.py:540
  50.5 1.0 %shard_map.38.refs_0_ = f32[4,3,4,4,8,128]{5,4,3,2,1,0:T(8,128)S(1)} custom-call(f32[4,3,4,4,8,128]{5,4,3,2,1,0:T(8,128)S(1)} %get-tuple-element.47.state.start, f32[3,128,128]{2,1,0:T(8,128)S(1)} %get-tuple-element.46.refs_9_.speed.refs_7_), custom_call_target="tpu_custom_call" | custom-call | flops 10000000 | bytes 2097152 | tf_op jit(solution)/shard_map/pallas_call | solution.py:515
  51.5 0.4 shard_map.41
  51.9 0.8 %collective-permute-done.10.arrived = f32[4,10,8,128]{3,2,1,0:T(8,128)S(1)} collective-permute-done((f32[4,10,8,128]{3,2,1,0:T(8,128)S(1)}, f32[4,10,8,128]{3,2,1,0:T(8,128)S(1)}, u32[]{:S(2)}, u32[]{:S(2)}) %collective-permute-start.10) | collective-permute-done | bytes 163872 | tf_op jit(solution)/shard_map/ppermute | solution.py:540
  52.7 1.0 %collective-permute-done.11.refs_3_ = f32[4,5,8,128]{3,2,1,0:T(8,128)S(1)} collective-permute-done((f32[4,5,8,128]{3,2,1,0:T(8,128)S(1)}, f32[4,5,8,128]{3,2,1,0:T(8,128)S(1)}, u32[]{:S(2)}, u32[]{:S(2)}) %collective-permute-start.11) | collective-permute-done | bytes 81952 | tf_op jit(solution)/shard_map/ppermute | solution.py:540
  54.0 1.6 %collective-permute-start.13 = (f32[4,6,8,128]{3,2,1,0:T(8,128)S(1)}, f32[4,6,8,128]{3,2,1,0:T(8,128)S(1)}, u32[]{:S(2)}, u32[]{:S(2)}) collective-permute-start(f32[4,6,8,128]{3,2,1,0:T(8,128)S(1)} %get-tuple-element.55), channel_id=1, source_target_pairs={{0,1},{1,0},{2,3},{3,2},{4,5},{5,4},{6,7},{7,6},{8,9},{9,8},{10,11... | collective-permute-start | bytes 294920 | tf_op jit(solution)/shard_map/ppermute | solution.py:540
  55.6 3.8 %collective-permute-start.14 = (f32[4,12,8,128]{3,2,1,0:T(8,128)S(1)}, f32[4,12,8,128]{3,2,1,0:T(8,128)S(1)}, u32[]{:S(2)}, u32[]{:S(2)}) collective-permute-start(f32[4,12,8,128]{3,2,1,0:T(8,128)S(1)} %get-tuple-element.56), channel_id=1, source_target_pairs={{8,16},{16,8},{24,32},{32,24},{40,48},{48,40},{56,64},{64,56},{72,... | collective-permute-start | bytes 589832 | tf_op jit(solution)/shard_map/ppermute | solution.py:540
  59.4 1.9 %collective-permute-start.15 = (f32[4,6,8,128]{3,2,1,0:T(8,128)S(1)}, f32[4,6,8,128]{3,2,1,0:T(8,128)S(1)}, u32[]{:S(2)}, u32[]{:S(2)}) collective-permute-start(f32[4,6,8,128]{3,2,1,0:T(8,128)S(1)} %get-tuple-element.57), channel_id=1, source_target_pairs={{1,2},{2,1},{3,4},{4,3},{5,6},{6,5},{9,10},{10,9},{11,12},{12,11},... | collective-permute-start | bytes 294920 | tf_op jit(solution)/shard_map/ppermute | solution.py:540
  61.4 1.0 %shard_map.43.refs_0_ = f32[4,3,4,4,8,128]{5,4,3,2,1,0:T(8,128)S(1)} custom-call(f32[4,3,4,4,8,128]{5,4,3,2,1,0:T(8,128)S(1)} %get-tuple-element.54.state, f32[4,3,4,4,8,128]{5,4,3,2,1,0:T(8,128)S(1)} %get-tuple-element.47.state.start, f32[3,128,128]{2,1,0:T(8,128)S(1)} %get-tuple-element.46.refs_9_.speed.refs_7_), custom_call_target="tpu_custom_call" | custom-call | flops 10000000 | bytes 2097152 | tf_op jit(solution)/shard_map/pallas_call | solution.py:515
  62.5 5.2 %collective-permute-done.14.arrived = f32[4,12,8,128]{3,2,1,0:T(8,128)S(1)} collective-permute-done((f32[4,12,8,128]{3,2,1,0:T(8,128)S(1)}, f32[4,12,8,128]{3,2,1,0:T(8,128)S(1)}, u32[]{:S(2)}, u32[]{:S(2)}) %collective-permute-start.14) | collective-permute-done | bytes 196640 | tf_op jit(solution)/shard_map/ppermute | solution.py:540
  67.7 1.0 %shard_map.46 = f32[4,3,4,4,8,128]{5,4,3,2,1,0:T(8,128)} custom-call(f32[4,3,4,4,8,128]{5,4,3,2,1,0:T(8,128)S(1)} %shard_map.43.refs_0_, f32[4,6,8,128]{3,2,1,0:T(8,128)S(1)} %shard_map.44.refs_0_.refs_1_, f32[4,12,8,128]{3,2,1,0:T(8,128)S(1)} %shard_map.45.refs_2_, f32[4,6,8,128]{3,2,1,0:T(8,128)S(1)} %collective-permute-done.15.refs_3_, ...), custom_call_target="tpu_custom_call" | custom-call | flops 1000000 | bytes 2097152 | tf_op jit(solution)/shard_map/pallas_call | solution.py:515
  (27 shorter events, 1.3 us)
Async XLA Ops:
  0.0 1.1 %copy-start.1 = (f32[2,3,64,1,16,16]{2,5,4,3,1,0:T(8,128)S(1)}, f32[2,3,64,1,16,16]{2,5,4,3,1,0:T(8,128)}, u32[]{:S(2)}) copy-start(f32[2,3,64,1,16,16]{2,5,4,3,1,0:T(8,128)} %param.3) | copy-start | bytes 1179652
  2.5 10.7 %copy-start = (f32[4,3,64,1,2,128]{5,4,3,2,1,0:T(2,128)S(1)}, f32[4,3,64,1,2,128]{5,4,3,2,1,0:T(2,128)}, u32[]{:S(2)}) copy-start(f32[4,3,64,1,2,128]{5,4,3,2,1,0:T(2,128)} %param.2) | copy-start | bytes 2359300
  2.5 21.5 %all-to-all-start = ((f32[128,1,1024]{2,1,0:T(1,128)}), f32[128,1,1024]{2,1,0:T(1,128)S(1)}, u32[]{:S(2)}, u32[]{:S(2)}) async-start(f32[128,1,1024]{2,1,0:T(1,128)} %bitcast.3), calls=%async_computation | async-start | bytes 1048576 | tf_op jit(solution)/shard_map/all_to_all | solution.py:576
  13.3 17.0 %collective-permute-start.1 = (f32[4,12,8,128]{3,2,1,0:T(8,128)S(1)}, f32[4,12,8,128]{3,2,1,0:T(8,128)S(1)}, u32[]{:S(2)}, u32[]{:S(2)}) collective-permute-start(f32[4,12,8,128]{3,2,1,0:T(8,128)S(1)} %get-tuple-element.34), channel_id=1, source_target_pairs={{8,16},{16,8},{24,32},{32,24},{40,48},{48,40},{56,64},{64,56},{72,... | collective-permute-start | bytes 589832 | tf_op jit(solution)/shard_map/ppermute | solution.py:540
  18.7 11.7 %collective-permute-start.3 = (f32[4,12,8,128]{3,2,1,0:T(8,128)S(1)}, f32[4,12,8,128]{3,2,1,0:T(8,128)S(1)}, u32[]{:S(2)}, u32[]{:S(2)}) collective-permute-start(f32[4,12,8,128]{3,2,1,0:T(8,128)S(1)} %get-tuple-element.36), channel_id=1, source_target_pairs={{0,8},{8,0},{16,24},{24,16},{32,40},{40,32},{48,56},{56,48},{64,72... | collective-permute-start | bytes 589832 | tf_op jit(solution)/shard_map/ppermute | solution.py:540
  18.9 10.8 %collective-permute-start = (f32[4,6,8,128]{3,2,1,0:T(8,128)S(1)}, f32[4,6,8,128]{3,2,1,0:T(8,128)S(1)}, u32[]{:S(2)}, u32[]{:S(2)}) collective-permute-start(f32[4,6,8,128]{3,2,1,0:T(8,128)S(1)} %get-tuple-element.33), channel_id=1, source_target_pairs={{0,1},{1,0},{2,3},{3,2},{4,5},{5,4},{6,7},{7,6},{8,9},{9,8},{10,11... | collective-permute-start | bytes 294920 | tf_op jit(solution)/shard_map/ppermute | solution.py:540
  19.4 10.3 %collective-permute-start.2 = (f32[4,6,8,128]{3,2,1,0:T(8,128)S(1)}, f32[4,6,8,128]{3,2,1,0:T(8,128)S(1)}, u32[]{:S(2)}, u32[]{:S(2)}) collective-permute-start(f32[4,6,8,128]{3,2,1,0:T(8,128)S(1)} %get-tuple-element.35), channel_id=1, source_target_pairs={{1,2},{2,1},{3,4},{4,3},{5,6},{6,5},{9,10},{10,9},{11,12},{12,11},... | collective-permute-start | bytes 294920 | tf_op jit(solution)/shard_map/ppermute | solution.py:540
  24.3 6.1 %collective-permute-start.4 = (f32[3,32,128]{2,1,0:T(8,128)S(1)}, f32[3,32,128]{2,1,0:T(8,128)S(1)}, u32[]{:S(2)}, u32[]{:S(2)}) collective-permute-start(f32[3,32,128]{2,1,0:T(8,128)S(1)} %get-tuple-element.38), channel_id=1, source_target_pairs={{0,8},{8,0},{16,24},{24,16},{32,40},{40,32},{48,56},{56,48},{64,72... | collective-permute-start | bytes 147464 | tf_op jit(solution)/shard_map/ppermute | solution.py:582
  30.6 8.8 %collective-permute-start.5 = (f32[4,5,8,128]{3,2,1,0:T(8,128)S(1)}, f32[4,5,8,128]{3,2,1,0:T(8,128)S(1)}, u32[]{:S(2)}, u32[]{:S(2)}) collective-permute-start(f32[4,5,8,128]{3,2,1,0:T(8,128)S(1)} %get-tuple-element.40), channel_id=1, source_target_pairs={{0,1},{1,0},{2,3},{3,2},{4,5},{5,4},{6,7},{7,6},{8,9},{9,8},{10,11... | collective-permute-start | bytes 245768 | tf_op jit(solution)/shard_map/ppermute | solution.py:540
  31.2 9.8 %collective-permute-start.6 = (f32[4,10,8,128]{3,2,1,0:T(8,128)S(1)}, f32[4,10,8,128]{3,2,1,0:T(8,128)S(1)}, u32[]{:S(2)}, u32[]{:S(2)}) collective-permute-start(f32[4,10,8,128]{3,2,1,0:T(8,128)S(1)} %get-tuple-element.41), channel_id=1, source_target_pairs={{8,16},{16,8},{24,32},{32,24},{40,48},{48,40},{56,64},{64,56},{72,... | collective-permute-start | bytes 491528 | tf_op jit(solution)/shard_map/ppermute | solution.py:540
  36.0 6.1 %collective-permute-start.7 = (f32[4,5,8,128]{3,2,1,0:T(8,128)S(1)}, f32[4,5,8,128]{3,2,1,0:T(8,128)S(1)}, u32[]{:S(2)}, u32[]{:S(2)}) collective-permute-start(f32[4,5,8,128]{3,2,1,0:T(8,128)S(1)} %get-tuple-element.42), channel_id=1, source_target_pairs={{1,2},{2,1},{3,4},{4,3},{5,6},{6,5},{9,10},{10,9},{11,12},{12,11},... | collective-permute-start | bytes 245768 | tf_op jit(solution)/shard_map/ppermute | solution.py:540
  37.9 4.2 %collective-permute-start.8 = (f32[4,10,8,128]{3,2,1,0:T(8,128)S(1)}, f32[4,10,8,128]{3,2,1,0:T(8,128)S(1)}, u32[]{:S(2)}, u32[]{:S(2)}) collective-permute-start(f32[4,10,8,128]{3,2,1,0:T(8,128)S(1)} %get-tuple-element.43), channel_id=1, source_target_pairs={{0,8},{8,0},{16,24},{24,16},{32,40},{40,32},{48,56},{56,48},{64,72... | collective-permute-start | bytes 491528 | tf_op jit(solution)/shard_map/ppermute | solution.py:540
  42.3 9.6 %collective-permute-start.9 = (f32[4,5,8,128]{3,2,1,0:T(8,128)S(1)}, f32[4,5,8,128]{3,2,1,0:T(8,128)S(1)}, u32[]{:S(2)}, u32[]{:S(2)}) collective-permute-start(f32[4,5,8,128]{3,2,1,0:T(8,128)S(1)} %get-tuple-element.48), channel_id=1, source_target_pairs={{0,1},{1,0},{2,3},{3,2},{4,5},{5,4},{6,7},{7,6},{8,9},{9,8},{10,11... | collective-permute-start | bytes 245768 | tf_op jit(solution)/shard_map/ppermute | solution.py:540
  43.1 9.6 %collective-permute-start.10 = (f32[4,10,8,128]{3,2,1,0:T(8,128)S(1)}, f32[4,10,8,128]{3,2,1,0:T(8,128)S(1)}, u32[]{:S(2)}, u32[]{:S(2)}) collective-permute-start(f32[4,10,8,128]{3,2,1,0:T(8,128)S(1)} %get-tuple-element.49), channel_id=1, source_target_pairs={{8,16},{16,8},{24,32},{32,24},{40,48},{48,40},{56,64},{64,56},{72,... | collective-permute-start | bytes 491528 | tf_op jit(solution)/shard_map/ppermute | solution.py:540
  47.7 6.1 %collective-permute-start.11 = (f32[4,5,8,128]{3,2,1,0:T(8,128)S(1)}, f32[4,5,8,128]{3,2,1,0:T(8,128)S(1)}, u32[]{:S(2)}, u32[]{:S(2)}) collective-permute-start(f32[4,5,8,128]{3,2,1,0:T(8,128)S(1)} %get-tuple-element.50), channel_id=1, source_target_pairs={{1,2},{2,1},{3,4},{4,3},{5,6},{6,5},{9,10},{10,9},{11,12},{12,11},... | collective-permute-start | bytes 245768 | tf_op jit(solution)/shard_map/ppermute | solution.py:540
  50.4 3.3 %collective-permute-start.12 = (f32[4,10,8,128]{3,2,1,0:T(8,128)S(1)}, f32[4,10,8,128]{3,2,1,0:T(8,128)S(1)}, u32[]{:S(2)}, u32[]{:S(2)}) collective-permute-start(f32[4,10,8,128]{3,2,1,0:T(8,128)S(1)} %get-tuple-element.51), channel_id=1, source_target_pairs={{0,8},{8,0},{16,24},{24,16},{32,40},{40,32},{48,56},{56,48},{64,72... | collective-permute-start | bytes 491528 | tf_op jit(solution)/shard_map/ppermute | solution.py:540
  54.0 8.5 %collective-permute-start.13 = (f32[4,6,8,128]{3,2,1,0:T(8,128)S(1)}, f32[4,6,8,128]{3,2,1,0:T(8,128)S(1)}, u32[]{:S(2)}, u32[]{:S(2)}) collective-permute-start(f32[4,6,8,128]{3,2,1,0:T(8,128)S(1)} %get-tuple-element.55), channel_id=1, source_target_pairs={{0,1},{1,0},{2,3},{3,2},{4,5},{5,4},{6,7},{7,6},{8,9},{9,8},{10,11... | collective-permute-start | bytes 294920 | tf_op jit(solution)/shard_map/ppermute | solution.py:540
  55.6 12.1 %collective-permute-start.14 = (f32[4,12,8,128]{3,2,1,0:T(8,128)S(1)}, f32[4,12,8,128]{3,2,1,0:T(8,128)S(1)}, u32[]{:S(2)}, u32[]{:S(2)}) collective-permute-start(f32[4,12,8,128]{3,2,1,0:T(8,128)S(1)} %get-tuple-element.56), channel_id=1, source_target_pairs={{8,16},{16,8},{24,32},{32,24},{40,48},{48,40},{56,64},{64,56},{72,... | collective-permute-start | bytes 589832 | tf_op jit(solution)/shard_map/ppermute | solution.py:540
  59.4 8.3 %collective-permute-start.15 = (f32[4,6,8,128]{3,2,1,0:T(8,128)S(1)}, f32[4,6,8,128]{3,2,1,0:T(8,128)S(1)}, u32[]{:S(2)}, u32[]{:S(2)}) collective-permute-start(f32[4,6,8,128]{3,2,1,0:T(8,128)S(1)} %get-tuple-element.57), channel_id=1, source_target_pairs={{1,2},{2,1},{3,4},{4,3},{5,6},{6,5},{9,10},{10,9},{11,12},{12,11},... | collective-permute-start | bytes 294920 | tf_op jit(solution)/shard_map/ppermute | solution.py:540
  61.3 6.3 %collective-permute-start.16 = (f32[4,12,8,128]{3,2,1,0:T(8,128)S(1)}, f32[4,12,8,128]{3,2,1,0:T(8,128)S(1)}, u32[]{:S(2)}, u32[]{:S(2)}) collective-permute-start(f32[4,12,8,128]{3,2,1,0:T(8,128)S(1)} %get-tuple-element.58), channel_id=1, source_target_pairs={{0,8},{8,0},{16,24},{24,16},{32,40},{40,32},{48,56},{56,48},{64,72... | collective-permute-start | bytes 589832 | tf_op jit(solution)/shard_map/ppermute | solution.py:540

commit v6 on v3

--- a/solution.py
+++ b/solution.py
@@ -456,7 +456,7 @@
         inside(k, state, now, before, ghost_speed, inner_x, inner_y, coef)
         return carry
 
-    lax.fori_loop(0, KRYLOV, step, 0)
+    lax.fori_loop(0, KRYLOV, step, 0, unroll=True)
 
 
 def finish_kernel(coef, form, has_ghosts, next_form, next_speed, *refs):
@@ -479,7 +479,7 @@
             send_faces(k, next_form, out, speed, px, py, *leaving)
         return carry
 
-    lax.fori_loop(0, KRYLOV, step, 0)
+    lax.fori_loop(0, KRYLOV, step, 0, unroll=True)
 
 
 STATE = (KRYLOV, 3, SIDE, SIDE, 8, LANES)

time: 68.9 us -> 68.7 us (level)
  transfers between devices with their start and end apart: 17 -> 17, of which waited for: 8 -> 9; matrix products, arithmetic and copies ran while one was open for 0% -> 0% of each run, Pallas kernels for 8% -> 7%
where the time goes in v6:
time: 68.7 us; the launch traced here: 68.3 us
  starting transfers between devices  42.5 us (62%)
  waiting for transfers between devices  16.9 us (25%)
  Pallas kernels  7.55 us (11%)
  local copies, waits for them, and re-layouts  1.14 us (2%)
    ppermute x16, starting transfers between devices, exchange(): received.append(lax.ppermute(face, axis, pairs))  31.8 us
    ppermute x16, waiting for transfers between devices, exchange(): received.append(lax.ppermute(face, axis, pairs))  14.3 us
    all_to_all x1, starting transfers between devices, shards(): lax.all_to_all(packed, ('gx', 'gy'), split_axis=0, concat_axis=0, tiled=T...  10.7 us
    pallas_call x13, Pallas kernels, call(): pl.pallas_call(kernel, out_shape=[jax.ShapeDtypeStruct(shape, F32) for sh...  7.49 us
    all_to_all x1, waiting for transfers between devices, shards(): lax.all_to_all(packed, ('gx', 'gy'), split_axis=0, concat_axis=0, tiled=T...  2.62 us
  transfers between devices with their start and end apart: 17, of which 9 were waited for; matrix products, arithmetic and copies ran while one was open for 0% of the time, Pallas kernels for 7%

profile of v6, /device:TPU:13, one launch (start us, length us, event | category | flops | bytes accessed | tf_op | source)
XLA Modules:
  0.0 68.3 jit_solution(12316823535745144277)
XLA Ops:
  0.0 1.1 %copy-done.1 = f32[2,3,64,1,16,16]{2,5,4,3,1,0:T(8,128)S(1)} copy-done((f32[2,3,64,1,16,16]{2,5,4,3,1,0:T(8,128)S(1)}, f32[2,3,64,1,16,16]{2,5,4,3,1,0:T(8,128)}, u32[]{:S(2)}) %copy-start.1) | copy-done | bytes 393240
  1.1 1.2 %shard_map.28 = f32[1152,128]{1,0:T(8,128)} custom-call(f32[6,16,16,64]{3,2,1,0:T(8,128)S(1)} %bitcast.14), custom_call_target="tpu_custom_call" | custom-call | flops 1000000 | bytes 2097152 | tf_op jit(solution)/shard_map/pallas_call | solution.py:493
  2.3 10.7 %all-to-all-start = ((f32[128,1,1152]{2,1,0:T(1,128)}), f32[128,1,1152]{2,1,0:T(1,128)S(1)}, u32[]{:S(2)}, u32[]{:S(2)}) async-start(f32[128,1,1152]{2,1,0:T(1,128)} %bitcast.3), calls=%async_computation | async-start | bytes 1179648 | tf_op jit(solution)/shard_map/all_to_all | solution.py:554
  13.1 5.3 %collective-permute-start.1 = (f32[4,12,8,128]{3,2,1,0:T(8,128)S(1)}, f32[4,12,8,128]{3,2,1,0:T(8,128)S(1)}, u32[]{:S(2)}, u32[]{:S(2)}) collective-permute-start(f32[4,12,8,128]{3,2,1,0:T(8,128)S(1)} %get-tuple-element.33), channel_id=1, source_target_pairs={{8,16},{16,8},{24,32},{32,24},{40,48},{48,40},{56,64},{64,56},{72,... | collective-permute-start | bytes 589832 | tf_op jit(solution)/shard_map/ppermute | solution.py:518
  18.5 0.2 collective-permute-start.3
  18.7 0.6 collective-permute-start
  19.2 2.7 %collective-permute-start.2 = (f32[4,6,8,128]{3,2,1,0:T(8,128)S(1)}, f32[4,6,8,128]{3,2,1,0:T(8,128)S(1)}, u32[]{:S(2)}, u32[]{:S(2)}) collective-permute-start(f32[4,6,8,128]{3,2,1,0:T(8,128)S(1)} %get-tuple-element.34), channel_id=1, source_target_pairs={{1,2},{2,1},{3,4},{4,3},{5,6},{6,5},{9,10},{10,9},{11,12},{12,11},... | collective-permute-start | bytes 294920 | tf_op jit(solution)/shard_map/ppermute | solution.py:518
  22.0 2.6 %all-to-all-done = f32[128,1,1152]{2,1,0:T(1,128)S(1)} async-done(((f32[128,1,1152]{2,1,0:T(1,128)}), f32[128,1,1152]{2,1,0:T(1,128)S(1)}, u32[]{:S(2)}, u32[]{:S(2)}) %all-to-all-start) | async-done | bytes 589856 | tf_op jit(solution)/shard_map/all_to_all | solution.py:554
  24.6 0.2 shard_map.29
  24.8 1.0 %shard_map.30.refs_0_ = f32[4,3,4,4,8,128]{5,4,3,2,1,0:T(8,128)S(1)} custom-call(f32[4,3,4,4,8,128]{5,4,3,2,1,0:T(8,128)S(1)} %bitcast.10, f32[3,128,128]{2,1,0:T(8,128)S(1)} %get-tuple-element.31.speed), custom_call_target="tpu_custom_call" | custom-call | flops 10000000 | bytes 2097152 | tf_op jit(solution)/shard_map/pallas_call | solution.py:493
  25.8 4.3 %collective-permute-done.refs_1_.refs_2_.refs_8_ = f32[4,6,8,128]{3,2,1,0:T(8,128)S(1)} collective-permute-done((f32[4,6,8,128]{3,2,1,0:T(8,128)S(1)}, f32[4,6,8,128]{3,2,1,0:T(8,128)S(1)}, u32[]{:S(2)}, u32[]{:S(2)}) %collective-permute-start) | collective-permute-done | bytes 98336 | tf_op jit(solution)/shard_map/ppermute | solution.py:518
  30.1 0.7 %collective-permute-done.1.refs_2_.refs_3_.refs_9_ = f32[4,12,8,128]{3,2,1,0:T(8,128)S(1)} collective-permute-done((f32[4,12,8,128]{3,2,1,0:T(8,128)S(1)}, f32[4,12,8,128]{3,2,1,0:T(8,128)S(1)}, u32[]{:S(2)}, u32[]{:S(2)}) %collective-permute-start.1) | collective-permute-done | bytes 196640 | tf_op jit(solution)/shard_map/ppermute | solution.py:518
  31.0 0.5 collective-permute-start.4
  31.5 4.9 %collective-permute-start.5 = (f32[4,10,8,128]{3,2,1,0:T(8,128)S(1)}, f32[4,10,8,128]{3,2,1,0:T(8,128)S(1)}, u32[]{:S(2)}, u32[]{:S(2)}) collective-permute-start(f32[4,10,8,128]{3,2,1,0:T(8,128)S(1)} %get-tuple-element.39), channel_id=1, source_target_pairs={{8,16},{16,8},{24,32},{32,24},{40,48},{48,40},{56,64},{64,56},{72,... | collective-permute-start | bytes 491528 | tf_op jit(solution)/shard_map/ppermute | solution.py:518
  36.4 1.9 %collective-permute-start.6 = (f32[4,5,8,128]{3,2,1,0:T(8,128)S(1)}, f32[4,5,8,128]{3,2,1,0:T(8,128)S(1)}, u32[]{:S(2)}, u32[]{:S(2)}) collective-permute-start(f32[4,5,8,128]{3,2,1,0:T(8,128)S(1)} %get-tuple-element.40), channel_id=1, source_target_pairs={{1,2},{2,1},{3,4},{4,3},{5,6},{6,5},{9,10},{10,9},{11,12},{12,11},... | collective-permute-start | bytes 245768 | tf_op jit(solution)/shard_map/ppermute | solution.py:518
  38.4 1.0 %shard_map.33.refs_0_ = f32[4,3,4,4,8,128]{5,4,3,2,1,0:T(8,128)S(1)} custom-call(f32[4,3,4,4,8,128]{5,4,3,2,1,0:T(8,128)S(1)} %get-tuple-element.37.state.refs_0_, f32[4,3,4,4,8,128]{5,4,3,2,1,0:T(8,128)S(1)} %bitcast.11, f32[3,128,128]{2,1,0:T(8,128)S(1)} %get-tuple-element.31.speed), custom_call_target="tpu_custom_call" | custom-call | flops 10000000 | bytes 2097152 | tf_op jit(solution)/shard_map/pallas_call | solution.py:493
  39.7 1.3 %collective-permute-done.5.arrived = f32[4,10,8,128]{3,2,1,0:T(8,128)S(1)} collective-permute-done((f32[4,10,8,128]{3,2,1,0:T(8,128)S(1)}, f32[4,10,8,128]{3,2,1,0:T(8,128)S(1)}, u32[]{:S(2)}, u32[]{:S(2)}) %collective-permute-start.5) | collective-permute-done | bytes 163872 | tf_op jit(solution)/shard_map/ppermute | solution.py:518
  41.0 1.5 %collective-permute-done.6.refs_3_.refs_4_ = f32[4,5,8,128]{3,2,1,0:T(8,128)S(1)} collective-permute-done((f32[4,5,8,128]{3,2,1,0:T(8,128)S(1)}, f32[4,5,8,128]{3,2,1,0:T(8,128)S(1)}, u32[]{:S(2)}, u32[]{:S(2)}) %collective-permute-start.6) | collective-permute-done | bytes 81952 | tf_op jit(solution)/shard_map/ppermute | solution.py:518
  42.5 0.2 shard_map.37
  42.7 0.7 %collective-permute-start.8 = (f32[4,5,8,128]{3,2,1,0:T(8,128)S(1)}, f32[4,5,8,128]{3,2,1,0:T(8,128)S(1)}, u32[]{:S(2)}, u32[]{:S(2)}) collective-permute-start(f32[4,5,8,128]{3,2,1,0:T(8,128)S(1)} %get-tuple-element.46), channel_id=1, source_target_pairs={{0,1},{1,0},{2,3},{3,2},{4,5},{5,4},{6,7},{7,6},{8,9},{9,8},{10,11... | collective-permute-start | bytes 245768 | tf_op jit(solution)/shard_map/ppermute | solution.py:518
  43.4 4.6 %collective-permute-start.9 = (f32[4,10,8,128]{3,2,1,0:T(8,128)S(1)}, f32[4,10,8,128]{3,2,1,0:T(8,128)S(1)}, u32[]{:S(2)}, u32[]{:S(2)}) collective-permute-start(f32[4,10,8,128]{3,2,1,0:T(8,128)S(1)} %get-tuple-element.47), channel_id=1, source_target_pairs={{8,16},{16,8},{24,32},{32,24},{40,48},{48,40},{56,64},{64,56},{72,... | collective-permute-start | bytes 491528 | tf_op jit(solution)/shard_map/ppermute | solution.py:518
  48.1 2.7 %collective-permute-start.10 = (f32[4,5,8,128]{3,2,1,0:T(8,128)S(1)}, f32[4,5,8,128]{3,2,1,0:T(8,128)S(1)}, u32[]{:S(2)}, u32[]{:S(2)}) collective-permute-start(f32[4,5,8,128]{3,2,1,0:T(8,128)S(1)} %get-tuple-element.48), channel_id=1, source_target_pairs={{1,2},{2,1},{3,4},{4,3},{5,6},{6,5},{9,10},{10,9},{11,12},{12,11},... | collective-permute-start | bytes 245768 | tf_op jit(solution)/shard_map/ppermute | solution.py:518
  50.9 1.0 %shard_map.38.refs_0_ = f32[4,3,4,4,8,128]{5,4,3,2,1,0:T(8,128)S(1)} custom-call(f32[4,3,4,4,8,128]{5,4,3,2,1,0:T(8,128)S(1)} %get-tuple-element.45.state.start, f32[3,128,128]{2,1,0:T(8,128)S(1)} %get-tuple-element.44.refs_8_.speed.refs_7_), custom_call_target="tpu_custom_call" | custom-call | flops 10000000 | bytes 2097152 | tf_op jit(solution)/shard_map/pallas_call | solution.py:493
  51.8 0.2 shard_map.41
  52.1 0.8 %collective-permute-done.9.arrived = f32[4,10,8,128]{3,2,1,0:T(8,128)S(1)} collective-permute-done((f32[4,10,8,128]{3,2,1,0:T(8,128)S(1)}, f32[4,10,8,128]{3,2,1,0:T(8,128)S(1)}, u32[]{:S(2)}, u32[]{:S(2)}) %collective-permute-start.9) | collective-permute-done | bytes 163872 | tf_op jit(solution)/shard_map/ppermute | solution.py:518
  52.9 1.3 %collective-permute-done.10.refs_3_ = f32[4,5,8,128]{3,2,1,0:T(8,128)S(1)} collective-permute-done((f32[4,5,8,128]{3,2,1,0:T(8,128)S(1)}, f32[4,5,8,128]{3,2,1,0:T(8,128)S(1)}, u32[]{:S(2)}, u32[]{:S(2)}) %collective-permute-start.10) | collective-permute-done | bytes 81952 | tf_op jit(solution)/shard_map/ppermute | solution.py:518
  54.4 1.6 %collective-permute-start.12 = (f32[4,6,8,128]{3,2,1,0:T(8,128)S(1)}, f32[4,6,8,128]{3,2,1,0:T(8,128)S(1)}, u32[]{:S(2)}, u32[]{:S(2)}) collective-permute-start(f32[4,6,8,128]{3,2,1,0:T(8,128)S(1)} %get-tuple-element.53), channel_id=1, source_target_pairs={{0,1},{1,0},{2,3},{3,2},{4,5},{5,4},{6,7},{7,6},{8,9},{9,8},{10,11... | collective-permute-start | bytes 294920 | tf_op jit(solution)/shard_map/ppermute | solution.py:518
  56.0 3.9 %collective-permute-start.13 = (f32[4,12,8,128]{3,2,1,0:T(8,128)S(1)}, f32[4,12,8,128]{3,2,1,0:T(8,128)S(1)}, u32[]{:S(2)}, u32[]{:S(2)}) collective-permute-start(f32[4,12,8,128]{3,2,1,0:T(8,128)S(1)} %get-tuple-element.54), channel_id=1, source_target_pairs={{8,16},{16,8},{24,32},{32,24},{40,48},{48,40},{56,64},{64,56},{72,... | collective-permute-start | bytes 589832 | tf_op jit(solution)/shard_map/ppermute | solution.py:518
  59.9 1.9 %collective-permute-start.14 = (f32[4,6,8,128]{3,2,1,0:T(8,128)S(1)}, f32[4,6,8,128]{3,2,1,0:T(8,128)S(1)}, u32[]{:S(2)}, u32[]{:S(2)}) collective-permute-start(f32[4,6,8,128]{3,2,1,0:T(8,128)S(1)} %get-tuple-element.55), channel_id=1, source_target_pairs={{1,2},{2,1},{3,4},{4,3},{5,6},{6,5},{9,10},{10,9},{11,12},{12,11},... | collective-permute-start | bytes 294920 | tf_op jit(solution)/shard_map/ppermute | solution.py:518
  61.9 1.0 %shard_map.43.refs_0_ = f32[4,3,4,4,8,128]{5,4,3,2,1,0:T(8,128)S(1)} custom-call(f32[4,3,4,4,8,128]{5,4,3,2,1,0:T(8,128)S(1)} %get-tuple-element.52.state, f32[4,3,4,4,8,128]{5,4,3,2,1,0:T(8,128)S(1)} %get-tuple-element.45.state.start, f32[3,128,128]{2,1,0:T(8,128)S(1)} %get-tuple-element.44.refs_8_.speed.refs_7_), custom_call_target="tpu_custom_call" | custom-call | flops 10000000 | bytes 2097152 | tf_op jit(solution)/shard_map/pallas_call | solution.py:493
  62.9 4.3 %collective-permute-done.13.arrived = f32[4,12,8,128]{3,2,1,0:T(8,128)S(1)} collective-permute-done((f32[4,12,8,128]{3,2,1,0:T(8,128)S(1)}, f32[4,12,8,128]{3,2,1,0:T(8,128)S(1)}, u32[]{:S(2)}, u32[]{:S(2)}) %collective-permute-start.13) | collective-permute-done | bytes 196640 | tf_op jit(solution)/shard_map/ppermute | solution.py:518
  67.4 1.0 %shard_map.46 = f32[4,3,4,4,8,128]{5,4,3,2,1,0:T(8,128)} custom-call(f32[4,3,4,4,8,128]{5,4,3,2,1,0:T(8,128)S(1)} %shard_map.43.refs_0_, f32[4,6,8,128]{3,2,1,0:T(8,128)S(1)} %shard_map.44.refs_0_.refs_1_, f32[4,12,8,128]{3,2,1,0:T(8,128)S(1)} %shard_map.45.refs_2_, f32[4,6,8,128]{3,2,1,0:T(8,128)S(1)} %collective-permute-done.14.refs_3_, ...), custom_call_target="tpu_custom_call" | custom-call | flops 1000000 | bytes 2097152 | tf_op jit(solution)/shard_map/pallas_call | solution.py:493
  (25 shorter events, 1.1 us)
Async XLA Ops:
  0.0 1.1 %copy-start.1 = (f32[2,3,64,1,16,16]{2,5,4,3,1,0:T(8,128)S(1)}, f32[2,3,64,1,16,16]{2,5,4,3,1,0:T(8,128)}, u32[]{:S(2)}) copy-start(f32[2,3,64,1,16,16]{2,5,4,3,1,0:T(8,128)} %param.3) | copy-start | bytes 1179652
  2.3 10.7 %copy-start = (f32[4,3,64,1,2,128]{5,4,3,2,1,0:T(2,128)S(1)}, f32[4,3,64,1,2,128]{5,4,3,2,1,0:T(2,128)}, u32[]{:S(2)}) copy-start(f32[4,3,64,1,2,128]{5,4,3,2,1,0:T(2,128)} %param.2) | copy-start | bytes 2359300
  2.3 22.3 %all-to-all-start = ((f32[128,1,1152]{2,1,0:T(1,128)}), f32[128,1,1152]{2,1,0:T(1,128)S(1)}, u32[]{:S(2)}, u32[]{:S(2)}) async-start(f32[128,1,1152]{2,1,0:T(1,128)} %bitcast.3), calls=%async_computation | async-start | bytes 1179648 | tf_op jit(solution)/shard_map/all_to_all | solution.py:554
  13.1 17.7 %collective-permute-start.1 = (f32[4,12,8,128]{3,2,1,0:T(8,128)S(1)}, f32[4,12,8,128]{3,2,1,0:T(8,128)S(1)}, u32[]{:S(2)}, u32[]{:S(2)}) collective-permute-start(f32[4,12,8,128]{3,2,1,0:T(8,128)S(1)} %get-tuple-element.33), channel_id=1, source_target_pairs={{8,16},{16,8},{24,32},{32,24},{40,48},{48,40},{56,64},{64,56},{72,... | collective-permute-start | bytes 589832 | tf_op jit(solution)/shard_map/ppermute | solution.py:518
  18.5 12.4 %collective-permute-start.3 = (f32[4,12,8,128]{3,2,1,0:T(8,128)S(1)}, f32[4,12,8,128]{3,2,1,0:T(8,128)S(1)}, u32[]{:S(2)}, u32[]{:S(2)}) collective-permute-start(f32[4,12,8,128]{3,2,1,0:T(8,128)S(1)} %get-tuple-element.35), channel_id=1, source_target_pairs={{0,8},{8,0},{16,24},{24,16},{32,40},{40,32},{48,56},{56,48},{64,72... | collective-permute-start | bytes 589832 | tf_op jit(solution)/shard_map/ppermute | solution.py:518
  18.7 11.4 %collective-permute-start = (f32[4,6,8,128]{3,2,1,0:T(8,128)S(1)}, f32[4,6,8,128]{3,2,1,0:T(8,128)S(1)}, u32[]{:S(2)}, u32[]{:S(2)}) collective-permute-start(f32[4,6,8,128]{3,2,1,0:T(8,128)S(1)} %get-tuple-element.32), channel_id=1, source_target_pairs={{0,1},{1,0},{2,3},{3,2},{4,5},{5,4},{6,7},{7,6},{8,9},{9,8},{10,11... | collective-permute-start | bytes 294920 | tf_op jit(solution)/shard_map/ppermute | solution.py:518
  19.2 10.9 %collective-permute-start.2 = (f32[4,6,8,128]{3,2,1,0:T(8,128)S(1)}, f32[4,6,8,128]{3,2,1,0:T(8,128)S(1)}, u32[]{:S(2)}, u32[]{:S(2)}) collective-permute-start(f32[4,6,8,128]{3,2,1,0:T(8,128)S(1)} %get-tuple-element.34), channel_id=1, source_target_pairs={{1,2},{2,1},{3,4},{4,3},{5,6},{6,5},{9,10},{10,9},{11,12},{12,11},... | collective-permute-start | bytes 294920 | tf_op jit(solution)/shard_map/ppermute | solution.py:518
  31.0 8.6 %collective-permute-start.4 = (f32[4,5,8,128]{3,2,1,0:T(8,128)S(1)}, f32[4,5,8,128]{3,2,1,0:T(8,128)S(1)}, u32[]{:S(2)}, u32[]{:S(2)}) collective-permute-start(f32[4,5,8,128]{3,2,1,0:T(8,128)S(1)} %get-tuple-element.38), channel_id=1, source_target_pairs={{0,1},{1,0},{2,3},{3,2},{4,5},{5,4},{6,7},{7,6},{8,9},{9,8},{10,11... | collective-permute-start | bytes 245768 | tf_op jit(solution)/shard_map/ppermute | solution.py:518
  31.5 9.5 %collective-permute-start.5 = (f32[4,10,8,128]{3,2,1,0:T(8,128)S(1)}, f32[4,10,8,128]{3,2,1,0:T(8,128)S(1)}, u32[]{:S(2)}, u32[]{:S(2)}) collective-permute-start(f32[4,10,8,128]{3,2,1,0:T(8,128)S(1)} %get-tuple-element.39), channel_id=1, source_target_pairs={{8,16},{16,8},{24,32},{32,24},{40,48},{48,40},{56,64},{64,56},{72,... | collective-permute-start | bytes 491528 | tf_op jit(solution)/shard_map/ppermute | solution.py:518
  36.4 6.1 %collective-permute-start.6 = (f32[4,5,8,128]{3,2,1,0:T(8,128)S(1)}, f32[4,5,8,128]{3,2,1,0:T(8,128)S(1)}, u32[]{:S(2)}, u32[]{:S(2)}) collective-permute-start(f32[4,5,8,128]{3,2,1,0:T(8,128)S(1)} %get-tuple-element.40), channel_id=1, source_target_pairs={{1,2},{2,1},{3,4},{4,3},{5,6},{6,5},{9,10},{10,9},{11,12},{12,11},... | collective-permute-start | bytes 245768 | tf_op jit(solution)/shard_map/ppermute | solution.py:518
  38.3 4.2 %collective-permute-start.7 = (f32[4,10,8,128]{3,2,1,0:T(8,128)S(1)}, f32[4,10,8,128]{3,2,1,0:T(8,128)S(1)}, u32[]{:S(2)}, u32[]{:S(2)}) collective-permute-start(f32[4,10,8,128]{3,2,1,0:T(8,128)S(1)} %get-tuple-element.41), channel_id=1, source_target_pairs={{0,8},{8,0},{16,24},{24,16},{32,40},{40,32},{48,56},{56,48},{64,72... | collective-permute-start | bytes 491528 | tf_op jit(solution)/shard_map/ppermute | solution.py:518
  42.7 9.3 %collective-permute-start.8 = (f32[4,5,8,128]{3,2,1,0:T(8,128)S(1)}, f32[4,5,8,128]{3,2,1,0:T(8,128)S(1)}, u32[]{:S(2)}, u32[]{:S(2)}) collective-permute-start(f32[4,5,8,128]{3,2,1,0:T(8,128)S(1)} %get-tuple-element.46), channel_id=1, source_target_pairs={{0,1},{1,0},{2,3},{3,2},{4,5},{5,4},{6,7},{7,6},{8,9},{9,8},{10,11... | collective-permute-start | bytes 245768 | tf_op jit(solution)/shard_map/ppermute | solution.py:518
  43.4 9.4 %collective-permute-start.9 = (f32[4,10,8,128]{3,2,1,0:T(8,128)S(1)}, f32[4,10,8,128]{3,2,1,0:T(8,128)S(1)}, u32[]{:S(2)}, u32[]{:S(2)}) collective-permute-start(f32[4,10,8,128]{3,2,1,0:T(8,128)S(1)} %get-tuple-element.47), channel_id=1, source_target_pairs={{8,16},{16,8},{24,32},{32,24},{40,48},{48,40},{56,64},{64,56},{72,... | collective-permute-start | bytes 491528 | tf_op jit(solution)/shard_map/ppermute | solution.py:518
  48.1 6.1 %collective-permute-start.10 = (f32[4,5,8,128]{3,2,1,0:T(8,128)S(1)}, f32[4,5,8,128]{3,2,1,0:T(8,128)S(1)}, u32[]{:S(2)}, u32[]{:S(2)}) collective-permute-start(f32[4,5,8,128]{3,2,1,0:T(8,128)S(1)} %get-tuple-element.48), channel_id=1, source_target_pairs={{1,2},{2,1},{3,4},{4,3},{5,6},{6,5},{9,10},{10,9},{11,12},{12,11},... | collective-permute-start | bytes 245768 | tf_op jit(solution)/shard_map/ppermute | solution.py:518
  50.8 3.4 %collective-permute-start.11 = (f32[4,10,8,128]{3,2,1,0:T(8,128)S(1)}, f32[4,10,8,128]{3,2,1,0:T(8,128)S(1)}, u32[]{:S(2)}, u32[]{:S(2)}) collective-permute-start(f32[4,10,8,128]{3,2,1,0:T(8,128)S(1)} %get-tuple-element.49), channel_id=1, source_target_pairs={{0,8},{8,0},{16,24},{24,16},{32,40},{40,32},{48,56},{56,48},{64,72... | collective-permute-start | bytes 491528 | tf_op jit(solution)/shard_map/ppermute | solution.py:518
  54.4 8.6 %collective-permute-start.12 = (f32[4,6,8,128]{3,2,1,0:T(8,128)S(1)}, f32[4,6,8,128]{3,2,1,0:T(8,128)S(1)}, u32[]{:S(2)}, u32[]{:S(2)}) collective-permute-start(f32[4,6,8,128]{3,2,1,0:T(8,128)S(1)} %get-tuple-element.53), channel_id=1, source_target_pairs={{0,1},{1,0},{2,3},{3,2},{4,5},{5,4},{6,7},{7,6},{8,9},{9,8},{10,11... | collective-permute-start | bytes 294920 | tf_op jit(solution)/shard_map/ppermute | solution.py:518
  56.0 11.3 %collective-permute-start.13 = (f32[4,12,8,128]{3,2,1,0:T(8,128)S(1)}, f32[4,12,8,128]{3,2,1,0:T(8,128)S(1)}, u32[]{:S(2)}, u32[]{:S(2)}) collective-permute-start(f32[4,12,8,128]{3,2,1,0:T(8,128)S(1)} %get-tuple-element.54), channel_id=1, source_target_pairs={{8,16},{16,8},{24,32},{32,24},{40,48},{48,40},{56,64},{64,56},{72,... | collective-permute-start | bytes 589832 | tf_op jit(solution)/shard_map/ppermute | solution.py:518
  59.9 7.5 %collective-permute-start.14 = (f32[4,6,8,128]{3,2,1,0:T(8,128)S(1)}, f32[4,6,8,128]{3,2,1,0:T(8,128)S(1)}, u32[]{:S(2)}, u32[]{:S(2)}) collective-permute-start(f32[4,6,8,128]{3,2,1,0:T(8,128)S(1)} %get-tuple-element.55), channel_id=1, source_target_pairs={{1,2},{2,1},{3,4},{4,3},{5,6},{6,5},{9,10},{10,9},{11,12},{12,11},... | collective-permute-start | bytes 294920 | tf_op jit(solution)/shard_map/ppermute | solution.py:518
  61.8 5.6 %collective-permute-start.15 = (f32[4,12,8,128]{3,2,1,0:T(8,128)S(1)}, f32[4,12,8,128]{3,2,1,0:T(8,128)S(1)}, u32[]{:S(2)}, u32[]{:S(2)}) collective-permute-start(f32[4,12,8,128]{3,2,1,0:T(8,128)S(1)} %get-tuple-element.56), channel_id=1, source_target_pairs={{0,8},{8,0},{16,24},{24,16},{32,40},{40,32},{48,56},{56,48},{64,72... | collective-permute-start | bytes 589832 | tf_op jit(solution)/shard_map/ppermute | solution.py:518

commit v7 on v4

--- a/solution.py
+++ b/solution.py
@@ -455,7 +455,7 @@
         inside(k, state, now, before, ghost_speed, inner_x, inner_y, weights)
         return carry
 
-    lax.fori_loop(0, KRYLOV, step, 0)
+    lax.fori_loop(0, KRYLOV, step, 0, unroll=True)
 
 
 def finish_kernel(coef, form, has_ghosts, next_form, next_speed, *refs):
@@ -478,7 +478,7 @@
             send_faces(k, next_form, out, speed, px, py, *leaving)
         return carry
 
-    lax.fori_loop(0, KRYLOV, step, 0)
+    lax.fori_loop(0, KRYLOV, step, 0, unroll=True)
 
 
 def last_kernel(coef, pre, *refs):

time: 68.7 us -> 69.1 us (level)
  transfers between devices with their start and end apart: 17 -> 17, of which waited for: 8 -> 9; matrix products, arithmetic and copies ran while one was open for 0% -> 0% of each run, Pallas kernels for 7% -> 6%
where the time goes in v7:
time: 69.1 us; the launch traced here: 68.3 us
  starting transfers between devices  42.5 us (62%)
  waiting for transfers between devices  17.3 us (25%)
  Pallas kernels  7.08 us (10%)
  local copies, waits for them, and re-layouts  1.14 us (2%)
    ppermute x16, starting transfers between devices, exchange(): received.append(lax.ppermute(face, axis, pairs))  31.8 us
    ppermute x16, waiting for transfers between devices, exchange(): received.append(lax.ppermute(face, axis, pairs))  14.7 us
    all_to_all x1, starting transfers between devices, shards(): lax.all_to_all(packed, ('gx', 'gy'), split_axis=0, concat_axis=0, tiled=T...  10.7 us
    pallas_call x12, Pallas kernels, call(): pl.pallas_call(kernel, out_shape=[jax.ShapeDtypeStruct(shape, F32) for sh...  6.08 us
    all_to_all x1, waiting for transfers between devices, shards(): lax.all_to_all(packed, ('gx', 'gy'), split_axis=0, concat_axis=0, tiled=T...  2.62 us
  transfers between devices with their start and end apart: 17, of which 9 were waited for; matrix products, arithmetic and copies ran while one was open for 0% of the time, Pallas kernels for 6%

profile of v7, /device:TPU:13, one launch (start us, length us, event | category | flops | bytes accessed | tf_op | source)
XLA Modules:
  0.0 68.3 jit_solution(13267551197178315469)
XLA Ops:
  0.0 1.1 %copy-done.1 = f32[2,3,64,1,16,16]{2,5,4,3,1,0:T(8,128)S(1)} copy-done((f32[2,3,64,1,16,16]{2,5,4,3,1,0:T(8,128)S(1)}, f32[2,3,64,1,16,16]{2,5,4,3,1,0:T(8,128)}, u32[]{:S(2)}) %copy-start.1) | copy-done | bytes 393240
  1.1 1.2 %shard_map.28 = f32[1152,128]{1,0:T(8,128)} custom-call(f32[6,16,16,64]{3,2,1,0:T(8,128)S(1)} %bitcast.14), custom_call_target="tpu_custom_call" | custom-call | flops 1000000 | bytes 2097152 | tf_op jit(solution)/shard_map/pallas_call | solution.py:507
  2.3 10.7 %all-to-all-start = ((f32[128,1,1152]{2,1,0:T(1,128)}), f32[128,1,1152]{2,1,0:T(1,128)S(1)}, u32[]{:S(2)}, u32[]{:S(2)}) async-start(f32[128,1,1152]{2,1,0:T(1,128)} %bitcast.3), calls=%async_computation | async-start | bytes 1179648 | tf_op jit(solution)/shard_map/all_to_all | solution.py:568
  13.1 5.3 %collective-permute-start.1 = (f32[4,12,8,128]{3,2,1,0:T(8,128)S(1)}, f32[4,12,8,128]{3,2,1,0:T(8,128)S(1)}, u32[]{:S(2)}, u32[]{:S(2)}) collective-permute-start(f32[4,12,8,128]{3,2,1,0:T(8,128)S(1)} %get-tuple-element.33), channel_id=1, source_target_pairs={{8,16},{16,8},{24,32},{32,24},{40,48},{48,40},{56,64},{64,56},{72,... | collective-permute-start | bytes 589832 | tf_op jit(solution)/shard_map/ppermute | solution.py:532
  18.5 0.2 collective-permute-start.3
  18.7 0.6 collective-permute-start
  19.2 2.7 %collective-permute-start.2 = (f32[4,6,8,128]{3,2,1,0:T(8,128)S(1)}, f32[4,6,8,128]{3,2,1,0:T(8,128)S(1)}, u32[]{:S(2)}, u32[]{:S(2)}) collective-permute-start(f32[4,6,8,128]{3,2,1,0:T(8,128)S(1)} %get-tuple-element.34), channel_id=1, source_target_pairs={{1,2},{2,1},{3,4},{4,3},{5,6},{6,5},{9,10},{10,9},{11,12},{12,11},... | collective-permute-start | bytes 294920 | tf_op jit(solution)/shard_map/ppermute | solution.py:532
  22.0 2.6 %all-to-all-done = f32[128,1,1152]{2,1,0:T(1,128)S(1)} async-done(((f32[128,1,1152]{2,1,0:T(1,128)}), f32[128,1,1152]{2,1,0:T(1,128)S(1)}, u32[]{:S(2)}, u32[]{:S(2)}) %all-to-all-start) | async-done | bytes 589856 | tf_op jit(solution)/shard_map/all_to_all | solution.py:568
  24.6 0.2 shard_map.29
  24.8 0.9 %shard_map.30.refs_0_ = f32[4,3,4,4,8,128]{5,4,3,2,1,0:T(8,128)S(1)} custom-call(f32[4,3,4,4,8,128]{5,4,3,2,1,0:T(8,128)S(1)} %bitcast.10, f32[3,128,128]{2,1,0:T(8,128)S(1)} %get-tuple-element.31.speed), custom_call_target="tpu_custom_call" | custom-call | flops 10000000 | bytes 2097152 | tf_op jit(solution)/shard_map/pallas_call | solution.py:507
  25.7 4.4 %collective-permute-done.refs_1_.refs_2_.refs_8_ = f32[4,6,8,128]{3,2,1,0:T(8,128)S(1)} collective-permute-done((f32[4,6,8,128]{3,2,1,0:T(8,128)S(1)}, f32[4,6,8,128]{3,2,1,0:T(8,128)S(1)}, u32[]{:S(2)}, u32[]{:S(2)}) %collective-permute-start) | collective-permute-done | bytes 98336 | tf_op jit(solution)/shard_map/ppermute | solution.py:532
  30.1 0.7 %collective-permute-done.1.refs_2_.refs_3_.refs_9_ = f32[4,12,8,128]{3,2,1,0:T(8,128)S(1)} collective-permute-done((f32[4,12,8,128]{3,2,1,0:T(8,128)S(1)}, f32[4,12,8,128]{3,2,1,0:T(8,128)S(1)}, u32[]{:S(2)}, u32[]{:S(2)}) %collective-permute-start.1) | collective-permute-done | bytes 196640 | tf_op jit(solution)/shard_map/ppermute | solution.py:532
  31.0 0.5 collective-permute-start.4
  31.5 4.9 %collective-permute-start.5 = (f32[4,10,8,128]{3,2,1,0:T(8,128)S(1)}, f32[4,10,8,128]{3,2,1,0:T(8,128)S(1)}, u32[]{:S(2)}, u32[]{:S(2)}) collective-permute-start(f32[4,10,8,128]{3,2,1,0:T(8,128)S(1)} %get-tuple-element.39), channel_id=1, source_target_pairs={{8,16},{16,8},{24,32},{32,24},{40,48},{48,40},{56,64},{64,56},{72,... | collective-permute-start | bytes 491528 | tf_op jit(solution)/shard_map/ppermute | solution.py:532
  36.4 1.9 %collective-permute-start.6 = (f32[4,5,8,128]{3,2,1,0:T(8,128)S(1)}, f32[4,5,8,128]{3,2,1,0:T(8,128)S(1)}, u32[]{:S(2)}, u32[]{:S(2)}) collective-permute-start(f32[4,5,8,128]{3,2,1,0:T(8,128)S(1)} %get-tuple-element.40), channel_id=1, source_target_pairs={{1,2},{2,1},{3,4},{4,3},{5,6},{6,5},{9,10},{10,9},{11,12},{12,11},... | collective-permute-start | bytes 245768 | tf_op jit(solution)/shard_map/ppermute | solution.py:532
  38.4 0.9 %shard_map.33.refs_0_ = f32[4,3,4,4,8,128]{5,4,3,2,1,0:T(8,128)S(1)} custom-call(f32[4,3,4,4,8,128]{5,4,3,2,1,0:T(8,128)S(1)} %get-tuple-element.37.state.refs_0_, f32[4,3,4,4,8,128]{5,4,3,2,1,0:T(8,128)S(1)} %bitcast.11, f32[3,128,128]{2,1,0:T(8,128)S(1)} %get-tuple-element.31.speed), custom_call_target="tpu_custom_call" | custom-call | flops 10000000 | bytes 2097152 | tf_op jit(solution)/shard_map/pallas_call | solution.py:507
  39.6 1.4 %collective-permute-done.5.arrived = f32[4,10,8,128]{3,2,1,0:T(8,128)S(1)} collective-permute-done((f32[4,10,8,128]{3,2,1,0:T(8,128)S(1)}, f32[4,10,8,128]{3,2,1,0:T(8,128)S(1)}, u32[]{:S(2)}, u32[]{:S(2)}) %collective-permute-start.5) | collective-permute-done | bytes 163872 | tf_op jit(solution)/shard_map/ppermute | solution.py:532
  41.0 1.5 %collective-permute-done.6.refs_3_.refs_4_ = f32[4,5,8,128]{3,2,1,0:T(8,128)S(1)} collective-permute-done((f32[4,5,8,128]{3,2,1,0:T(8,128)S(1)}, f32[4,5,8,128]{3,2,1,0:T(8,128)S(1)}, u32[]{:S(2)}, u32[]{:S(2)}) %collective-permute-start.6) | collective-permute-done | bytes 81952 | tf_op jit(solution)/shard_map/ppermute | solution.py:532
  42.5 0.2 shard_map.37
  42.7 0.7 %collective-permute-start.8 = (f32[4,5,8,128]{3,2,1,0:T(8,128)S(1)}, f32[4,5,8,128]{3,2,1,0:T(8,128)S(1)}, u32[]{:S(2)}, u32[]{:S(2)}) collective-permute-start(f32[4,5,8,128]{3,2,1,0:T(8,128)S(1)} %get-tuple-element.46), channel_id=1, source_target_pairs={{0,1},{1,0},{2,3},{3,2},{4,5},{5,4},{6,7},{7,6},{8,9},{9,8},{10,11... | collective-permute-start | bytes 245768 | tf_op jit(solution)/shard_map/ppermute | solution.py:532
  43.4 4.6 %collective-permute-start.9 = (f32[4,10,8,128]{3,2,1,0:T(8,128)S(1)}, f32[4,10,8,128]{3,2,1,0:T(8,128)S(1)}, u32[]{:S(2)}, u32[]{:S(2)}) collective-permute-start(f32[4,10,8,128]{3,2,1,0:T(8,128)S(1)} %get-tuple-element.47), channel_id=1, source_target_pairs={{8,16},{16,8},{24,32},{32,24},{40,48},{48,40},{56,64},{64,56},{72,... | collective-permute-start | bytes 491528 | tf_op jit(solution)/shard_map/ppermute | solution.py:532
  48.1 2.7 %collective-permute-start.10 = (f32[4,5,8,128]{3,2,1,0:T(8,128)S(1)}, f32[4,5,8,128]{3,2,1,0:T(8,128)S(1)}, u32[]{:S(2)}, u32[]{:S(2)}) collective-permute-start(f32[4,5,8,128]{3,2,1,0:T(8,128)S(1)} %get-tuple-element.48), channel_id=1, source_target_pairs={{1,2},{2,1},{3,4},{4,3},{5,6},{6,5},{9,10},{10,9},{11,12},{12,11},... | collective-permute-start | bytes 245768 | tf_op jit(solution)/shard_map/ppermute | solution.py:532
  50.9 0.9 %shard_map.38.refs_0_ = f32[4,3,4,4,8,128]{5,4,3,2,1,0:T(8,128)S(1)} custom-call(f32[4,3,4,4,8,128]{5,4,3,2,1,0:T(8,128)S(1)} %get-tuple-element.45.state.start, f32[3,128,128]{2,1,0:T(8,128)S(1)} %get-tuple-element.44.refs_8_.speed.refs_7_), custom_call_target="tpu_custom_call" | custom-call | flops 10000000 | bytes 2097152 | tf_op jit(solution)/shard_map/pallas_call | solution.py:507
  52.0 0.9 %collective-permute-done.9.arrived = f32[4,10,8,128]{3,2,1,0:T(8,128)S(1)} collective-permute-done((f32[4,10,8,128]{3,2,1,0:T(8,128)S(1)}, f32[4,10,8,128]{3,2,1,0:T(8,128)S(1)}, u32[]{:S(2)}, u32[]{:S(2)}) %collective-permute-start.9) | collective-permute-done | bytes 163872 | tf_op jit(solution)/shard_map/ppermute | solution.py:532
  52.9 1.3 %collective-permute-done.10.refs_3_ = f32[4,5,8,128]{3,2,1,0:T(8,128)S(1)} collective-permute-done((f32[4,5,8,128]{3,2,1,0:T(8,128)S(1)}, f32[4,5,8,128]{3,2,1,0:T(8,128)S(1)}, u32[]{:S(2)}, u32[]{:S(2)}) %collective-permute-start.10) | collective-permute-done | bytes 81952 | tf_op jit(solution)/shard_map/ppermute | solution.py:532
  54.4 1.6 %collective-permute-start.12 = (f32[4,6,8,128]{3,2,1,0:T(8,128)S(1)}, f32[4,6,8,128]{3,2,1,0:T(8,128)S(1)}, u32[]{:S(2)}, u32[]{:S(2)}) collective-permute-start(f32[4,6,8,128]{3,2,1,0:T(8,128)S(1)} %get-tuple-element.53), channel_id=1, source_target_pairs={{0,1},{1,0},{2,3},{3,2},{4,5},{5,4},{6,7},{7,6},{8,9},{9,8},{10,11... | collective-permute-start | bytes 294920 | tf_op jit(solution)/shard_map/ppermute | solution.py:532
  56.0 3.9 %collective-permute-start.13 = (f32[4,12,8,128]{3,2,1,0:T(8,128)S(1)}, f32[4,12,8,128]{3,2,1,0:T(8,128)S(1)}, u32[]{:S(2)}, u32[]{:S(2)}) collective-permute-start(f32[4,12,8,128]{3,2,1,0:T(8,128)S(1)} %get-tuple-element.54), channel_id=1, source_target_pairs={{8,16},{16,8},{24,32},{32,24},{40,48},{48,40},{56,64},{64,56},{72,... | collective-permute-start | bytes 589832 | tf_op jit(solution)/shard_map/ppermute | solution.py:532
  59.9 1.9 %collective-permute-start.14 = (f32[4,6,8,128]{3,2,1,0:T(8,128)S(1)}, f32[4,6,8,128]{3,2,1,0:T(8,128)S(1)}, u32[]{:S(2)}, u32[]{:S(2)}) collective-permute-start(f32[4,6,8,128]{3,2,1,0:T(8,128)S(1)} %get-tuple-element.55), channel_id=1, source_target_pairs={{1,2},{2,1},{3,4},{4,3},{5,6},{6,5},{9,10},{10,9},{11,12},{12,11},... | collective-permute-start | bytes 294920 | tf_op jit(solution)/shard_map/ppermute | solution.py:532
  61.9 0.9 %shard_map.43.refs_0_ = f32[4,3,4,4,8,128]{5,4,3,2,1,0:T(8,128)S(1)} custom-call(f32[4,3,4,4,8,128]{5,4,3,2,1,0:T(8,128)S(1)} %get-tuple-element.52.state, f32[4,3,4,4,8,128]{5,4,3,2,1,0:T(8,128)S(1)} %get-tuple-element.45.state.start, f32[3,128,128]{2,1,0:T(8,128)S(1)} %get-tuple-element.44.refs_8_.speed.refs_7_), custom_call_target="tpu_custom_call" | custom-call | flops 10000000 | bytes 2097152 | tf_op jit(solution)/shard_map/pallas_call | solution.py:507
  62.8 3.8 %collective-permute-done.13.arrived = f32[4,12,8,128]{3,2,1,0:T(8,128)S(1)} collective-permute-done((f32[4,12,8,128]{3,2,1,0:T(8,128)S(1)}, f32[4,12,8,128]{3,2,1,0:T(8,128)S(1)}, u32[]{:S(2)}, u32[]{:S(2)}) %collective-permute-start.13) | collective-permute-done | bytes 196640 | tf_op jit(solution)/shard_map/ppermute | solution.py:532
  66.7 0.7 collective-permute-done.14.refs_3_
  67.4 0.9 %shard_map.46 = f32[4,3,4,4,8,128]{5,4,3,2,1,0:T(8,128)} custom-call(f32[4,3,4,4,8,128]{5,4,3,2,1,0:T(8,128)S(1)} %shard_map.43.refs_0_, f32[4,6,8,128]{3,2,1,0:T(8,128)S(1)} %shard_map.44.refs_0_.refs_1_, f32[4,12,8,128]{3,2,1,0:T(8,128)S(1)} %shard_map.45.refs_2_, f32[4,6,8,128]{3,2,1,0:T(8,128)S(1)} %collective-permute-done.14.refs_3_, ...), custom_call_target="tpu_custom_call" | custom-call | flops 1000000 | bytes 2000000 | tf_op jit(solution)/shard_map/pallas_call | solution.py:608
  (25 shorter events, 1.2 us)
Async XLA Ops:
  0.0 1.1 %copy-start.1 = (f32[2,3,64,1,16,16]{2,5,4,3,1,0:T(8,128)S(1)}, f32[2,3,64,1,16,16]{2,5,4,3,1,0:T(8,128)}, u32[]{:S(2)}) copy-start(f32[2,3,64,1,16,16]{2,5,4,3,1,0:T(8,128)} %param.3) | copy-start | bytes 1179652
  2.3 10.7 %copy-start = (f32[4,3,64,1,2,128]{5,4,3,2,1,0:T(2,128)S(1)}, f32[4,3,64,1,2,128]{5,4,3,2,1,0:T(2,128)}, u32[]{:S(2)}) copy-start(f32[4,3,64,1,2,128]{5,4,3,2,1,0:T(2,128)} %param.2) | copy-start | bytes 2359300
  2.3 22.3 %all-to-all-start = ((f32[128,1,1152]{2,1,0:T(1,128)}), f32[128,1,1152]{2,1,0:T(1,128)S(1)}, u32[]{:S(2)}, u32[]{:S(2)}) async-start(f32[128,1,1152]{2,1,0:T(1,128)} %bitcast.3), calls=%async_computation | async-start | bytes 1179648 | tf_op jit(solution)/shard_map/all_to_all | solution.py:568
  13.1 17.7 %collective-permute-start.1 = (f32[4,12,8,128]{3,2,1,0:T(8,128)S(1)}, f32[4,12,8,128]{3,2,1,0:T(8,128)S(1)}, u32[]{:S(2)}, u32[]{:S(2)}) collective-permute-start(f32[4,12,8,128]{3,2,1,0:T(8,128)S(1)} %get-tuple-element.33), channel_id=1, source_target_pairs={{8,16},{16,8},{24,32},{32,24},{40,48},{48,40},{56,64},{64,56},{72,... | collective-permute-start | bytes 589832 | tf_op jit(solution)/shard_map/ppermute | solution.py:532
  18.5 12.4 %collective-permute-start.3 = (f32[4,12,8,128]{3,2,1,0:T(8,128)S(1)}, f32[4,12,8,128]{3,2,1,0:T(8,128)S(1)}, u32[]{:S(2)}, u32[]{:S(2)}) collective-permute-start(f32[4,12,8,128]{3,2,1,0:T(8,128)S(1)} %get-tuple-element.35), channel_id=1, source_target_pairs={{0,8},{8,0},{16,24},{24,16},{32,40},{40,32},{48,56},{56,48},{64,72... | collective-permute-start | bytes 589832 | tf_op jit(solution)/shard_map/ppermute | solution.py:532
  18.7 11.4 %collective-permute-start = (f32[4,6,8,128]{3,2,1,0:T(8,128)S(1)}, f32[4,6,8,128]{3,2,1,0:T(8,128)S(1)}, u32[]{:S(2)}, u32[]{:S(2)}) collective-permute-start(f32[4,6,8,128]{3,2,1,0:T(8,128)S(1)} %get-tuple-element.32), channel_id=1, source_target_pairs={{0,1},{1,0},{2,3},{3,2},{4,5},{5,4},{6,7},{7,6},{8,9},{9,8},{10,11... | collective-permute-start | bytes 294920 | tf_op jit(solution)/shard_map/ppermute | solution.py:532
  19.2 10.9 %collective-permute-start.2 = (f32[4,6,8,128]{3,2,1,0:T(8,128)S(1)}, f32[4,6,8,128]{3,2,1,0:T(8,128)S(1)}, u32[]{:S(2)}, u32[]{:S(2)}) collective-permute-start(f32[4,6,8,128]{3,2,1,0:T(8,128)S(1)} %get-tuple-element.34), channel_id=1, source_target_pairs={{1,2},{2,1},{3,4},{4,3},{5,6},{6,5},{9,10},{10,9},{11,12},{12,11},... | collective-permute-start | bytes 294920 | tf_op jit(solution)/shard_map/ppermute | solution.py:532
  31.0 8.5 %collective-permute-start.4 = (f32[4,5,8,128]{3,2,1,0:T(8,128)S(1)}, f32[4,5,8,128]{3,2,1,0:T(8,128)S(1)}, u32[]{:S(2)}, u32[]{:S(2)}) collective-permute-start(f32[4,5,8,128]{3,2,1,0:T(8,128)S(1)} %get-tuple-element.38), channel_id=1, source_target_pairs={{0,1},{1,0},{2,3},{3,2},{4,5},{5,4},{6,7},{7,6},{8,9},{9,8},{10,11... | collective-permute-start | bytes 245768 | tf_op jit(solution)/shard_map/ppermute | solution.py:532
  31.5 9.5 %collective-permute-start.5 = (f32[4,10,8,128]{3,2,1,0:T(8,128)S(1)}, f32[4,10,8,128]{3,2,1,0:T(8,128)S(1)}, u32[]{:S(2)}, u32[]{:S(2)}) collective-permute-start(f32[4,10,8,128]{3,2,1,0:T(8,128)S(1)} %get-tuple-element.39), channel_id=1, source_target_pairs={{8,16},{16,8},{24,32},{32,24},{40,48},{48,40},{56,64},{64,56},{72,... | collective-permute-start | bytes 491528 | tf_op jit(solution)/shard_map/ppermute | solution.py:532
  36.4 6.1 %collective-permute-start.6 = (f32[4,5,8,128]{3,2,1,0:T(8,128)S(1)}, f32[4,5,8,128]{3,2,1,0:T(8,128)S(1)}, u32[]{:S(2)}, u32[]{:S(2)}) collective-permute-start(f32[4,5,8,128]{3,2,1,0:T(8,128)S(1)} %get-tuple-element.40), channel_id=1, source_target_pairs={{1,2},{2,1},{3,4},{4,3},{5,6},{6,5},{9,10},{10,9},{11,12},{12,11},... | collective-permute-start | bytes 245768 | tf_op jit(solution)/shard_map/ppermute | solution.py:532
  38.3 4.2 %collective-permute-start.7 = (f32[4,10,8,128]{3,2,1,0:T(8,128)S(1)}, f32[4,10,8,128]{3,2,1,0:T(8,128)S(1)}, u32[]{:S(2)}, u32[]{:S(2)}) collective-permute-start(f32[4,10,8,128]{3,2,1,0:T(8,128)S(1)} %get-tuple-element.41), channel_id=1, source_target_pairs={{0,8},{8,0},{16,24},{24,16},{32,40},{40,32},{48,56},{56,48},{64,72... | collective-permute-start | bytes 491528 | tf_op jit(solution)/shard_map/ppermute | solution.py:532
  42.7 9.2 %collective-permute-start.8 = (f32[4,5,8,128]{3,2,1,0:T(8,128)S(1)}, f32[4,5,8,128]{3,2,1,0:T(8,128)S(1)}, u32[]{:S(2)}, u32[]{:S(2)}) collective-permute-start(f32[4,5,8,128]{3,2,1,0:T(8,128)S(1)} %get-tuple-element.46), channel_id=1, source_target_pairs={{0,1},{1,0},{2,3},{3,2},{4,5},{5,4},{6,7},{7,6},{8,9},{9,8},{10,11... | collective-permute-start | bytes 245768 | tf_op jit(solution)/shard_map/ppermute | solution.py:532
  43.4 9.4 %collective-permute-start.9 = (f32[4,10,8,128]{3,2,1,0:T(8,128)S(1)}, f32[4,10,8,128]{3,2,1,0:T(8,128)S(1)}, u32[]{:S(2)}, u32[]{:S(2)}) collective-permute-start(f32[4,10,8,128]{3,2,1,0:T(8,128)S(1)} %get-tuple-element.47), channel_id=1, source_target_pairs={{8,16},{16,8},{24,32},{32,24},{40,48},{48,40},{56,64},{64,56},{72,... | collective-permute-start | bytes 491528 | tf_op jit(solution)/shard_map/ppermute | solution.py:532
  48.1 6.1 %collective-permute-start.10 = (f32[4,5,8,128]{3,2,1,0:T(8,128)S(1)}, f32[4,5,8,128]{3,2,1,0:T(8,128)S(1)}, u32[]{:S(2)}, u32[]{:S(2)}) collective-permute-start(f32[4,5,8,128]{3,2,1,0:T(8,128)S(1)} %get-tuple-element.48), channel_id=1, source_target_pairs={{1,2},{2,1},{3,4},{4,3},{5,6},{6,5},{9,10},{10,9},{11,12},{12,11},... | collective-permute-start | bytes 245768 | tf_op jit(solution)/shard_map/ppermute | solution.py:532
  50.8 3.4 %collective-permute-start.11 = (f32[4,10,8,128]{3,2,1,0:T(8,128)S(1)}, f32[4,10,8,128]{3,2,1,0:T(8,128)S(1)}, u32[]{:S(2)}, u32[]{:S(2)}) collective-permute-start(f32[4,10,8,128]{3,2,1,0:T(8,128)S(1)} %get-tuple-element.49), channel_id=1, source_target_pairs={{0,8},{8,0},{16,24},{24,16},{32,40},{40,32},{48,56},{56,48},{64,72... | collective-permute-start | bytes 491528 | tf_op jit(solution)/shard_map/ppermute | solution.py:532
  54.4 8.5 %collective-permute-start.12 = (f32[4,6,8,128]{3,2,1,0:T(8,128)S(1)}, f32[4,6,8,128]{3,2,1,0:T(8,128)S(1)}, u32[]{:S(2)}, u32[]{:S(2)}) collective-permute-start(f32[4,6,8,128]{3,2,1,0:T(8,128)S(1)} %get-tuple-element.53), channel_id=1, source_target_pairs={{0,1},{1,0},{2,3},{3,2},{4,5},{5,4},{6,7},{7,6},{8,9},{9,8},{10,11... | collective-permute-start | bytes 294920 | tf_op jit(solution)/shard_map/ppermute | solution.py:532
  56.0 10.7 %collective-permute-start.13 = (f32[4,12,8,128]{3,2,1,0:T(8,128)S(1)}, f32[4,12,8,128]{3,2,1,0:T(8,128)S(1)}, u32[]{:S(2)}, u32[]{:S(2)}) collective-permute-start(f32[4,12,8,128]{3,2,1,0:T(8,128)S(1)} %get-tuple-element.54), channel_id=1, source_target_pairs={{8,16},{16,8},{24,32},{32,24},{40,48},{48,40},{56,64},{64,56},{72,... | collective-permute-start | bytes 589832 | tf_op jit(solution)/shard_map/ppermute | solution.py:532
  59.9 7.5 %collective-permute-start.14 = (f32[4,6,8,128]{3,2,1,0:T(8,128)S(1)}, f32[4,6,8,128]{3,2,1,0:T(8,128)S(1)}, u32[]{:S(2)}, u32[]{:S(2)}) collective-permute-start(f32[4,6,8,128]{3,2,1,0:T(8,128)S(1)} %get-tuple-element.55), channel_id=1, source_target_pairs={{1,2},{2,1},{3,4},{4,3},{5,6},{6,5},{9,10},{10,9},{11,12},{12,11},... | collective-permute-start | bytes 294920 | tf_op jit(solution)/shard_map/ppermute | solution.py:532
  61.8 5.6 %collective-permute-start.15 = (f32[4,12,8,128]{3,2,1,0:T(8,128)S(1)}, f32[4,12,8,128]{3,2,1,0:T(8,128)S(1)}, u32[]{:S(2)}, u32[]{:S(2)}) collective-permute-start(f32[4,12,8,128]{3,2,1,0:T(8,128)S(1)} %get-tuple-element.56), channel_id=1, source_target_pairs={{0,8},{8,0},{16,24},{24,16},{32,40},{40,32},{48,56},{56,48},{64,72... | collective-permute-start | bytes 589832 | tf_op jit(solution)/shard_map/ppermute | solution.py:532
